TPU v7x, 32 devices: a whole 2x2x4 slice. The times are simulated.
32 devices in a mesh: segment: 4 (over z), expert: 8 (over y, x, core).
Axes of the slice: x: 2, y: 2, z: 4, core: 2. Of those that a mesh axis runs over, the one named last changes fastest.
Arguments:
- section_output: bfloat16 [4, 512, 2048], P('segment', 'expert'), may hold values from -6 to 6
- section_gradient: bfloat16 [4, 512, 2048], P('segment', 'expert'), may hold values from -6 to 6
- forward_routes: int32 [4, 512, 8], P('segment', 'expert'), may hold values from 0 to 127, all different within a row; in each aligned block of 64 rows (0 to 63, 64 to 127, ..., all dimensions but the last counted through in order) at most 5 rows name the same one
- forward_logits: float32 [4, 512, 8], P('segment', 'expert'), may hold values from -1.2 to 1.2
- backward_routes: int32 [4, 512, 8], P('segment', 'expert'), may hold values from 0 to 127, all different within a row; in each aligned block of 64 rows (0 to 63, 64 to 127, ..., all dimensions but the last counted through in order) at most 5 rows name the same one
- backward_logits: float32 [4, 512, 8], P('segment', 'expert'), may hold values from -1.2 to 1.2
- entry_weights: bfloat16 [4, 8, 2048, 384], P('segment', 'expert'), may hold values from -0.25 to 0.25
- down_weights: bfloat16 [4, 8, 192, 2048], P('segment', 'expert'), may hold values from -0.3125 to 0.3125
- saved_projections: bfloat16 [4, 8, 40, 384], P('segment', 'expert'), may hold values from -8 to 8
Outputs:
- forward_output: bfloat16 [4, 512, 2048], P('segment', 'expert')
- input_gradient: bfloat16 [4, 512, 2048], P('segment', 'expert')
Inputs may be any that keep to these rules, and one draw needn't show every extreme that they name: `forward_routes`: each token's 8 ids differ. Within one device's 64 tokens of a section (aligned blocks) no expert is named by more than 5 routes, and some block has an expert named by exactly 5. `backward_routes`: each token's 8 ids differ. Within one device's 64 tokens of a section (aligned blocks) no expert is named by more than 5 routes, and some block has an expert named by exactly 5.
All inputs are finite; a program needn't handle non-finite values.
Results may differ from a plain program's by a relative error of at most 0.0038.
Values may be sent and summed in bfloat16 or wider, within the bound.
No kernel may reach another device: no remote copies, remote signals or barrier semaphores. Data moves between devices by JAX's collectives and lax.ppermute only.
A program may use at most 64 MiB of HBM per device.

v0:
```python
import jax
import jax.numpy as jnp
from jax import lax
from jax.sharding import PartitionSpec as P

TOP = 8
FSPLIT = 8
CAP = 5


def from_behind(value, axis, steps):
    count = lax.axis_size(axis)
    pairs = [(source, (source + steps) % count) for source in range(count)]
    return lax.ppermute(value, axis, pairs)


def slot_table(block_routes, groups):
    flat_routes = block_routes.reshape(-1)
    expert_hit = (flat_routes[:, None] == jnp.arange(groups, dtype=jnp.int32)[None, :]).astype(
        jnp.int32
    )
    earlier = jnp.cumsum(expert_hit, axis=0) - expert_hit
    picked = expert_hit[:, :, None] * (
        earlier[:, :, None] == jnp.arange(CAP, dtype=jnp.int32)[None, None, :]
    ).astype(jnp.int32)
    return picked.reshape(flat_routes.shape[0], groups * CAP)


def route_probs(logits):
    scores = jnp.exp(logits)
    return scores / jnp.sum(scores, axis=-1, keepdims=True)


def dispatch(table, route_rows, groups):
    slots = jnp.einsum(
        "rs,rd->sd", table.astype(jnp.bfloat16), route_rows, preferred_element_type=jnp.float32
    )
    slots = slots.astype(jnp.bfloat16).reshape(groups, CAP, route_rows.shape[1])
    return jnp.repeat(slots, FSPLIT, axis=0)


def collect(table, returned, groups):
    width = returned.shape[2]
    summed = jnp.sum(returned.astype(jnp.float32).reshape(groups, FSPLIT, CAP, width), axis=1)
    summed = summed.reshape(groups * CAP, width)
    return jnp.dot(table.astype(jnp.float32), summed, precision=lax.Precision.HIGHEST)


def expert_forward(received, entry, down):
    shape = received.shape
    rows = received.reshape(-1, shape[2])
    half = entry.shape[1] // 2
    preacts = jnp.dot(rows, entry, preferred_element_type=jnp.float32)
    gate = preacts[:, :half]
    hidden = (gate * jax.nn.sigmoid(gate) * preacts[:, half:]).astype(jnp.bfloat16)
    partial_value = jnp.dot(hidden, down, preferred_element_type=jnp.float32).astype(jnp.bfloat16)
    return partial_value.reshape(shape)


def expert_backward(received, saved, entry, down):
    shape = received.shape
    rows = received.reshape(-1, shape[2])
    half = entry.shape[1] // 2
    stored = saved.astype(jnp.float32)
    gate = stored[:, :half]
    upper = stored[:, half:]
    grad_hidden = jnp.einsum("rd,hd->rh", rows, down, preferred_element_type=jnp.float32)
    logistic = jax.nn.sigmoid(gate)
    grad_gate = grad_hidden * upper * logistic * (1.0 + gate * (1.0 - logistic))
    grad_upper = grad_hidden * gate * logistic
    grad_pre = jnp.concatenate([grad_gate, grad_upper], axis=1).astype(jnp.bfloat16)
    partial_value = jnp.einsum(
        "rk,dk->rd", grad_pre, entry, preferred_element_type=jnp.float32
    ).astype(jnp.bfloat16)
    return partial_value.reshape(shape)


def shards(
    section_output,
    section_gradient,
    forward_routes,
    forward_logits,
    backward_routes,
    backward_logits,
    entry_weights,
    down_weights,
    saved_projections,
):
    owners = lax.axis_size("expert")
    groups = owners // FSPLIT
    layer_input = from_behind(section_output[0], "segment", 1)
    upstream = from_behind(section_gradient[0], "segment", -1)
    tok_rows = layer_input.shape[0]
    width = layer_input.shape[1]
    forward_table = slot_table(forward_routes[0], groups)
    backward_table = slot_table(backward_routes[0], groups)
    probs_a = route_probs(forward_logits[0])
    probs_b = route_probs(backward_logits[0])
    forward_slots = dispatch(forward_table, jnp.repeat(layer_input, TOP, axis=0), groups)
    scaled = (
        jnp.repeat(upstream.astype(jnp.float32), TOP, axis=0) * probs_b.reshape(-1)[:, None]
    ).astype(jnp.bfloat16)
    backward_slots = dispatch(backward_table, scaled, groups)
    entry = entry_weights[0, 0]
    down = down_weights[0, 0]
    saved = saved_projections[0, 0]
    partial_value = expert_forward(
        lax.all_to_all(forward_slots, "expert", split_axis=0, concat_axis=0, tiled=True),
        entry,
        down,
    )
    returned_a = lax.all_to_all(partial_value, "expert", split_axis=0, concat_axis=0, tiled=True)
    received_b = lax.all_to_all(backward_slots, "expert", split_axis=0, concat_axis=0, tiled=True)
    partial_b = expert_backward(received_b, saved, entry, down)
    returned_b = lax.all_to_all(partial_b, "expert", split_axis=0, concat_axis=0, tiled=True)
    route_out = collect(forward_table, returned_a, groups).reshape(tok_rows, TOP, width)
    branch = jnp.sum(route_out * probs_a[:, :, None], axis=1)
    forward_output = (layer_input.astype(jnp.float32) + branch).astype(jnp.bfloat16)
    route_back = collect(backward_table, returned_b, groups).reshape(tok_rows, TOP, width)
    input_gradient = (upstream.astype(jnp.float32) + jnp.sum(route_back, axis=1)).astype(
        jnp.bfloat16
    )
    return (forward_output[None], input_gradient[None])


def solution(mesh):
    placed = (
        P("segment", "expert", None),
        P("segment", "expert", None),
        P("segment", "expert", None),
        P("segment", "expert", None),
        P("segment", "expert", None),
        P("segment", "expert", None),
        P("segment", "expert", None, None),
        P("segment", "expert", None, None),
        P("segment", "expert", None, None),
    )
    return jax.shard_map(
        shards,
        mesh=mesh,
        in_specs=placed,
        out_specs=(P("segment", "expert", None), P("segment", "expert", None)),
        check_vma=False,
    )
```

profile of v0, /device:TPU:0, one launch (start us, length us, event | category | flops | bytes accessed | tf_op | source)
XLA Modules:
  0.0 65.3 jit_solution(399076528213492020)
XLA Ops:
  0.6 5.1 %collective-permute-start.1 = (bf16[64,2048]{1,0:T(8,128)(2,1)}, bf16[64,2048]{1,0:T(8,128)(2,1)S(1)}, u32[]{:S(2)}, u32[]{:S(2)}) collective-permute-start(bf16[64,2048]{1,0:T(8,128)(2,1)} %bitcast.75), channel_id=1, source_target_pairs={{0,24},{8,0},{16,8},{24,16},{1,25},{9,1},{17,9},{25,17},{2,26},{10... | collective-permute-start | bytes 786440 | tf_op jit(solution)/shard_map/ppermute | solution.py:14
  5.8 0.7 %compare_convert_fusion = (s32[1,64,8]{1,2,0:T(8,128)S(1)}, s32[64,8]{0,1:T(8,128)S(1)}) fusion(s32[1,64,8]{1,2,0:T(8,128)} %param.13), kind=kLoop, calls=%fused_computation.67 | loop fusion | flops 1024 | bytes 6144 | tf_op jit(solution)/shard_map/convert_element_type | solution.py:19
  6.4 0.1 copy.32
  6.5 0.1 reshape.489
  6.6 0.1 reshape.491
  6.7 0.3 reduce-window.16
  7.0 0.2 slice_reduce_fusion
  7.2 0.1 reshape.477
  7.3 0.7 %compare_convert_fusion.1 = (s32[1,64,8]{1,2,0:T(8,128)S(1)}, s32[64,8]{0,1:T(8,128)S(1)}) fusion(s32[1,64,8]{1,2,0:T(8,128)} %param.11), kind=kLoop, calls=%fused_computation.68 | loop fusion | flops 1024 | bytes 6144 | tf_op jit(solution)/shard_map/convert_element_type | solution.py:19
  8.0 0.1 copy.25
  8.1 0.1 reshape.486
  8.2 0.3 reduce-window.14
  8.5 0.2 slice_reduce_fusion.1
  8.7 0.1 reshape.467
  8.8 0.2 reduce-window.19
  8.9 0.7 %exponential_reduce_fusion = f32[64]{0:T(128)S(1)} fusion(f32[1,64,8]{1,2,0:T(8,128)} %param.14), kind=kLoop, calls=%fused_computation.69 | loop fusion | flops 448 | bytes 2304 | tf_op jit(solution)/shard_map/reduce_sum | solution.py:31
  9.7 0.7 %bitcast_divide_fusion = f32[64,8]{0,1:T(8,128)S(1)} fusion(f32[1,64,8]{1,2,0:T(8,128)} %param.14, f32[64]{0:T(128)S(1)} %exponential_reduce_fusion), kind=kLoop, calls=%fused_computation.63 | loop fusion | flops 512 | bytes 4352 | tf_op jit(solution)/shard_map/div | solution.py:31
  10.3 0.8 %bitcast_convert_fusion = f32[40,384]{1,0:T(8,128)S(1)} fusion(bf16[1,1,40,384]{3,2,1,0:T(8,128)(2,1)} %param.17), kind=kLoop, calls=%fused_computation.49 | loop fusion | flops 15360 | bytes 92160 | tf_op jit(solution)/shard_map/convert_element_type | solution.py:64
  11.2 0.1 reshape.480
  11.4 0.2 reduce-window.15
  11.6 0.1 reshape.470
  11.9 0.7 %exponential_reduce_fusion.1 = f32[64]{0:T(128)S(1)} fusion(f32[1,64,8]{1,2,0:T(8,128)} %param.12), kind=kLoop, calls=%fused_computation.70 | loop fusion | flops 448 | bytes 2304 | tf_op jit(solution)/shard_map/reduce_sum | solution.py:31
  12.6 0.7 %bitcast_divide_fusion.1 = f32[64,8]{0,1:T(8,128)S(1)} fusion(f32[1,64,8]{1,2,0:T(8,128)} %param.12, f32[64]{0:T(128)S(1)} %exponential_reduce_fusion.1), kind=kLoop, calls=%fused_computation.64 | loop fusion | flops 512 | bytes 4352 | tf_op jit(solution)/shard_map/div | solution.py:31
  13.3 0.7 %add_subtract_fusion = s32[64,8]{0,1:T(8,128)S(1)} fusion(s32[64,8]{0,1:T(8,128)S(1)} %copy.33, s32[64,8]{0,1:T(8,128)S(1)} %copy.34, s32[1,64,8]{1,2,0:T(8,128)} %param.13), kind=kLoop, calls=%fused_computation.65 | loop fusion | flops 2048 | bytes 8192 | tf_op jit(solution)/shard_map/sub | solution.py:22
  14.0 0.7 %add_subtract_fusion.1 = s32[64,8]{0,1:T(8,128)S(1)} fusion(s32[64,8]{0,1:T(8,128)S(1)} %copy.26, s32[64,8]{0,1:T(8,128)S(1)} %copy.27, s32[1,64,8]{1,2,0:T(8,128)} %param.11), kind=kLoop, calls=%fused_computation.66 | loop fusion | flops 2048 | bytes 8192 | tf_op jit(solution)/shard_map/sub | solution.py:22
  14.8 0.1 reshape.488
  15.5 0.4 convolution_convert_fusion.2
  15.9 0.7 %reshape.483 = bf16[8,5,2048]{2,1,0:T(8,128)(2,1)} broadcast(bf16[5,2048]{1,0:T(8,128)(2,1)S(1)} %convolution_convert_fusion.2), dimensions={1,2} | broadcast | bytes 184320 | tf_op jit(solution)/shard_map/reshape | solution.py:39
  16.7 3.7 %all-to-all-start.2 = ((bf16[8,5,2048]{2,1,0:T(8,128)(2,1)}), bf16[8,5,2048]{2,1,0:T(8,128)(2,1)S(1)}, u32[]{:S(2)}, u32[]{:S(2)}) async-start(bf16[8,5,2048]{2,1,0:T(8,128)(2,1)} %reshape.483), calls=%async_computation.2 | async-start | bytes 524288 | tf_op jit(solution)/shard_map/all_to_all | solution.py:113
  20.4 0.4 convolution_convert_fusion.3
  20.8 6.5 %all-to-all-done.2 = bf16[8,5,2048]{2,1,0:T(8,128)(2,1)S(1)} async-done(((bf16[8,5,2048]{2,1,0:T(8,128)(2,1)}), bf16[8,5,2048]{2,1,0:T(8,128)(2,1)S(1)}, u32[]{:S(2)}, u32[]{:S(2)}) %all-to-all-start.2) | async-done | bytes 163872 | tf_op jit(solution)/shard_map/all_to_all | solution.py:113
  27.3 0.7 %reshape.474 = bf16[8,5,2048]{2,1,0:T(8,128)(2,1)} broadcast(bf16[5,2048]{1,0:T(8,128)(2,1)S(1)} %convolution_convert_fusion.3), dimensions={1,2} | broadcast | bytes 184320 | tf_op jit(solution)/shard_map/reshape | solution.py:39
  28.0 3.4 %all-to-all-start = ((bf16[8,5,2048]{2,1,0:T(8,128)(2,1)}), bf16[8,5,2048]{2,1,0:T(8,128)(2,1)S(1)}, u32[]{:S(2)}, u32[]{:S(2)}) async-start(bf16[8,5,2048]{2,1,0:T(8,128)(2,1)} %reshape.474), calls=%async_computation | async-start | bytes 524288 | tf_op jit(solution)/shard_map/all_to_all | solution.py:108
  31.6 0.4 fusion.28
  31.9 0.7 %convolution_convert_fusion = bf16[40,2048]{1,0:T(8,128)(2,1)S(1)} fusion(bf16[1,1,2048,384]{3,2,1,0:T(8,128)(2,1)S(1)} %copy-done, bf16[40,192]{1,0:T(8,128)(2,1)S(1)} %get-tuple-element.3, bf16[40,192]{1,0:T(8,128)(2,1)S(1)} %get-tuple-element.2), kind=kOutput, calls=%fused_computation.2 | convolution fusion | flops 63057920 | bytes 1767424 | tf_op jit(solution)/shard_map/rk,dk->rd/dot_general | solution.py:72
  32.7 0.8 %reshape.485 = bf16[8,5,2048]{2,1,0:T(8,128)(2,1)} reshape(bf16[40,2048]{1,0:T(8,128)(2,1)S(1)} %convolution_convert_fusion) | data formatting | bytes 327680 | tf_op jit(solution)/shard_map/reshape | solution.py:75
  33.4 4.9 %all-to-all-done = bf16[8,5,2048]{2,1,0:T(8,128)(2,1)S(1)} async-done(((bf16[8,5,2048]{2,1,0:T(8,128)(2,1)}), bf16[8,5,2048]{2,1,0:T(8,128)(2,1)S(1)}, u32[]{:S(2)}, u32[]{:S(2)}) %all-to-all-start) | async-done | bytes 163872 | tf_op jit(solution)/shard_map/all_to_all | solution.py:108
  38.3 3.4 %all-to-all-start.3 = ((bf16[8,5,2048]{2,1,0:T(8,128)(2,1)}), bf16[8,5,2048]{2,1,0:T(8,128)(2,1)S(1)}, u32[]{:S(2)}, u32[]{:S(2)}) async-start(bf16[8,5,2048]{2,1,0:T(8,128)(2,1)} %reshape.485), calls=%async_computation.3 | async-start | bytes 524288 | tf_op jit(solution)/shard_map/all_to_all | solution.py:115
  41.8 0.3 fusion.6
  42.2 0.3 convolution_convert_fusion.1
  42.5 0.8 %reshape.476 = bf16[8,5,2048]{2,1,0:T(8,128)(2,1)} reshape(bf16[40,2048]{1,0:T(8,128)(2,1)S(1)} %convolution_convert_fusion.1) | data formatting | bytes 327680 | tf_op jit(solution)/shard_map/reshape | solution.py:57
  43.3 5.3 %all-to-all-done.3 = bf16[8,5,2048]{2,1,0:T(8,128)(2,1)S(1)} async-done(((bf16[8,5,2048]{2,1,0:T(8,128)(2,1)}), bf16[8,5,2048]{2,1,0:T(8,128)(2,1)S(1)}, u32[]{:S(2)}, u32[]{:S(2)}) %all-to-all-start.3) | async-done | bytes 163872 | tf_op jit(solution)/shard_map/all_to_all | solution.py:115
  48.6 3.4 %all-to-all-start.1 = ((bf16[8,5,2048]{2,1,0:T(8,128)(2,1)}), bf16[8,5,2048]{2,1,0:T(8,128)(2,1)S(1)}, u32[]{:S(2)}, u32[]{:S(2)}) async-start(bf16[8,5,2048]{2,1,0:T(8,128)(2,1)} %reshape.476), calls=%async_computation.1 | async-start | bytes 524288 | tf_op jit(solution)/shard_map/all_to_all | solution.py:112
  52.1 4.7 %convolution_reduce_fusion = f32[64,2048]{1,0:T(8,128)S(1)} fusion(s32[64,8]{1,0:T(8,128)S(1)} %copy.36, s32[64,8]{1,0:T(8,128)S(1)} %copy.35, f32[5,2048]{1,0:T(8,128)S(1)} %convert_reduce_fusion), kind=kOutput, calls=%fused_computation.10 | convolution fusion | flops 63839744 | bytes 569344 | tf_op jit(solution)/shard_map/dot_general | solution.py:46
  56.9 2.1 %all-to-all-done.1 = bf16[8,5,2048]{2,1,0:T(8,128)(2,1)S(1)} async-done(((bf16[8,5,2048]{2,1,0:T(8,128)(2,1)}), bf16[8,5,2048]{2,1,0:T(8,128)(2,1)S(1)}, u32[]{:S(2)}, u32[]{:S(2)}) %all-to-all-start.1) | async-done | bytes 163872 | tf_op jit(solution)/shard_map/all_to_all | solution.py:112
  59.0 4.8 %multiply_reduce_fusion = f32[64,2048]{1,0:T(8,128)S(1)} fusion(f32[64,8]{1,0:T(8,128)S(1)} %copy.31, s32[64,8]{1,0:T(8,128)S(1)} %copy.29, s32[64,8]{1,0:T(8,128)S(1)} %copy.28, f32[5,2048]{1,0:T(8,128)S(1)} %convert_reduce_fusion.1), kind=kOutput, calls=%fused_computation.1 | convolution fusion | flops 64888320 | bytes 571392 | tf_op jit(solution)/shard_map/dot_general | solution.py:46
  63.8 0.8 %fusion.13 = bf16[1,64,2048]{2,1,0:T(8,128)(2,1)} fusion(f32[64,2048]{1,0:T(8,128)S(1)} %convolution_reduce_fusion, bf16[64,2048]{1,0:T(8,128)(2,1)S(1)} %collective-permute-done.1), kind=kLoop, calls=%fused_computation.23 | loop fusion | flops 393216 | bytes 1048576 | tf_op jit(solution)/shard_map/broadcast_in_dim | solution.py:123
  64.6 0.8 %fusion.12 = bf16[1,64,2048]{2,1,0:T(8,128)(2,1)} fusion(f32[64,2048]{1,0:T(8,128)S(1)} %multiply_reduce_fusion, bf16[64,2048]{1,0:T(8,128)(2,1)S(1)} %copy-done.3), kind=kLoop, calls=%fused_computation.22 | loop fusion | flops 393216 | bytes 1048576 | tf_op jit(solution)/shard_map/broadcast_in_dim | solution.py:123
  (32 shorter events, 1.4 us)
Async XLA Ops:
  0.6 31.3 %copy-start = (bf16[1,1,2048,384]{3,2,1,0:T(8,128)(2,1)S(1)}, bf16[1,1,2048,384]{3,2,1,0:T(8,128)(2,1)}, u32[]{:S(2)}) copy-start(bf16[1,1,2048,384]{3,2,1,0:T(8,128)(2,1)} %param.15) | copy-start | bytes 4718596
  0.6 14.8 %collective-permute-start.1 = (bf16[64,2048]{1,0:T(8,128)(2,1)}, bf16[64,2048]{1,0:T(8,128)(2,1)S(1)}, u32[]{:S(2)}, u32[]{:S(2)}) collective-permute-start(bf16[64,2048]{1,0:T(8,128)(2,1)} %bitcast.75), channel_id=1, source_target_pairs={{0,24},{8,0},{16,8},{24,16},{1,25},{9,1},{17,9},{25,17},{2,26},{10... | collective-permute-start | bytes 786440 | tf_op jit(solution)/shard_map/ppermute | solution.py:14
  5.7 14.6 %collective-permute-start = (bf16[64,2048]{1,0:T(8,128)(2,1)}, bf16[64,2048]{1,0:T(8,128)(2,1)S(1)}, u32[]{:S(2)}, u32[]{:S(2)}) collective-permute-start(bf16[64,2048]{1,0:T(8,128)(2,1)} %bitcast.76), channel_id=1, source_target_pairs={{0,8},{8,16},{16,24},{24,0},{1,9},{9,17},{17,25},{25,1},{2,10},{10... | collective-permute-start | bytes 786440 | tf_op jit(solution)/shard_map/ppermute | solution.py:14
  15.9 15.6 %copy-start.1 = (bf16[1,1,192,2048]{3,2,1,0:T(8,128)(2,1)S(1)}, bf16[1,1,192,2048]{3,2,1,0:T(8,128)(2,1)}, u32[]{:S(2)}) copy-start(bf16[1,1,192,2048]{3,2,1,0:T(8,128)(2,1)} %param.16) | copy-start | bytes 2359300
  16.7 10.7 %all-to-all-start.2 = ((bf16[8,5,2048]{2,1,0:T(8,128)(2,1)}), bf16[8,5,2048]{2,1,0:T(8,128)(2,1)S(1)}, u32[]{:S(2)}, u32[]{:S(2)}) async-start(bf16[8,5,2048]{2,1,0:T(8,128)(2,1)} %reshape.483), calls=%async_computation.2 | async-start | bytes 524288 | tf_op jit(solution)/shard_map/all_to_all | solution.py:113
  20.4 7.7 %copy-start.2 = (bf16[64,2048]{1,0:T(8,128)(2,1)}, bf16[64,2048]{1,0:T(8,128)(2,1)S(1)}, u32[]{:S(2)}) copy-start(bf16[64,2048]{1,0:T(8,128)(2,1)S(1)} %collective-permute-done) | copy-start | bytes 786436
  28.0 10.3 %all-to-all-start = ((bf16[8,5,2048]{2,1,0:T(8,128)(2,1)}), bf16[8,5,2048]{2,1,0:T(8,128)(2,1)S(1)}, u32[]{:S(2)}, u32[]{:S(2)}) async-start(bf16[8,5,2048]{2,1,0:T(8,128)(2,1)} %reshape.474), calls=%async_computation | async-start | bytes 524288 | tf_op jit(solution)/shard_map/all_to_all | solution.py:108
  38.3 10.3 %all-to-all-start.3 = ((bf16[8,5,2048]{2,1,0:T(8,128)(2,1)}), bf16[8,5,2048]{2,1,0:T(8,128)(2,1)S(1)}, u32[]{:S(2)}, u32[]{:S(2)}) async-start(bf16[8,5,2048]{2,1,0:T(8,128)(2,1)} %reshape.485), calls=%async_computation.3 | async-start | bytes 524288 | tf_op jit(solution)/shard_map/all_to_all | solution.py:115
  48.6 10.3 %all-to-all-start.1 = ((bf16[8,5,2048]{2,1,0:T(8,128)(2,1)}), bf16[8,5,2048]{2,1,0:T(8,128)(2,1)S(1)}, u32[]{:S(2)}, u32[]{:S(2)}) async-start(bf16[8,5,2048]{2,1,0:T(8,128)(2,1)} %reshape.476), calls=%async_computation.1 | async-start | bytes 524288 | tf_op jit(solution)/shard_map/all_to_all | solution.py:112
  59.0 5.6 %copy-start.3 = (bf16[64,2048]{1,0:T(8,128)(2,1)S(1)}, bf16[64,2048]{1,0:T(8,128)(2,1)}, u32[]{:S(2)}) copy-start(bf16[64,2048]{1,0:T(8,128)(2,1)} %copy-done.2) | copy-start | bytes 786436
where the time goes:
time: 66.2 us; the launch traced here: 65.3 us
  starting transfers between devices  19.1 us (29%)
  waiting for transfers between devices  18.8 us (28%)
  matrix products  12.1 us (18%)
  other arithmetic  9.12 us (14%)
  local copies, waits for them, and re-layouts  5.35 us (8%)
  between operations  0.83 us (1%)
    dot_general x2, matrix products, collect(): jnp.dot(table.astype(jnp.float32), summed, precision=lax.Precision.HIGHEST)  9.58 us
    all_to_all x1, waiting for transfers between devices, shards(): lax.all_to_all(backward_slots, 'expert', split_axis=0, concat_axis=0, til...  6.54 us
    all_to_all x1, waiting for transfers between devices, shards(): lax.all_to_all(partial_b, 'expert', split_axis=0, concat_axis=0, tiled=True)  5.35 us
    ppermute x2, starting transfers between devices, from_behind(): return lax.ppermute(value, axis, pairs)  5.1 us
    all_to_all x1, waiting for transfers between devices, shards(): lax.all_to_all(forward_slots, 'expert', split_axis=0, concat_axis=0, tile...  4.89 us
    all_to_all x1, starting transfers between devices, shards(): lax.all_to_all(backward_slots, 'expert', split_axis=0, concat_axis=0, til...  3.72 us
    all_to_all x1, starting transfers between devices, shards(): lax.all_to_all(forward_slots, 'expert', split_axis=0, concat_axis=0, tile...  3.41 us
    all_to_all x1, starting transfers between devices, shards(): lax.all_to_all(partial_value, 'expert', split_axis=0, concat_axis=0, tile...  3.41 us
  transfers between devices with their start and end apart: 6, of which 4 were waited for; matrix products, arithmetic and copies ran while one was open for 30% of the time, Pallas kernels for 0%

commit v1 on v0

v1 whole, which is shorter than its diff:
```python
import functools

import jax
import jax.numpy as jnp
from jax import lax
from jax.experimental import pallas as pl
from jax.experimental.pallas import tpu as pltpu
from jax.sharding import PartitionSpec as P

FSPLIT = 8
CAP = 5
CORES = 2
SLOTS = 8
PAIR = 2 * SLOTS
MIB = 1 << 20


def along_sections(value, steps):
    count = lax.axis_size("segment")
    pairs = [(source, (source + steps) % count) for source in range(count)]
    return lax.ppermute(value, "segment", pairs)


def across_owners(value, flip):
    count = lax.axis_size("expert")
    return lax.ppermute(value, "expert", [(source, source ^ flip) for source in range(count)])


def in_vmem(count):
    return [pl.BlockSpec(memory_space=pltpu.VMEM)] * count


def call(kernel, outs, args, limit, flops, moved):
    return pl.pallas_call(
        kernel,
        out_shape=outs,
        in_specs=in_vmem(len(args)),
        out_specs=jax.tree.map(lambda _: pl.BlockSpec(memory_space=pltpu.VMEM), outs),
        compiler_params=pltpu.CompilerParams(vmem_limit_bytes=limit),
        cost_estimate=pl.CostEstimate(flops=flops, bytes_accessed=moved, transcendentals=0),
    )(*args)


def dot(left, right):
    return jnp.dot(left, right, preferred_element_type=jnp.float32)


def dot_rows(left, right):
    return lax.dot_general(left, right, (((1,), (1,)), ((), ())), preferred_element_type=jnp.float32)


def prepare_kernel(
    groups,
    chips,
    mixed,
    routes_a,
    logits_a,
    routes_b,
    logits_b,
    saved_own,
    saved_pair,
    pick_x,
    pick_u,
    place_x,
    place_u,
    send_scale,
    sum_scale,
    *factors,
):
    toks = routes_a.shape[1]
    top = routes_a.shape[2]
    before = lax.broadcasted_iota(jnp.int32, (toks, toks), 0) < lax.broadcasted_iota(
        jnp.int32, (toks, toks), 1
    )
    before = before.astype(jnp.float32).astype(jnp.bfloat16)
    after = lax.broadcasted_iota(jnp.int32, (toks, toks), 0) > lax.broadcasted_iota(
        jnp.int32, (toks, toks), 1
    )
    after = after.astype(jnp.float32).astype(jnp.bfloat16)
    row = lax.broadcasted_iota(jnp.int32, (PAIR, toks), 0)
    lane = lax.broadcasted_iota(jnp.int32, (toks, place_x.shape[1]), 1)
    half_row = lax.broadcasted_iota(jnp.int32, (PAIR, 128), 0)
    ones = jnp.ones((PAIR, top), jnp.bfloat16)

    def micro(routes, logits, offset):
        scores = jnp.exp(logits[0])
        probs = scores / jnp.sum(scores, axis=1, keepdims=True)
        picks, scales = [], []
        place = jnp.zeros((toks, place_x.shape[1]), jnp.float32)
        for group in range(groups):
            hit = (routes[0] == group).astype(jnp.float32)
            along = dot_rows(ones, hit.astype(jnp.bfloat16))
            rank = dot(along.astype(jnp.bfloat16), before)
            pick = jnp.where(rank == (row - offset).astype(jnp.float32), along, 0.0)
            prob = jnp.sum(hit * probs, axis=1, keepdims=True)
            scales.append(
                jnp.dot(
                    pick,
                    jnp.broadcast_to(prob, (toks, 128)),
                    preferred_element_type=jnp.float32,
                    precision=lax.Precision.HIGHEST,
                )
            )
            picks.append(pick)
            down = jnp.broadcast_to(jnp.sum(hit, axis=1, keepdims=True), place.shape)
            down_rank = dot(after, down.astype(jnp.bfloat16))
            spot = lane % (groups * PAIR) - group * PAIR - offset
            place = place + jnp.where(down_rank == spot.astype(jnp.float32), down, 0.0)
        return picks, scales, place

    picks_a, scales_a, place_a = micro(routes_a, logits_a, 0)
    picks_b, scales_b, place_b = micro(routes_b, logits_b, SLOTS)
    for group in range(groups):
        rows = pl.ds(group * PAIR, PAIR)
        pick_x[rows, :] = picks_a[group].astype(jnp.bfloat16)
        pick_u[rows, :] = picks_b[group].astype(jnp.bfloat16)
        send_scale[rows, :] = jnp.where(half_row < SLOTS, 1.0, scales_b[group])
        sum_scale[rows, :] = jnp.where(half_row < SLOTS, scales_a[group], 1.0)
    place_x[...] = place_a.astype(jnp.bfloat16)
    place_u[...] = place_b.astype(jnp.bfloat16)

    me = lax.axis_index("expert")
    held = saved_own.shape[2]
    line = lax.broadcasted_iota(jnp.int32, (chips * PAIR, held), 0)
    origin = line // PAIR
    if mixed:
        origin = origin ^ (me // CORES)
    slot = line % PAIR - SLOTS
    wanted = (CORES * origin + me % CORES) * CAP + slot
    wanted = jnp.where((slot >= 0) & (slot < CAP), wanted, -1)
    chosen = (wanted == lax.broadcasted_iota(jnp.int32, (chips * PAIR, held), 1)).astype(jnp.float32)
    chosen = chosen.astype(jnp.bfloat16)
    for owner, saved in enumerate((saved_own, saved_pair)):
        stored = dot(chosen, saved[0, 0])
        half = stored.shape[1] // 2
        gate = stored[:, :half]
        upper = stored[:, half:]
        logistic = jax.nn.sigmoid(gate)
        factors[owner][:, :half] = upper * logistic * (1.0 + gate * (1.0 - logistic))
        factors[owner][:, half:] = gate * logistic


def select_kernel(groups, x, u, pick_x, pick_u, send_scale, message):
    for group in range(groups):
        rows = pl.ds(group * PAIR, PAIR)
        chosen = dot(pick_x[rows, :], x[0]) + dot(pick_u[rows, :], u[0])
        message[group] = (chosen * send_scale[rows, :1]).astype(jnp.bfloat16)


def expert_kernel(chips, *refs):
    arrived = refs[:chips]
    entries = refs[chips : chips + 2]
    downs = refs[chips + 2 : chips + 4]
    factors = refs[chips + 4 : chips + 6]
    results = refs[chips + 6 :]
    rows = jnp.concatenate([ref[...] for ref in arrived], axis=0)
    total = None
    for entry, down, factor in zip(entries, downs, factors):
        half = down.shape[2]
        preacts = dot(rows, entry[0, 0])
        back = dot_rows(rows, down[0, 0])
        half = back.shape[1]
        line = lax.broadcasted_iota(jnp.int32, back.shape, 0) % PAIR
        gate = preacts[:, :half]
        hidden = gate * jax.nn.sigmoid(gate) * preacts[:, half:]
        hidden = jnp.where(line < SLOTS, hidden, 0.0).astype(jnp.bfloat16)
        grads = (jnp.concatenate([back, back], axis=1) * factor[...]).astype(jnp.bfloat16)
        part = dot(hidden, down[0, 0]) + dot_rows(grads, entry[0, 0])
        total = part if total is None else total + part
    total = total.astype(jnp.bfloat16)
    for index, ref in enumerate(results):
        ref[...] = total[index * PAIR : (index + 1) * PAIR]


def finish_kernel(groups, chips, *refs):
    x, u, place_x, place_u, sum_scale = refs[:5]
    returned = refs[5 : 5 + chips]
    out_x, out_u = refs[5 + chips :]
    share = chips // groups
    sums = []
    for group in range(groups):
        total = returned[group * share][...].astype(jnp.float32)
        for ref in returned[group * share + 1 : (group + 1) * share]:
            total = total + ref[...].astype(jnp.float32)
        sums.append(total * sum_scale[pl.ds(group * PAIR, PAIR), :1])
    rest = sums[0] if groups == 1 else jnp.concatenate(sums, axis=0)
    pieces = []
    for _ in range(3):
        piece = rest.astype(jnp.bfloat16)
        pieces.append(piece)
        rest = rest - piece.astype(jnp.float32)
    pieces = jnp.concatenate(pieces, axis=0)
    out_x[0] = (x[0].astype(jnp.float32) + dot(place_x[...], pieces)).astype(jnp.bfloat16)
    out_u[0] = (u[0].astype(jnp.float32) + dot(place_u[...], pieces)).astype(jnp.bfloat16)


def shards(
    section_output,
    section_gradient,
    forward_routes,
    forward_logits,
    backward_routes,
    backward_logits,
    entry_weights,
    down_weights,
    saved_projections,
):
    owners = lax.axis_size("expert")
    groups = owners // FSPLIT
    chips = owners // CORES
    direct = chips == 4
    toks, width = section_output.shape[1:]
    half = down_weights.shape[2]
    shape = jax.ShapeDtypeStruct
    bf16, f32 = jnp.bfloat16, jnp.float32

    layer_input = along_sections(section_output, 1)
    upstream = along_sections(section_gradient, -1)
    saved_pair = across_owners(saved_projections, 1)
    entry_pair = across_owners(entry_weights, 1)
    down_pair = across_owners(down_weights, 1)

    prepared = call(
        functools.partial(prepare_kernel, groups, chips, direct),
        (
            shape((groups * PAIR, toks), bf16),
            shape((groups * PAIR, toks), bf16),
            shape((toks, 3 * groups * PAIR), bf16),
            shape((toks, 3 * groups * PAIR), bf16),
            shape((groups * PAIR, 128), f32),
            shape((groups * PAIR, 128), f32),
            shape((chips * PAIR, 2 * half), f32),
            shape((chips * PAIR, 2 * half), f32),
        ),
        (
            forward_routes,
            forward_logits,
            backward_routes,
            backward_logits,
            saved_projections,
            saved_pair,
        ),
        8 * MIB,
        10_000_000,
        1_000_000,
    )
    pick_x, pick_u, place_x, place_u, send_scale, sum_scale, factor_own, factor_pair = prepared

    message = call(
        functools.partial(select_kernel, groups),
        shape((groups, PAIR, width), bf16),
        (layer_input, upstream, pick_x, pick_u, send_scale),
        8 * MIB,
        10_000_000,
        1_000_000,
    )
    if direct:
        arrived = [message[0]] + [across_owners(message[0], CORES * flip) for flip in range(1, chips)]
    else:
        same_core = [list(range(core, owners, CORES)) for core in range(CORES)]
        spread = jnp.repeat(message, chips // groups, axis=0)
        gathered = lax.all_to_all(
            spread, "expert", 0, 0, axis_index_groups=same_core, tiled=True
        )
        arrived = [gathered[index] for index in range(chips)]
    results = call(
        functools.partial(expert_kernel, chips),
        (shape((PAIR, width), bf16),) * chips,
        (
            *arrived,
            entry_weights,
            entry_pair,
            down_weights,
            down_pair,
            factor_own,
            factor_pair,
        ),
        24 * MIB,
        800_000_000,
        5_000_000,
    )
    if direct:
        returned = [results[0]] + [
            across_owners(results[flip], CORES * flip) for flip in range(1, chips)
        ]
    else:
        gathered = lax.all_to_all(
            jnp.stack(results), "expert", 0, 0, axis_index_groups=same_core, tiled=True
        )
        returned = [gathered[index] for index in range(chips)]
    return call(
        functools.partial(finish_kernel, groups, chips),
        (shape((1, toks, width), bf16), shape((1, toks, width), bf16)),
        (layer_input, upstream, place_x, place_u, sum_scale, *returned),
        16 * MIB,
        10_000_000,
        1_000_000,
    )


def solution(mesh):
    rows = P("segment", "expert", None)
    blocks = P("segment", "expert", None, None)
    return jax.shard_map(
        shards,
        mesh=mesh,
        in_specs=(rows,) * 6 + (blocks,) * 3,
        out_specs=(rows, rows),
        check_vma=False,
    )
```

time: 66.2 us -> 39.5 us (0.60)
  matrix products: 12.1 us -> 0 us
  other arithmetic: 9.12 us -> 0 us
  starting transfers between devices: 19.1 us -> 12.7 us
  Pallas kernels: 0 us -> 4.62 us
  waiting for transfers between devices: 18.8 us -> 14.8 us
  local copies, waits for them, and re-layouts: 5.35 us -> 6.36 us
    all_to_all x4 -> x0, waiting for transfers between devices: 18.8 us -> none  [the longest x1 6.54 us: shards(): lax.all_to_all(backward_slots, 'expert', split_axis=0, concat_axis=0, til...]
    ppermute x2 -> x11, waiting for transfers between devices: 0.01 us -> 14.8 us  [the longest x9 7.47 us: across_owners(): lax.ppermute(value, 'expert', [(source, source ^ flip) for source in rang...]
    all_to_all x4 -> x0, starting transfers between devices: 14 us -> none  [the longest x1 3.72 us: shards(): lax.all_to_all(backward_slots, 'expert', split_axis=0, concat_axis=0, til...]
    dot_general x8 -> x0, matrix products: 12.1 us -> none  [the longest x2 9.58 us: collect(): jnp.dot(table.astype(jnp.float32), summed, precision=lax.Precision.HIGHEST)]
    ppermute x2 -> x11, starting transfers between devices: 5.1 us -> 12.7 us  [the longest x9 7.71 us: across_owners(): lax.ppermute(value, 'expert', [(source, source ^ flip) for source in rang...]
    unnamed x8 -> x10, local copies, waits for them, and re-layouts: 0.03 us -> 6.36 us
    pallas_call x0 -> x4, Pallas kernels: none -> 4.62 us  [call(): pl.pallas_call(kernel, out_shape=outs, in_specs=in_vmem(len(args)), out_s...]
    reshape x6 -> x0, local copies, waits for them, and re-layouts: 3.16 us -> none  [the longest x2 1.45 us: dispatch(): return jnp.repeat(slots, FSPLIT, axis=0)]
  transfers between devices with their start and end apart: 6 -> 11, of which waited for: 4 -> 8; matrix products, arithmetic and copies ran while one was open for 30% -> 8% of each run, Pallas kernels for 0% -> 2%
where the time goes in v1:
time: 39.5 us; the launch traced here: 39.2 us
  waiting for transfers between devices  14.8 us (37%)
  starting transfers between devices  12.7 us (32%)
  local copies, waits for them, and re-layouts  6.36 us (16%)
  Pallas kernels  4.62 us (12%)
  between operations  0.68 us (2%)
    ppermute x9, starting transfers between devices, across_owners(): lax.ppermute(value, 'expert', [(source, source ^ flip) for source in rang...  7.71 us
    ppermute x9, waiting for transfers between devices, across_owners(): lax.ppermute(value, 'expert', [(source, source ^ flip) for source in rang...  7.47 us
    ppermute x2, waiting for transfers between devices, along_sections(): return lax.ppermute(value, 'segment', pairs)  7.3 us
    unnamed x10, local copies, waits for them, and re-layouts  6.36 us
    ppermute x2, starting transfers between devices, along_sections(): return lax.ppermute(value, 'segment', pairs)  5.03 us
    pallas_call x4, Pallas kernels, call(): pl.pallas_call(kernel, out_shape=outs, in_specs=in_vmem(len(args)), out_s...  4.62 us
  transfers between devices with their start and end apart: 11, of which 8 were waited for; matrix products, arithmetic and copies ran while one was open for 8% of the time, Pallas kernels for 2%

profile of v1, /device:TPU:0, one launch (start us, length us, event | category | flops | bytes accessed | tf_op | source)
XLA Modules:
  0.0 39.2 jit_solution(11855068510016480869)
XLA Ops:
  0.6 0.5 %collective-permute-start.6 = (bf16[1,1,2048,384]{3,2,1,0:T(8,128)(2,1)}, bf16[1,1,2048,384]{3,2,1,0:T(8,128)(2,1)S(1)}, u32[]{:S(2)}, u32[]{:S(2)}) collective-permute-start(bf16[1,1,2048,384]{3,2,1,0:T(8,128)(2,1)} %refs_4_.1), channel_id=1, source_target_pairs={{0,1},{1,0},{2,3},{3,2},{4,5},{5,4},{6,7},{7,6},{8,9},{9,8},{10,11... | collective-permute-start | bytes 4718600 | tf_op jit(solution)/shard_map/ppermute | solution.py:26
  1.1 0.1 collective-permute-start.7
  1.2 3.0 %collective-permute-start = (bf16[1,64,2048]{2,1,0:T(8,128)(2,1)}, bf16[1,64,2048]{2,1,0:T(8,128)(2,1)S(1)}, u32[]{:S(2)}, u32[]{:S(2)}) collective-permute-start(bf16[1,64,2048]{2,1,0:T(8,128)(2,1)} %param.9), channel_id=1, source_target_pairs={{0,8},{8,16},{16,24},{24,0},{1,9},{9,17},{17,25},{25,1},{2,10},{10... | collective-permute-start | bytes 786440 | tf_op jit(solution)/shard_map/ppermute | solution.py:21
  4.2 2.0 %collective-permute-start.1 = (bf16[1,64,2048]{2,1,0:T(8,128)(2,1)}, bf16[1,64,2048]{2,1,0:T(8,128)(2,1)S(1)}, u32[]{:S(2)}, u32[]{:S(2)}) collective-permute-start(bf16[1,64,2048]{2,1,0:T(8,128)(2,1)} %param.10), channel_id=1, source_target_pairs={{0,24},{8,0},{16,8},{24,16},{1,25},{9,1},{17,9},{25,17},{2,26},{10... | collective-permute-start | bytes 786440 | tf_op jit(solution)/shard_map/ppermute | solution.py:21
  6.3 0.0 collective-permute-start.2
  6.3 0.8 %copy.11.routes_a = s32[1,64,8]{2,1,0:T(8,128)S(1)} copy(s32[1,64,8]{1,2,0:T(8,128)} %param.11) | data formatting | bytes 4096 | tf_op args[2]
  7.0 0.8 %copy.12.logits_a = f32[1,64,8]{2,1,0:T(8,128)S(1)} copy(f32[1,64,8]{1,2,0:T(8,128)} %param.12) | data formatting | bytes 4096 | tf_op args[3]
  7.8 0.8 %copy.13.routes_b = s32[1,64,8]{2,1,0:T(8,128)S(1)} copy(s32[1,64,8]{1,2,0:T(8,128)} %param.13) | data formatting | bytes 4096 | tf_op args[4]
  8.6 0.8 %copy.14.logits_b = f32[1,64,8]{2,1,0:T(8,128)S(1)} copy(f32[1,64,8]{1,2,0:T(8,128)} %param.14) | data formatting | bytes 4096 | tf_op args[5]
  9.3 0.0 collective-permute-done.2.saved_pair
  9.3 0.0 copy-start.2
  9.4 0.7 %copy-done.2 = bf16[1,1,40,384]{3,2,1,0:T(8,128)(2,1)S(1)} copy-done((bf16[1,1,40,384]{3,2,1,0:T(8,128)(2,1)S(1)}, bf16[1,1,40,384]{3,2,1,0:T(8,128)(2,1)}, u32[]{:S(2)}) %copy-start.2) | copy-done | bytes 30744
  10.1 0.7 %shard_map.104 = (bf16[16,64]{1,0:T(8,128)(2,1)S(1)}, bf16[16,64]{1,0:T(8,128)(2,1)S(1)}, bf16[64,48]{1,0:T(8,128)(2,1)S(1)}, bf16[64,48]{1,0:T(8,128)(2,1)S(1)}...) custom-call(s32[1,64,8]{2,1,0:T(8,128)S(1)} %copy.11.routes_a, ...), custom_call_target="tpu_custom_call" | custom-call | flops 10000000 | bytes 1000000 | tf_op jit(solution)/shard_map/pallas_call | solution.py:34
  10.8 2.8 %collective-permute-done.x.refs_0_ = bf16[1,64,2048]{2,1,0:T(8,128)(2,1)S(1)} collective-permute-done((bf16[1,64,2048]{2,1,0:T(8,128)(2,1)}, bf16[1,64,2048]{2,1,0:T(8,128)(2,1)S(1)}, u32[]{:S(2)}, u32[]{:S(2)}) %collective-permute-start) | collective-permute-done | bytes 262176 | tf_op jit(solution)/shard_map/ppermute | solution.py:21
  13.6 4.5 %collective-permute-done.1.u.refs_1_ = bf16[1,64,2048]{2,1,0:T(8,128)(2,1)S(1)} collective-permute-done((bf16[1,64,2048]{2,1,0:T(8,128)(2,1)}, bf16[1,64,2048]{2,1,0:T(8,128)(2,1)S(1)}, u32[]{:S(2)}, u32[]{:S(2)}) %collective-permute-start.1) | collective-permute-done | bytes 262176 | tf_op jit(solution)/shard_map/ppermute | solution.py:21
  18.1 0.2 shard_map.105
  18.3 2.5 %collective-permute-start.5 = (bf16[16,2048]{1,0:T(8,128)(2,1)S(1)}, bf16[16,2048]{1,0:T(8,128)(2,1)S(1)}, u32[]{:S(2)}, u32[]{:S(2)}) collective-permute-start(bf16[16,2048]{1,0:T(8,128)(2,1)S(1)} %bitcast.1), channel_id=1, source_target_pairs={{0,6},{1,7},{2,4},{3,5},{4,2},{5,3},{6,0},{7,1},{8,14},{9,15},{10,... | collective-permute-start | bytes 196616 | tf_op jit(solution)/shard_map/ppermute | solution.py:26
  20.8 0.5 %collective-permute-start.4 = (bf16[16,2048]{1,0:T(8,128)(2,1)S(1)}, bf16[16,2048]{1,0:T(8,128)(2,1)S(1)}, u32[]{:S(2)}, u32[]{:S(2)}) collective-permute-start(bf16[16,2048]{1,0:T(8,128)(2,1)S(1)} %bitcast.2), channel_id=1, source_target_pairs={{0,4},{1,5},{2,6},{3,7},{4,0},{5,1},{6,2},{7,3},{8,12},{9,13},{10,... | collective-permute-start | bytes 196616 | tf_op jit(solution)/shard_map/ppermute | solution.py:26
  21.3 0.5 %collective-permute-start.3 = (bf16[16,2048]{1,0:T(8,128)(2,1)S(1)}, bf16[16,2048]{1,0:T(8,128)(2,1)S(1)}, u32[]{:S(2)}, u32[]{:S(2)}) collective-permute-start(bf16[16,2048]{1,0:T(8,128)(2,1)S(1)} %bitcast.3), channel_id=1, source_target_pairs={{0,2},{1,3},{2,0},{3,1},{4,6},{5,7},{6,4},{7,5},{8,10},{9,11},{10,... | collective-permute-start | bytes 196616 | tf_op jit(solution)/shard_map/ppermute | solution.py:26
  21.8 1.8 %collective-permute-done.5.refs_3_ = bf16[16,2048]{1,0:T(8,128)(2,1)S(1)} collective-permute-done((bf16[16,2048]{1,0:T(8,128)(2,1)S(1)}, bf16[16,2048]{1,0:T(8,128)(2,1)S(1)}, u32[]{:S(2)}, u32[]{:S(2)}) %collective-permute-start.5) | collective-permute-done | bytes 65568 | tf_op jit(solution)/shard_map/ppermute | solution.py:26
  23.6 1.4 %collective-permute-done.4.refs_2_ = bf16[16,2048]{1,0:T(8,128)(2,1)S(1)} collective-permute-done((bf16[16,2048]{1,0:T(8,128)(2,1)S(1)}, bf16[16,2048]{1,0:T(8,128)(2,1)S(1)}, u32[]{:S(2)}, u32[]{:S(2)}) %collective-permute-start.4) | collective-permute-done | bytes 65568 | tf_op jit(solution)/shard_map/ppermute | solution.py:26
  25.0 0.5 %collective-permute-done.3.refs_1_ = bf16[16,2048]{1,0:T(8,128)(2,1)S(1)} collective-permute-done((bf16[16,2048]{1,0:T(8,128)(2,1)S(1)}, bf16[16,2048]{1,0:T(8,128)(2,1)S(1)}, u32[]{:S(2)}, u32[]{:S(2)}) %collective-permute-start.3) | collective-permute-done | bytes 65568 | tf_op jit(solution)/shard_map/ppermute | solution.py:26
  25.5 0.0 collective-permute-done.7.refs_7_
  25.5 0.0 collective-permute-done.6.refs_5_
  25.6 0.0 copy-start
  25.6 1.4 %copy-done = bf16[1,1,2048,384]{3,2,1,0:T(8,128)(2,1)S(1)} copy-done((bf16[1,1,2048,384]{3,2,1,0:T(8,128)(2,1)S(1)}, bf16[1,1,2048,384]{3,2,1,0:T(8,128)(2,1)}, u32[]{:S(2)}) %copy-start) | copy-done | bytes 1572888
  27.0 0.0 copy-start.1
  27.0 1.1 %copy-done.1 = bf16[1,1,192,2048]{3,2,1,0:T(8,128)(2,1)S(1)} copy-done((bf16[1,1,192,2048]{3,2,1,0:T(8,128)(2,1)S(1)}, bf16[1,1,192,2048]{3,2,1,0:T(8,128)(2,1)}, u32[]{:S(2)}) %copy-start.1) | copy-done | bytes 786456
  28.1 2.7 %shard_map.106 = (bf16[16,2048]{1,0:T(8,128)(2,1)S(1)}, bf16[16,2048]{1,0:T(8,128)(2,1)S(1)}, bf16[16,2048]{1,0:T(8,128)(2,1)S(1)}, bf16[16,2048]{1,0:T(8,128)(2,1)S(1)}) custom-call(bf16[16,2048]{1,0:T(8,128)(2,1)S(1)} %bitcast.4, bf16[16,2048]{1,0:T(8,128)(2,1)S(1)} %collective-permute-done.3.refs_1_, bf16[16,2048]{1,0:T(8,128)(2,1)S(1)} %collective-permute-done.4.refs_2_, ...), custom_call_target="tpu_custom_call" | custom-call | flops 800000000 | bytes 5000000 | tf_op jit(solution)/shard_map/pallas_call | solution.py:34
  30.8 0.6 %collective-permute-start.8 = (bf16[16,2048]{1,0:T(8,128)(2,1)S(1)}, bf16[16,2048]{1,0:T(8,128)(2,1)S(1)}, u32[]{:S(2)}, u32[]{:S(2)}) collective-permute-start(bf16[16,2048]{1,0:T(8,128)(2,1)S(1)} %get-tuple-element.23), channel_id=1, source_target_pairs={{0,2},{1,3},{2,0},{3,1},{4,6},{5,7},{6,4},{7,5},{8,10},{9,11},{10,... | collective-permute-start | bytes 196616 | tf_op jit(solution)/shard_map/ppermute | solution.py:26
  31.4 1.5 %collective-permute-start.9 = (bf16[16,2048]{1,0:T(8,128)(2,1)S(1)}, bf16[16,2048]{1,0:T(8,128)(2,1)S(1)}, u32[]{:S(2)}, u32[]{:S(2)}) collective-permute-start(bf16[16,2048]{1,0:T(8,128)(2,1)S(1)} %get-tuple-element.24), channel_id=1, source_target_pairs={{0,4},{1,5},{2,6},{3,7},{4,0},{5,1},{6,2},{7,3},{8,12},{9,13},{10,... | collective-permute-start | bytes 196616 | tf_op jit(solution)/shard_map/ppermute | solution.py:26
  32.9 1.4 %collective-permute-start.10 = (bf16[16,2048]{1,0:T(8,128)(2,1)S(1)}, bf16[16,2048]{1,0:T(8,128)(2,1)S(1)}, u32[]{:S(2)}, u32[]{:S(2)}) collective-permute-start(bf16[16,2048]{1,0:T(8,128)(2,1)S(1)} %get-tuple-element.25), channel_id=1, source_target_pairs={{0,6},{1,7},{2,4},{3,5},{4,2},{5,3},{6,0},{7,1},{8,14},{9,15},{10,... | collective-permute-start | bytes 196616 | tf_op jit(solution)/shard_map/ppermute | solution.py:26
  34.4 0.8 %collective-permute-done.8.refs_6_ = bf16[16,2048]{1,0:T(8,128)(2,1)S(1)} collective-permute-done((bf16[16,2048]{1,0:T(8,128)(2,1)S(1)}, bf16[16,2048]{1,0:T(8,128)(2,1)S(1)}, u32[]{:S(2)}, u32[]{:S(2)}) %collective-permute-start.8) | collective-permute-done | bytes 65568 | tf_op jit(solution)/shard_map/ppermute | solution.py:26
  35.1 0.8 %collective-permute-done.9.refs_7_ = bf16[16,2048]{1,0:T(8,128)(2,1)S(1)} collective-permute-done((bf16[16,2048]{1,0:T(8,128)(2,1)S(1)}, bf16[16,2048]{1,0:T(8,128)(2,1)S(1)}, u32[]{:S(2)}, u32[]{:S(2)}) %collective-permute-start.9) | collective-permute-done | bytes 65568 | tf_op jit(solution)/shard_map/ppermute | solution.py:26
  35.9 2.2 %collective-permute-done.10.refs_8_ = bf16[16,2048]{1,0:T(8,128)(2,1)S(1)} collective-permute-done((bf16[16,2048]{1,0:T(8,128)(2,1)S(1)}, bf16[16,2048]{1,0:T(8,128)(2,1)S(1)}, u32[]{:S(2)}, u32[]{:S(2)}) %collective-permute-start.10) | collective-permute-done | bytes 65568 | tf_op jit(solution)/shard_map/ppermute | solution.py:26
  38.1 1.1 %shard_map.107 = (bf16[1,64,2048]{2,1,0:T(8,128)(2,1)}, bf16[1,64,2048]{2,1,0:T(8,128)(2,1)}) custom-call(bf16[1,64,2048]{2,1,0:T(8,128)(2,1)S(1)} %collective-permute-done.x.refs_0_, bf16[1,64,2048]{2,1,0:T(8,128)(2,1)S(1)} %collective-permute-done.1.u.refs_1_, bf16[64,48]{1,0:T(8,128)(2,1)S(1)} %get-tuple-element.14.refs_2_, ...), custom_call_target="tpu_custom_call" | custom-call | flops 10000000 | bytes 1000000 | tf_op jit(solution)/shard_map/pallas_call | solution.py:34
Async XLA Ops:
  0.6 24.9 %collective-permute-start.6 = (bf16[1,1,2048,384]{3,2,1,0:T(8,128)(2,1)}, bf16[1,1,2048,384]{3,2,1,0:T(8,128)(2,1)S(1)}, u32[]{:S(2)}, u32[]{:S(2)}) collective-permute-start(bf16[1,1,2048,384]{3,2,1,0:T(8,128)(2,1)} %refs_4_.1), channel_id=1, source_target_pairs={{0,1},{1,0},{2,3},{3,2},{4,5},{5,4},{6,7},{7,6},{8,9},{9,8},{10,11... | collective-permute-start | bytes 4718600 | tf_op jit(solution)/shard_map/ppermute | solution.py:26
  1.1 24.4 %collective-permute-start.7 = (bf16[1,1,192,2048]{3,2,1,0:T(8,128)(2,1)}, bf16[1,1,192,2048]{3,2,1,0:T(8,128)(2,1)S(1)}, u32[]{:S(2)}, u32[]{:S(2)}) collective-permute-start(bf16[1,1,192,2048]{3,2,1,0:T(8,128)(2,1)} %refs_6_.1), channel_id=1, source_target_pairs={{0,1},{1,0},{2,3},{3,2},{4,5},{5,4},{6,7},{7,6},{8,9},{9,8},{10,11... | collective-permute-start | bytes 2359304 | tf_op jit(solution)/shard_map/ppermute | solution.py:26
  1.2 12.4 %collective-permute-start = (bf16[1,64,2048]{2,1,0:T(8,128)(2,1)}, bf16[1,64,2048]{2,1,0:T(8,128)(2,1)S(1)}, u32[]{:S(2)}, u32[]{:S(2)}) collective-permute-start(bf16[1,64,2048]{2,1,0:T(8,128)(2,1)} %param.9), channel_id=1, source_target_pairs={{0,8},{8,16},{16,24},{24,0},{1,9},{9,17},{17,25},{25,1},{2,10},{10... | collective-permute-start | bytes 786440 | tf_op jit(solution)/shard_map/ppermute | solution.py:21
  4.2 13.8 %collective-permute-start.1 = (bf16[1,64,2048]{2,1,0:T(8,128)(2,1)}, bf16[1,64,2048]{2,1,0:T(8,128)(2,1)S(1)}, u32[]{:S(2)}, u32[]{:S(2)}) collective-permute-start(bf16[1,64,2048]{2,1,0:T(8,128)(2,1)} %param.10), channel_id=1, source_target_pairs={{0,24},{8,0},{16,8},{24,16},{1,25},{9,1},{17,9},{25,17},{2,26},{10... | collective-permute-start | bytes 786440 | tf_op jit(solution)/shard_map/ppermute | solution.py:21
  6.3 3.1 %collective-permute-start.2 = (bf16[1,1,40,384]{3,2,1,0:T(8,128)(2,1)}, bf16[1,1,40,384]{3,2,1,0:T(8,128)(2,1)S(1)}, u32[]{:S(2)}, u32[]{:S(2)}) collective-permute-start(bf16[1,1,40,384]{3,2,1,0:T(8,128)(2,1)} %saved_own.1), channel_id=1, source_target_pairs={{0,1},{1,0},{2,3},{3,2},{4,5},{5,4},{6,7},{7,6},{8,9},{9,8},{10,11... | collective-permute-start | bytes 92168 | tf_op jit(solution)/shard_map/ppermute | solution.py:26
  9.3 0.8 %copy-start.2 = (bf16[1,1,40,384]{3,2,1,0:T(8,128)(2,1)S(1)}, bf16[1,1,40,384]{3,2,1,0:T(8,128)(2,1)}, u32[]{:S(2)}) copy-start(bf16[1,1,40,384]{3,2,1,0:T(8,128)(2,1)} %saved_own.1) | copy-start | bytes 92164
  18.3 5.3 %collective-permute-start.5 = (bf16[16,2048]{1,0:T(8,128)(2,1)S(1)}, bf16[16,2048]{1,0:T(8,128)(2,1)S(1)}, u32[]{:S(2)}, u32[]{:S(2)}) collective-permute-start(bf16[16,2048]{1,0:T(8,128)(2,1)S(1)} %bitcast.1), channel_id=1, source_target_pairs={{0,6},{1,7},{2,4},{3,5},{4,2},{5,3},{6,0},{7,1},{8,14},{9,15},{10,... | collective-permute-start | bytes 196616 | tf_op jit(solution)/shard_map/ppermute | solution.py:26
  20.8 4.3 %collective-permute-start.4 = (bf16[16,2048]{1,0:T(8,128)(2,1)S(1)}, bf16[16,2048]{1,0:T(8,128)(2,1)S(1)}, u32[]{:S(2)}, u32[]{:S(2)}) collective-permute-start(bf16[16,2048]{1,0:T(8,128)(2,1)S(1)} %bitcast.2), channel_id=1, source_target_pairs={{0,4},{1,5},{2,6},{3,7},{4,0},{5,1},{6,2},{7,3},{8,12},{9,13},{10,... | collective-permute-start | bytes 196616 | tf_op jit(solution)/shard_map/ppermute | solution.py:26
  21.3 4.3 %collective-permute-start.3 = (bf16[16,2048]{1,0:T(8,128)(2,1)S(1)}, bf16[16,2048]{1,0:T(8,128)(2,1)S(1)}, u32[]{:S(2)}, u32[]{:S(2)}) collective-permute-start(bf16[16,2048]{1,0:T(8,128)(2,1)S(1)} %bitcast.3), channel_id=1, source_target_pairs={{0,2},{1,3},{2,0},{3,1},{4,6},{5,7},{6,4},{7,5},{8,10},{9,11},{10,... | collective-permute-start | bytes 196616 | tf_op jit(solution)/shard_map/ppermute | solution.py:26
  25.6 1.4 %copy-start = (bf16[1,1,2048,384]{3,2,1,0:T(8,128)(2,1)S(1)}, bf16[1,1,2048,384]{3,2,1,0:T(8,128)(2,1)}, u32[]{:S(2)}) copy-start(bf16[1,1,2048,384]{3,2,1,0:T(8,128)(2,1)} %refs_4_.1) | copy-start | bytes 4718596
  27.0 1.1 %copy-start.1 = (bf16[1,1,192,2048]{3,2,1,0:T(8,128)(2,1)S(1)}, bf16[1,1,192,2048]{3,2,1,0:T(8,128)(2,1)}, u32[]{:S(2)}) copy-start(bf16[1,1,192,2048]{3,2,1,0:T(8,128)(2,1)} %refs_6_.1) | copy-start | bytes 2359300
  30.8 4.3 %collective-permute-start.8 = (bf16[16,2048]{1,0:T(8,128)(2,1)S(1)}, bf16[16,2048]{1,0:T(8,128)(2,1)S(1)}, u32[]{:S(2)}, u32[]{:S(2)}) collective-permute-start(bf16[16,2048]{1,0:T(8,128)(2,1)S(1)} %get-tuple-element.23), channel_id=1, source_target_pairs={{0,2},{1,3},{2,0},{3,1},{4,6},{5,7},{6,4},{7,5},{8,10},{9,11},{10,... | collective-permute-start | bytes 196616 | tf_op jit(solution)/shard_map/ppermute | solution.py:26
  31.4 4.5 %collective-permute-start.9 = (bf16[16,2048]{1,0:T(8,128)(2,1)S(1)}, bf16[16,2048]{1,0:T(8,128)(2,1)S(1)}, u32[]{:S(2)}, u32[]{:S(2)}) collective-permute-start(bf16[16,2048]{1,0:T(8,128)(2,1)S(1)} %get-tuple-element.24), channel_id=1, source_target_pairs={{0,4},{1,5},{2,6},{3,7},{4,0},{5,1},{6,2},{7,3},{8,12},{9,13},{10,... | collective-permute-start | bytes 196616 | tf_op jit(solution)/shard_map/ppermute | solution.py:26
  32.9 5.2 %collective-permute-start.10 = (bf16[16,2048]{1,0:T(8,128)(2,1)S(1)}, bf16[16,2048]{1,0:T(8,128)(2,1)S(1)}, u32[]{:S(2)}, u32[]{:S(2)}) collective-permute-start(bf16[16,2048]{1,0:T(8,128)(2,1)S(1)} %get-tuple-element.25), channel_id=1, source_target_pairs={{0,6},{1,7},{2,4},{3,5},{4,2},{5,3},{6,0},{7,1},{8,14},{9,15},{10,... | collective-permute-start | bytes 196616 | tf_op jit(solution)/shard_map/ppermute | solution.py:26

commit v2 on v1

v2 whole, which is shorter than its diff:
```python
import functools

import jax
import jax.numpy as jnp
from jax import lax
from jax.experimental import pallas as pl
from jax.experimental.pallas import tpu as pltpu
from jax.sharding import PartitionSpec as P

FSPLIT = 8
CAP = 5
CORES = 2
SLOTS = 8
PAIR = 2 * SLOTS
MIB = 1 << 20


def along_sections(value, steps):
    count = lax.axis_size("segment")
    pairs = [(source, (source + steps) % count) for source in range(count)]
    return lax.ppermute(value, "segment", pairs)


def across_owners(value, flip):
    count = lax.axis_size("expert")
    return lax.ppermute(value, "expert", [(source, source ^ flip) for source in range(count)])


def call(kernel, outs, args, limit, flops, moved, after=(), aliases=None, far=(), scratch=()):
    whole = pl.BlockSpec(memory_space=pltpu.VMEM)
    anywhere = pl.BlockSpec(memory_space=pl.ANY)
    distant = pl.BlockSpec(memory_space=pltpu.HBM)
    waits = len(after)

    def body(*refs):
        kernel(*refs[waits:])

    return pl.pallas_call(
        body,
        out_shape=outs,
        in_specs=[anywhere] * waits + [distant] * len(far) + [whole] * len(args),
        out_specs=jax.tree.map(lambda _: whole, outs),
        scratch_shapes=scratch,
        input_output_aliases={
            waits + len(far) + key: value for key, value in (aliases or {}).items()
        },
        compiler_params=pltpu.CompilerParams(vmem_limit_bytes=limit),
        cost_estimate=pl.CostEstimate(flops=flops, bytes_accessed=moved, transcendentals=0),
    )(*after, *[pltpu.with_memory_space_constraint(value, pltpu.HBM) for value in far], *args)


def dot(left, right):
    return jnp.dot(left, right, preferred_element_type=jnp.float32)


def hits(routes, group):
    return jnp.where(routes == group, 1.0, 0.0)


def slot_picks(routes, group, rows, offset):
    toks = routes.shape[1]
    shape = (toks, toks)
    before = lax.broadcasted_iota(jnp.int32, shape, 0) < lax.broadcasted_iota(jnp.int32, shape, 1)
    before = jnp.where(before, 1.0, 0.0).astype(jnp.bfloat16)
    along = jnp.sum(hits(routes, group), axis=0, keepdims=True)
    along = jnp.broadcast_to(along, (rows, toks))
    rank = dot(along.astype(jnp.bfloat16), before)
    slot = lax.broadcasted_iota(jnp.int32, (rows, toks), 0) - offset
    return jnp.where(rank == slot.astype(jnp.float32), along, 0.0)


def fetch(sources, targets, semaphores):
    copies = [
        pltpu.make_async_copy(source, target, semaphores.at[index])
        for index, (source, target) in enumerate(zip(sources, targets))
    ]
    for copy in copies:
        copy.start()
    for copy in copies:
        copy.wait()


def pick_kernel(groups, routes, staged, rows):
    picks = [slot_picks(routes[0], group, SLOTS, 0) for group in range(groups)]
    picks = picks[0] if groups == 1 else jnp.concatenate(picks, axis=0)
    rows[...] = dot(picks.astype(jnp.bfloat16), staged[0]).astype(jnp.bfloat16)


def merge_kernel(groups, x, pick_x, rows_b, send_scale, staged, message, whole):
    whole[...] = staged[...]
    all_a = dot(pick_x[...], x[0])
    all_b = rows_b[...].astype(jnp.float32)
    for group in range(groups):
        one = slice(group * SLOTS, (group + 1) * SLOTS)
        scaled = all_b[one] * send_scale[pl.ds(group * SLOTS, SLOTS), :1]
        both = [all_a[group * PAIR : group * PAIR + SLOTS], scaled]
        message[group] = jnp.concatenate(both, axis=0).astype(jnp.bfloat16)


def prepare_kernel(groups, *refs):
    far, refs = refs[:5], refs[5:]
    staged, pick_x, place_x, place_u, send_scale, sum_scale = refs[:6]
    near, semaphores, stage_semaphore = refs[6:10], refs[10], refs[11]
    stage = pltpu.make_async_copy(far[4], staged, stage_semaphore.at[0])
    stage.start()
    fetch(far[:4], near, semaphores)
    routes_a, logits_a, routes_b, logits_b = near

    def micro(routes, logits, offset):
        scores = jnp.exp(logits[0])
        probs = scores / jnp.sum(scores, axis=0, keepdims=True)
        picks, scales = [], []
        for group in range(groups):
            pick = slot_picks(routes[0], group, PAIR, offset)
            prob = jnp.sum(hits(routes[0], group) * probs, axis=0, keepdims=True)
            scales.append(jnp.sum(pick * prob, axis=1, keepdims=True))
            picks.append(pick)
        return picks, scales

    picks_a, scales_a = micro(routes_a, logits_a, 0)
    picks_b, scales_b = micro(routes_b, logits_b, SLOTS)
    place_x[...] = jnp.concatenate(picks_a * 3, axis=0).T.astype(jnp.bfloat16)
    place_u[...] = jnp.concatenate(picks_b * 3, axis=0).T.astype(jnp.bfloat16)
    half_row = lax.broadcasted_iota(jnp.int32, (PAIR, 128), 0)
    for group in range(groups):
        rows = pl.ds(group * PAIR, PAIR)
        pick_x[rows, :] = picks_a[group].astype(jnp.bfloat16)
        send_scale[pl.ds(group * SLOTS, SLOTS), :] = jnp.broadcast_to(
            scales_b[group][SLOTS:], (SLOTS, 128)
        )
        sum_scale[rows, :] = jnp.where(half_row < SLOTS, scales_a[group], 1.0)
    stage.wait()


def pack(index, chips, mixed, entry, down, saved, first, second, factors):
    half = down.shape[2]
    gate = slice(index * half, (index + 1) * half)
    upper = slice((2 + index) * half, (3 + index) * half)
    lower = slice((4 + index) * half, (5 + index) * half)
    first[:, gate] = entry[0, 0, :, :half]
    first[:, upper] = entry[0, 0, :, half:]
    first[:, lower] = down[0, 0].T
    second[gate, :] = entry[0, 0, :, :half].T
    second[upper, :] = entry[0, 0, :, half:].T
    second[lower, :] = down[0, 0]

    me = lax.axis_index("expert")
    held = saved.shape[2]
    shape = (chips * PAIR, held)
    line = lax.broadcasted_iota(jnp.int32, shape, 0)
    origin = line // PAIR
    if mixed:
        origin = origin ^ (me // CORES)
    slot = line % PAIR - SLOTS
    wanted = (CORES * origin + me % CORES) * CAP + slot
    wanted = jnp.where((slot >= 0) & (slot < CAP), wanted, -1)
    chosen = jnp.where(wanted == lax.broadcasted_iota(jnp.int32, shape, 1), 1.0, 0.0)
    stored = dot(chosen.astype(jnp.bfloat16), saved[0, 0])
    gates = stored[:, :half]
    uppers = stored[:, half:]
    logistic = jax.nn.sigmoid(gates)
    factors[:, gate] = uppers * logistic * (1.0 + gates * (1.0 - logistic))
    factors[:, upper] = gates * logistic


def pack_own_kernel(chips, mixed, *refs):
    far, packs, near, semaphores = refs[:3], refs[3:6], refs[6:9], refs[9]
    fetch(far, near, semaphores)
    pack(0, chips, mixed, *near, *packs)


def pack_pair_kernel(chips, mixed, *refs):
    pack(1, chips, mixed, *refs[:3], *refs[6:])


def expert_kernel(chips, *refs):
    arrived = refs[:chips]
    first, second, factors = refs[chips : chips + 3]
    results = refs[chips + 3 :]
    rows = jnp.concatenate([ref[...] for ref in arrived], axis=0)
    made = dot(rows, first[...])
    both = made.shape[1] // 3
    gate = made[:, :both]
    upper = made[:, both : 2 * both]
    back = made[:, 2 * both :]
    line = lax.broadcasted_iota(jnp.int32, back.shape, 0) % PAIR
    hidden = jnp.where(line < SLOTS, gate * jax.nn.sigmoid(gate) * upper, 0.0)
    grads = jnp.concatenate([back, back], axis=1) * factors[...]
    inner = jnp.concatenate([grads.astype(jnp.bfloat16), hidden.astype(jnp.bfloat16)], axis=1)
    total = dot(inner, second[...]).astype(jnp.bfloat16)
    for index, ref in enumerate(results):
        ref[...] = total[index * PAIR : (index + 1) * PAIR]


def finish_kernel(groups, chips, *refs):
    x, u, place_x, place_u, sum_scale = refs[:5]
    returned = refs[5 : 5 + chips]
    out_x, out_u = refs[5 + chips :]
    share = chips // groups
    sums = []
    for group in range(groups):
        total = returned[group * share][...].astype(jnp.float32)
        for ref in returned[group * share + 1 : (group + 1) * share]:
            total = total + ref[...].astype(jnp.float32)
        sums.append(total * sum_scale[pl.ds(group * PAIR, PAIR), :1])
    rest = sums[0] if groups == 1 else jnp.concatenate(sums, axis=0)
    pieces = []
    for _ in range(3):
        piece = rest.astype(jnp.bfloat16)
        pieces.append(piece)
        rest = rest - piece.astype(jnp.float32)
    pieces = jnp.concatenate(pieces, axis=0)
    out_x[0] = (x[0].astype(jnp.float32) + dot(place_x[...], pieces)).astype(jnp.bfloat16)
    out_u[0] = (u[0].astype(jnp.float32) + dot(place_u[...], pieces)).astype(jnp.bfloat16)


def shards(
    section_output,
    section_gradient,
    forward_routes,
    forward_logits,
    backward_routes,
    backward_logits,
    entry_weights,
    down_weights,
    saved_projections,
):
    owners = lax.axis_size("expert")
    groups = owners // FSPLIT
    chips = owners // CORES
    direct = chips == 4
    toks, width = section_output.shape[1:]
    half = down_weights.shape[2]
    shape = jax.ShapeDtypeStruct
    bf16, f32 = jnp.bfloat16, jnp.float32
    routes_a, logits_a, routes_b, logits_b = [
        jnp.swapaxes(value, 1, 2)
        for value in (forward_routes, forward_logits, backward_routes, backward_logits)
    ]

    block = shape((1, toks, width), bf16)
    asked = along_sections(routes_b, 1)
    layer_input = along_sections(section_output, 1)
    own_values = (routes_a, logits_a, routes_b, logits_b)
    staged, pick_x, place_x, place_u, send_scale, sum_scale = call(
        functools.partial(prepare_kernel, groups),
        (
            block,
            shape((groups * PAIR, toks), bf16),
            shape((toks, 3 * groups * PAIR), bf16),
            shape((toks, 3 * groups * PAIR), bf16),
            shape((groups * SLOTS, 128), f32),
            shape((groups * PAIR, 128), f32),
        ),
        (),
        8 * MIB,
        10_000_000,
        1_000_000,
        far=(*own_values, section_gradient),
        scratch=[
            *[pltpu.VMEM(value.shape, value.dtype) for value in own_values],
            pltpu.SemaphoreType.DMA((len(own_values),)),
            pltpu.SemaphoreType.DMA((1,)),
        ],
    )
    rows_b = call(
        functools.partial(pick_kernel, groups),
        shape((groups * SLOTS, width), bf16),
        (asked, staged),
        8 * MIB,
        50_000_000_000,
        1_000_000_000,
    )
    weights = (entry_weights, down_weights, saved_projections)
    packs = (
        shape((width, 6 * half), bf16),
        shape((6 * half, width), bf16),
        shape((chips * PAIR, 4 * half), f32),
    )
    packed = call(
        functools.partial(pack_own_kernel, chips, direct),
        packs,
        (),
        8 * MIB,
        10_000_000,
        5_000_000,
        after=(rows_b,),
        far=weights,
        scratch=[
            *[pltpu.VMEM(value.shape, value.dtype) for value in weights],
            pltpu.SemaphoreType.DMA((len(weights),)),
        ],
    )
    rows_b = along_sections(rows_b, -1)
    weights = [across_owners(value, 1) for value in weights]
    message, whole = call(
        functools.partial(merge_kernel, groups),
        (shape((groups, PAIR, width), bf16), block),
        (layer_input, pick_x, rows_b, send_scale, staged),
        8 * MIB,
        100_000,
        100_000,
        after=(*packed, *weights),
    )
    upstream = along_sections(whole, -1)
    if direct:
        arrived = [message[0]] + [across_owners(message[0], CORES * flip) for flip in range(1, chips)]
    else:
        same_core = [list(range(core, owners, CORES)) for core in range(CORES)]
        spread = jnp.repeat(message, chips // groups, axis=0)
        gathered = lax.all_to_all(
            spread, "expert", 0, 0, axis_index_groups=same_core, tiled=True
        )
        arrived = [gathered[index] for index in range(chips)]
    packed = call(
        functools.partial(pack_pair_kernel, chips, direct),
        packs,
        (*weights, *packed),
        8 * MIB,
        10_000_000,
        5_000_000,
        after=(arrived[-1],),
        aliases={3: 0, 4: 1, 5: 2},
    )
    results = call(
        functools.partial(expert_kernel, chips),
        (shape((PAIR, width), bf16),) * chips,
        (*arrived, *packed),
        16 * MIB,
        800_000_000,
        5_000_000,
    )
    if direct:
        returned = [results[0]] + [
            across_owners(results[flip], CORES * flip) for flip in range(1, chips)
        ]
    else:
        gathered = lax.all_to_all(
            jnp.stack(results), "expert", 0, 0, axis_index_groups=same_core, tiled=True
        )
        returned = [gathered[index] for index in range(chips)]
    return call(
        functools.partial(finish_kernel, groups, chips),
        (block, block),
        (layer_input, upstream, place_x, place_u, sum_scale, *returned),
        16 * MIB,
        10_000_000,
        1_000_000,
    )


def solution(mesh):
    rows = P("segment", "expert", None)
    blocks = P("segment", "expert", None, None)
    return jax.shard_map(
        shards,
        mesh=mesh,
        in_specs=(rows,) * 6 + (blocks,) * 3,
        out_specs=(rows, rows),
        check_vma=False,
    )
```

time: 39.5 us -> 34.6 us (0.88)
  waiting for transfers between devices: 14.8 us -> 8.1 us
  local copies, waits for them, and re-layouts: 6.36 us -> 0.01 us
  Pallas kernels: 4.62 us -> 9.52 us
  starting transfers between devices: 12.7 us -> 16.1 us
    unnamed x10 -> x2, local copies, waits for them, and re-layouts: 6.36 us -> 0.01 us
    ppermute x2 -> x4, waiting for transfers between devices: 7.3 us -> 1.62 us  [along_sections(): return lax.ppermute(value, 'segment', pairs)]
    pallas_call x4 -> x7, Pallas kernels: 4.62 us -> 9.52 us  [call(): pl.pallas_call(body, out_shape=outs, in_specs=[anywhere] * waits + [dista...]
    ppermute x2 -> x4, starting transfers between devices: 5.03 us -> 8.5 us  [along_sections(): return lax.ppermute(value, 'segment', pairs)]
    ppermute x9, waiting for transfers between devices: 7.47 us -> 6.48 us  [across_owners(): lax.ppermute(value, 'expert', [(source, source ^ flip) for source in rang...]
  transfers between devices with their start and end apart: 11 -> 13, of which waited for: 8 -> 6; matrix products, arithmetic and copies ran while one was open for 8% -> 0% of each run, Pallas kernels for 2% -> 24%
where the time goes in v2:
time: 34.6 us; the launch traced here: 34.4 us
  starting transfers between devices  16.1 us (47%)
  Pallas kernels  9.52 us (28%)
  waiting for transfers between devices  8.1 us (23%)
  between operations  0.71 us (2%)
    pallas_call x7, Pallas kernels, call(): pl.pallas_call(body, out_shape=outs, in_specs=[anywhere] * waits + [dista...  9.52 us
    ppermute x4, starting transfers between devices, along_sections(): return lax.ppermute(value, 'segment', pairs)  8.5 us
    ppermute x9, starting transfers between devices, across_owners(): lax.ppermute(value, 'expert', [(source, source ^ flip) for source in rang...  7.55 us
    ppermute x9, waiting for transfers between devices, across_owners(): lax.ppermute(value, 'expert', [(source, source ^ flip) for source in rang...  6.48 us
    ppermute x4, waiting for transfers between devices, along_sections(): return lax.ppermute(value, 'segment', pairs)  1.62 us
  transfers between devices with their start and end apart: 13, of which 6 were waited for; matrix products, arithmetic and copies ran while one was open for 0% of the time, Pallas kernels for 24%

profile of v2, /device:TPU:0, one launch (start us, length us, event | category | flops | bytes accessed | tf_op | source)
XLA Modules:
  0.0 34.4 jit_solution(9079017755188598234)
XLA Ops:
  0.6 3.1 %collective-permute-start.1 = (s32[1,8,64]{2,1,0:T(8,128)}, s32[1,8,64]{2,1,0:T(8,128)S(1)}, u32[]{:S(2)}, u32[]{:S(2)}) collective-permute-start(s32[1,8,64]{2,1,0:T(8,128)} %bitcast.12), channel_id=1, source_target_pairs={{0,8},{8,16},{16,24},{24,0},{1,9},{9,17},{17,25},{25,1},{2,10},{10... | collective-permute-start | bytes 6152 | tf_op jit(solution)/shard_map/ppermute | solution.py:21
  3.7 1.6 %collective-permute-start = (bf16[1,64,2048]{2,1,0:T(8,128)(2,1)}, bf16[1,64,2048]{2,1,0:T(8,128)(2,1)S(1)}, u32[]{:S(2)}, u32[]{:S(2)}) collective-permute-start(bf16[1,64,2048]{2,1,0:T(8,128)(2,1)} %param.9), channel_id=1, source_target_pairs={{0,8},{8,16},{16,24},{24,0},{1,9},{9,17},{17,25},{25,1},{2,10},{10... | collective-permute-start | bytes 786440 | tf_op jit(solution)/shard_map/ppermute | solution.py:21
  5.3 0.0 collective-permute-start.3
  5.3 0.5 %collective-permute-start.2 = (bf16[1,1,2048,384]{3,2,1,0:T(8,128)(2,1)}, bf16[1,1,2048,384]{3,2,1,0:T(8,128)(2,1)S(1)}, u32[]{:S(2)}, u32[]{:S(2)}) collective-permute-start(bf16[1,1,2048,384]{3,2,1,0:T(8,128)(2,1)} %refs_1_.1), channel_id=1, source_target_pairs={{0,1},{1,0},{2,3},{3,2},{4,5},{5,4},{6,7},{7,6},{8,9},{9,8},{10,11... | collective-permute-start | bytes 4718600 | tf_op jit(solution)/shard_map/ppermute | solution.py:26
  5.8 1.1 %shard_map.104 = (bf16[1,64,2048]{2,1,0:T(8,128)(2,1)S(1)}, bf16[16,64]{1,0:T(8,128)(2,1)S(1)}, bf16[64,48]{1,0:T(8,128)(2,1)S(1)}, bf16[64,48]{1,0:T(8,128)(2,1...) custom-call(s32[1,8,64]{2,1,0:T(8,128)} %bitcast.9, f32[1,8,64]{2,1,0:T(8,128)} %bitcast.10, s32[1,8,64]{2,1,0:T(8,128)} %bitcast.13, ...), custom_call_target="tpu_custom_call" | custom-call | flops 10000000 | bytes 1000000 | tf_op jit(solution)/shard_map/pallas_call | solution.py:38
  6.9 0.7 %collective-permute-done.1.refs_0_ = s32[1,8,64]{2,1,0:T(8,128)S(1)} collective-permute-done((s32[1,8,64]{2,1,0:T(8,128)}, s32[1,8,64]{2,1,0:T(8,128)S(1)}, u32[]{:S(2)}, u32[]{:S(2)}) %collective-permute-start.1) | collective-permute-done | bytes 2080 | tf_op jit(solution)/shard_map/ppermute | solution.py:21
  7.5 0.0 copy-start
  7.5 0.3 shard_map.105.refs_0_
  7.8 2.1 %collective-permute-start.5 = (bf16[8,2048]{1,0:T(8,128)(2,1)S(1)}, bf16[8,2048]{1,0:T(8,128)(2,1)S(1)}, u32[]{:S(2)}, u32[]{:S(2)}) collective-permute-start(bf16[8,2048]{1,0:T(8,128)(2,1)S(1)} %shard_map.105.refs_0_), channel_id=1, source_target_pairs={{0,24},{8,0},{16,8},{24,16},{1,25},{9,1},{17,9},{25,17},{2,26},{10... | collective-permute-start | bytes 98312 | tf_op jit(solution)/shard_map/ppermute | solution.py:21
  9.9 0.0 copy-done
  9.9 0.0 collective-permute-start.4
  9.9 3.3 %shard_map.106 = (bf16[2048,1152]{1,0:T(8,128)(2,1)S(1)}, bf16[1152,2048]{1,0:T(8,128)(2,1)S(1)}, f32[64,768]{1,0:T(8,128)S(1)}) custom-call(bf16[8,2048]{1,0:T(8,128)(2,1)S(1)} %shard_map.105.refs_0_, bf16[1,1,2048,384]{3,2,1,0:T(8,128)(2,1)} %refs_1_.1, bf16[1,1,192,2048]{3,2,1,0:T(8,128)(2,1)} %refs_2_.1, bf16[1,1,40,384]{3,2,1,0:T(8,128)(2,1)} %refs_3_.1), custom_call_target="tpu_custom_call" | custom-call | flops 10000000 | bytes 5000000 | tf_op jit(solution)/shard_map/pallas_call | solution.py:38
  13.2 0.0 collective-permute-done.4.refs_5_.refs_3_
  13.2 1.0 %collective-permute-done.5.refs_8_ = bf16[8,2048]{1,0:T(8,128)(2,1)S(1)} collective-permute-done((bf16[8,2048]{1,0:T(8,128)(2,1)S(1)}, bf16[8,2048]{1,0:T(8,128)(2,1)S(1)}, u32[]{:S(2)}, u32[]{:S(2)}) %collective-permute-start.5) | collective-permute-done | bytes 32800 | tf_op jit(solution)/shard_map/ppermute | solution.py:21
  14.2 0.0 collective-permute-done.refs_6_.refs_0_
  14.2 0.0 collective-permute-done.3.refs_4_.refs_2_
  14.2 0.0 collective-permute-done.2.refs_3_.refs_1_
  14.2 0.2 shard_map.107
  14.4 1.7 %collective-permute-start.6 = (bf16[1,64,2048]{2,1,0:T(8,128)(2,1)S(1)}, bf16[1,64,2048]{2,1,0:T(8,128)(2,1)S(1)}, u32[]{:S(2)}, u32[]{:S(2)}) collective-permute-start(bf16[1,64,2048]{2,1,0:T(8,128)(2,1)S(1)} %get-tuple-element.26), channel_id=1, source_target_pairs={{0,24},{8,0},{16,8},{24,16},{1,25},{9,1},{17,9},{25,17},{2,26},{10... | collective-permute-start | bytes 786440 | tf_op jit(solution)/shard_map/ppermute | solution.py:21
  16.1 2.4 %collective-permute-start.9 = (bf16[16,2048]{1,0:T(8,128)(2,1)S(1)}, bf16[16,2048]{1,0:T(8,128)(2,1)S(1)}, u32[]{:S(2)}, u32[]{:S(2)}) collective-permute-start(bf16[16,2048]{1,0:T(8,128)(2,1)S(1)} %bitcast.5), channel_id=1, source_target_pairs={{0,6},{1,7},{2,4},{3,5},{4,2},{5,3},{6,0},{7,1},{8,14},{9,15},{10,... | collective-permute-start | bytes 196616 | tf_op jit(solution)/shard_map/ppermute | solution.py:26
  18.5 0.5 %collective-permute-start.8 = (bf16[16,2048]{1,0:T(8,128)(2,1)S(1)}, bf16[16,2048]{1,0:T(8,128)(2,1)S(1)}, u32[]{:S(2)}, u32[]{:S(2)}) collective-permute-start(bf16[16,2048]{1,0:T(8,128)(2,1)S(1)} %bitcast.6), channel_id=1, source_target_pairs={{0,4},{1,5},{2,6},{3,7},{4,0},{5,1},{6,2},{7,3},{8,12},{9,13},{10,... | collective-permute-start | bytes 196616 | tf_op jit(solution)/shard_map/ppermute | solution.py:26
  19.0 0.5 %collective-permute-start.7 = (bf16[16,2048]{1,0:T(8,128)(2,1)S(1)}, bf16[16,2048]{1,0:T(8,128)(2,1)S(1)}, u32[]{:S(2)}, u32[]{:S(2)}) collective-permute-start(bf16[16,2048]{1,0:T(8,128)(2,1)S(1)} %bitcast.7), channel_id=1, source_target_pairs={{0,2},{1,3},{2,0},{3,1},{4,6},{5,7},{6,4},{7,5},{8,10},{9,11},{10,... | collective-permute-start | bytes 196616 | tf_op jit(solution)/shard_map/ppermute | solution.py:26
  19.6 2.2 %collective-permute-done.9.refs_0_.refs_3_ = bf16[16,2048]{1,0:T(8,128)(2,1)S(1)} collective-permute-done((bf16[16,2048]{1,0:T(8,128)(2,1)S(1)}, bf16[16,2048]{1,0:T(8,128)(2,1)S(1)}, u32[]{:S(2)}, u32[]{:S(2)}) %collective-permute-start.9) | collective-permute-done | bytes 65568 | tf_op jit(solution)/shard_map/ppermute | solution.py:26
  21.8 1.9 %shard_map.108 = (bf16[2048,1152]{1,0:T(8,128)(2,1)S(1)}, bf16[1152,2048]{1,0:T(8,128)(2,1)S(1)}, f32[64,768]{1,0:T(8,128)S(1)}) custom-call(bf16[16,2048]{1,0:T(8,128)(2,1)S(1)} %collective-permute-done.9.refs_0_.refs_3_, ...), custom_call_target="tpu_custom_call", output_to_operand_aliasing={{0}: (4, {}), {1}: (5, {}), {2}: (6, {})} | custom-call | flops 10000000 | bytes 5000000 | tf_op jit(solution)/shard_map/pallas_call | solution.py:38
  23.7 0.0 collective-permute-done.8.refs_2_
  23.7 0.0 collective-permute-done.7.refs_1_
  23.7 1.8 %shard_map.109 = (bf16[16,2048]{1,0:T(8,128)(2,1)S(1)}, bf16[16,2048]{1,0:T(8,128)(2,1)S(1)}, bf16[16,2048]{1,0:T(8,128)(2,1)S(1)}, bf16[16,2048]{1,0:T(8,128)(2,1)S(1)}) custom-call(bf16[16,2048]{1,0:T(8,128)(2,1)S(1)} %bitcast.8, bf16[16,2048]{1,0:T(8,128)(2,1)S(1)} %collective-permute-done.7.refs_1_, bf16[16,2048]{1,0:T(8,128)(2,1)S(1)} %collective-permute-done.8.refs_2_, ...), custom_call_target="tpu_custom_call" | custom-call | flops 800000000 | bytes 5000000 | tf_op jit(solution)/shard_map/pallas_call | solution.py:38
  25.5 1.0 %collective-permute-start.10 = (bf16[16,2048]{1,0:T(8,128)(2,1)S(1)}, bf16[16,2048]{1,0:T(8,128)(2,1)S(1)}, u32[]{:S(2)}, u32[]{:S(2)}) collective-permute-start(bf16[16,2048]{1,0:T(8,128)(2,1)S(1)} %get-tuple-element.35), channel_id=1, source_target_pairs={{0,2},{1,3},{2,0},{3,1},{4,6},{5,7},{6,4},{7,5},{8,10},{9,11},{10,... | collective-permute-start | bytes 196616 | tf_op jit(solution)/shard_map/ppermute | solution.py:26
  26.5 1.6 %collective-permute-start.11 = (bf16[16,2048]{1,0:T(8,128)(2,1)S(1)}, bf16[16,2048]{1,0:T(8,128)(2,1)S(1)}, u32[]{:S(2)}, u32[]{:S(2)}) collective-permute-start(bf16[16,2048]{1,0:T(8,128)(2,1)S(1)} %get-tuple-element.36), channel_id=1, source_target_pairs={{0,4},{1,5},{2,6},{3,7},{4,0},{5,1},{6,2},{7,3},{8,12},{9,13},{10,... | collective-permute-start | bytes 196616 | tf_op jit(solution)/shard_map/ppermute | solution.py:26
  28.1 0.9 %collective-permute-start.12 = (bf16[16,2048]{1,0:T(8,128)(2,1)S(1)}, bf16[16,2048]{1,0:T(8,128)(2,1)S(1)}, u32[]{:S(2)}, u32[]{:S(2)}) collective-permute-start(bf16[16,2048]{1,0:T(8,128)(2,1)S(1)} %get-tuple-element.37), channel_id=1, source_target_pairs={{0,6},{1,7},{2,4},{3,5},{4,2},{5,3},{6,0},{7,1},{8,14},{9,15},{10,... | collective-permute-start | bytes 196616 | tf_op jit(solution)/shard_map/ppermute | solution.py:26
  29.1 0.8 %collective-permute-done.10.refs_6_ = bf16[16,2048]{1,0:T(8,128)(2,1)S(1)} collective-permute-done((bf16[16,2048]{1,0:T(8,128)(2,1)S(1)}, bf16[16,2048]{1,0:T(8,128)(2,1)S(1)}, u32[]{:S(2)}, u32[]{:S(2)}) %collective-permute-start.10) | collective-permute-done | bytes 65568 | tf_op jit(solution)/shard_map/ppermute | solution.py:26
  29.9 0.9 %collective-permute-done.11.refs_7_ = bf16[16,2048]{1,0:T(8,128)(2,1)S(1)} collective-permute-done((bf16[16,2048]{1,0:T(8,128)(2,1)S(1)}, bf16[16,2048]{1,0:T(8,128)(2,1)S(1)}, u32[]{:S(2)}, u32[]{:S(2)}) %collective-permute-start.11) | collective-permute-done | bytes 65568 | tf_op jit(solution)/shard_map/ppermute | solution.py:26
  30.8 2.5 %collective-permute-done.12.refs_8_ = bf16[16,2048]{1,0:T(8,128)(2,1)S(1)} collective-permute-done((bf16[16,2048]{1,0:T(8,128)(2,1)S(1)}, bf16[16,2048]{1,0:T(8,128)(2,1)S(1)}, u32[]{:S(2)}, u32[]{:S(2)}) %collective-permute-start.12) | collective-permute-done | bytes 65568 | tf_op jit(solution)/shard_map/ppermute | solution.py:26
  33.3 0.0 collective-permute-done.6.refs_1_
  33.3 1.1 %shard_map.110 = (bf16[1,64,2048]{2,1,0:T(8,128)(2,1)}, bf16[1,64,2048]{2,1,0:T(8,128)(2,1)}) custom-call(bf16[1,64,2048]{2,1,0:T(8,128)(2,1)S(1)} %collective-permute-done.refs_6_.refs_0_, bf16[1,64,2048]{2,1,0:T(8,128)(2,1)S(1)} %collective-permute-done.6.refs_1_, bf16[64,48]{1,0:T(8,128)(2,1)S(1)} %get-tuple-element.27.refs_2_, ...), custom_call_target="tpu_custom_call" | custom-call | flops 10000000 | bytes 1000000 | tf_op jit(solution)/shard_map/pallas_call | solution.py:38
Async XLA Ops:
  0.6 6.9 %collective-permute-start.1 = (s32[1,8,64]{2,1,0:T(8,128)}, s32[1,8,64]{2,1,0:T(8,128)S(1)}, u32[]{:S(2)}, u32[]{:S(2)}) collective-permute-start(s32[1,8,64]{2,1,0:T(8,128)} %bitcast.12), channel_id=1, source_target_pairs={{0,8},{8,16},{16,24},{24,0},{1,9},{9,17},{17,25},{25,1},{2,10},{10... | collective-permute-start | bytes 6152 | tf_op jit(solution)/shard_map/ppermute | solution.py:21
  3.7 10.5 %collective-permute-start = (bf16[1,64,2048]{2,1,0:T(8,128)(2,1)}, bf16[1,64,2048]{2,1,0:T(8,128)(2,1)S(1)}, u32[]{:S(2)}, u32[]{:S(2)}) collective-permute-start(bf16[1,64,2048]{2,1,0:T(8,128)(2,1)} %param.9), channel_id=1, source_target_pairs={{0,8},{8,16},{16,24},{24,0},{1,9},{9,17},{17,25},{25,1},{2,10},{10... | collective-permute-start | bytes 786440 | tf_op jit(solution)/shard_map/ppermute | solution.py:21
  5.3 8.9 %collective-permute-start.3 = (bf16[1,1,192,2048]{3,2,1,0:T(8,128)(2,1)}, bf16[1,1,192,2048]{3,2,1,0:T(8,128)(2,1)S(1)}, u32[]{:S(2)}, u32[]{:S(2)}) collective-permute-start(bf16[1,1,192,2048]{3,2,1,0:T(8,128)(2,1)} %refs_2_.1), channel_id=1, source_target_pairs={{0,1},{1,0},{2,3},{3,2},{4,5},{5,4},{6,7},{7,6},{8,9},{9,8},{10,11... | collective-permute-start | bytes 2359304 | tf_op jit(solution)/shard_map/ppermute | solution.py:26
  5.3 8.9 %collective-permute-start.2 = (bf16[1,1,2048,384]{3,2,1,0:T(8,128)(2,1)}, bf16[1,1,2048,384]{3,2,1,0:T(8,128)(2,1)S(1)}, u32[]{:S(2)}, u32[]{:S(2)}) collective-permute-start(bf16[1,1,2048,384]{3,2,1,0:T(8,128)(2,1)} %refs_1_.1), channel_id=1, source_target_pairs={{0,1},{1,0},{2,3},{3,2},{4,5},{5,4},{6,7},{7,6},{8,9},{9,8},{10,11... | collective-permute-start | bytes 4718600 | tf_op jit(solution)/shard_map/ppermute | solution.py:26
  7.5 2.4 %copy-start = (bf16[1,1,40,384]{3,2,1,0:T(8,128)(2,1)S(1)}, bf16[1,1,40,384]{3,2,1,0:T(8,128)(2,1)}, u32[]{:S(2)}) copy-start(bf16[1,1,40,384]{3,2,1,0:T(8,128)(2,1)} %refs_3_.1) | copy-start | bytes 92164
  7.8 6.4 %collective-permute-start.5 = (bf16[8,2048]{1,0:T(8,128)(2,1)S(1)}, bf16[8,2048]{1,0:T(8,128)(2,1)S(1)}, u32[]{:S(2)}, u32[]{:S(2)}) collective-permute-start(bf16[8,2048]{1,0:T(8,128)(2,1)S(1)} %shard_map.105.refs_0_), channel_id=1, source_target_pairs={{0,24},{8,0},{16,8},{24,16},{1,25},{9,1},{17,9},{25,17},{2,26},{10... | collective-permute-start | bytes 98312 | tf_op jit(solution)/shard_map/ppermute | solution.py:21
  9.9 3.3 %collective-permute-start.4 = (bf16[1,1,40,384]{3,2,1,0:T(8,128)(2,1)S(1)}, bf16[1,1,40,384]{3,2,1,0:T(8,128)(2,1)S(1)}, u32[]{:S(2)}, u32[]{:S(2)}) collective-permute-start(bf16[1,1,40,384]{3,2,1,0:T(8,128)(2,1)S(1)} %copy-done), channel_id=1, source_target_pairs={{0,1},{1,0},{2,3},{3,2},{4,5},{5,4},{6,7},{7,6},{8,9},{9,8},{10,11... | collective-permute-start | bytes 92168 | tf_op jit(solution)/shard_map/ppermute | solution.py:26
  14.4 19.0 %collective-permute-start.6 = (bf16[1,64,2048]{2,1,0:T(8,128)(2,1)S(1)}, bf16[1,64,2048]{2,1,0:T(8,128)(2,1)S(1)}, u32[]{:S(2)}, u32[]{:S(2)}) collective-permute-start(bf16[1,64,2048]{2,1,0:T(8,128)(2,1)S(1)} %get-tuple-element.26), channel_id=1, source_target_pairs={{0,24},{8,0},{16,8},{24,16},{1,25},{9,1},{17,9},{25,17},{2,26},{10... | collective-permute-start | bytes 786440 | tf_op jit(solution)/shard_map/ppermute | solution.py:21
  16.1 5.7 %collective-permute-start.9 = (bf16[16,2048]{1,0:T(8,128)(2,1)S(1)}, bf16[16,2048]{1,0:T(8,128)(2,1)S(1)}, u32[]{:S(2)}, u32[]{:S(2)}) collective-permute-start(bf16[16,2048]{1,0:T(8,128)(2,1)S(1)} %bitcast.5), channel_id=1, source_target_pairs={{0,6},{1,7},{2,4},{3,5},{4,2},{5,3},{6,0},{7,1},{8,14},{9,15},{10,... | collective-permute-start | bytes 196616 | tf_op jit(solution)/shard_map/ppermute | solution.py:26
  18.5 5.2 %collective-permute-start.8 = (bf16[16,2048]{1,0:T(8,128)(2,1)S(1)}, bf16[16,2048]{1,0:T(8,128)(2,1)S(1)}, u32[]{:S(2)}, u32[]{:S(2)}) collective-permute-start(bf16[16,2048]{1,0:T(8,128)(2,1)S(1)} %bitcast.6), channel_id=1, source_target_pairs={{0,4},{1,5},{2,6},{3,7},{4,0},{5,1},{6,2},{7,3},{8,12},{9,13},{10,... | collective-permute-start | bytes 196616 | tf_op jit(solution)/shard_map/ppermute | solution.py:26
  19.0 4.7 %collective-permute-start.7 = (bf16[16,2048]{1,0:T(8,128)(2,1)S(1)}, bf16[16,2048]{1,0:T(8,128)(2,1)S(1)}, u32[]{:S(2)}, u32[]{:S(2)}) collective-permute-start(bf16[16,2048]{1,0:T(8,128)(2,1)S(1)} %bitcast.7), channel_id=1, source_target_pairs={{0,2},{1,3},{2,0},{3,1},{4,6},{5,7},{6,4},{7,5},{8,10},{9,11},{10,... | collective-permute-start | bytes 196616 | tf_op jit(solution)/shard_map/ppermute | solution.py:26
  25.5 4.3 %collective-permute-start.10 = (bf16[16,2048]{1,0:T(8,128)(2,1)S(1)}, bf16[16,2048]{1,0:T(8,128)(2,1)S(1)}, u32[]{:S(2)}, u32[]{:S(2)}) collective-permute-start(bf16[16,2048]{1,0:T(8,128)(2,1)S(1)} %get-tuple-element.35), channel_id=1, source_target_pairs={{0,2},{1,3},{2,0},{3,1},{4,6},{5,7},{6,4},{7,5},{8,10},{9,11},{10,... | collective-permute-start | bytes 196616 | tf_op jit(solution)/shard_map/ppermute | solution.py:26
  26.5 4.3 %collective-permute-start.11 = (bf16[16,2048]{1,0:T(8,128)(2,1)S(1)}, bf16[16,2048]{1,0:T(8,128)(2,1)S(1)}, u32[]{:S(2)}, u32[]{:S(2)}) collective-permute-start(bf16[16,2048]{1,0:T(8,128)(2,1)S(1)} %get-tuple-element.36), channel_id=1, source_target_pairs={{0,4},{1,5},{2,6},{3,7},{4,0},{5,1},{6,2},{7,3},{8,12},{9,13},{10,... | collective-permute-start | bytes 196616 | tf_op jit(solution)/shard_map/ppermute | solution.py:26
  28.1 5.2 %collective-permute-start.12 = (bf16[16,2048]{1,0:T(8,128)(2,1)S(1)}, bf16[16,2048]{1,0:T(8,128)(2,1)S(1)}, u32[]{:S(2)}, u32[]{:S(2)}) collective-permute-start(bf16[16,2048]{1,0:T(8,128)(2,1)S(1)} %get-tuple-element.37), channel_id=1, source_target_pairs={{0,6},{1,7},{2,4},{3,5},{4,2},{5,3},{6,0},{7,1},{8,14},{9,15},{10,... | collective-permute-start | bytes 196616 | tf_op jit(solution)/shard_map/ppermute | solution.py:26

commit v3 on v2

--- a/solution.py
+++ b/solution.py
@@ -86,8 +86,11 @@
     rows[...] = dot(picks.astype(jnp.bfloat16), staged[0]).astype(jnp.bfloat16)
 
 
-def merge_kernel(groups, x, pick_x, rows_b, send_scale, staged, message, whole):
+def release_kernel(staged, whole):
     whole[...] = staged[...]
+
+
+def merge_kernel(groups, x, pick_x, rows_b, send_scale, message):
     all_a = dot(pick_x[...], x[0])
     all_b = rows_b[...].astype(jnp.float32)
     for group in range(groups):
@@ -132,17 +135,14 @@
     stage.wait()
 
 
-def pack(index, chips, mixed, entry, down, saved, first, second, factors):
+def pack_half(index, chips, mixed, entry, down, saved, lower, second, factors):
     half = down.shape[2]
     gate = slice(index * half, (index + 1) * half)
     upper = slice((2 + index) * half, (3 + index) * half)
-    lower = slice((4 + index) * half, (5 + index) * half)
-    first[:, gate] = entry[0, 0, :, :half]
-    first[:, upper] = entry[0, 0, :, half:]
-    first[:, lower] = down[0, 0].T
-    second[gate, :] = entry[0, 0, :, :half].T
-    second[upper, :] = entry[0, 0, :, half:].T
-    second[lower, :] = down[0, 0]
+    lower[:, gate] = down[0, 0].T
+    turned = entry[0, 0].T
+    second[gate, :] = turned[:half]
+    second[upper, :] = turned[half:]
 
     me = lax.axis_index("expert")
     held = saved.shape[2]
@@ -164,28 +164,41 @@
 
 
 def pack_own_kernel(chips, mixed, *refs):
-    far, packs, near, semaphores = refs[:3], refs[3:6], refs[6:9], refs[9]
-    fetch(far, near, semaphores)
-    pack(0, chips, mixed, *near, *packs)
-
-
-def pack_pair_kernel(chips, mixed, *refs):
-    pack(1, chips, mixed, *refs[:3], *refs[6:])
+    entry_far, down_far, saved_far, entry, down, lower, second, factors, saved, semaphores = refs
+    half = down.shape[2]
+    rows = second.at[pl.ds(4 * half, half)]
+    fetch(
+        (entry_far, down_far, saved_far, down_far.at[0, 0]),
+        (entry, down, saved, rows),
+        semaphores,
+    )
+    pack_half(0, chips, mixed, entry, down, saved, lower, second, factors)
+
+
+def pack_pair_kernel(chips, mixed, entry, down, saved, *refs):
+    lower, second, factors = refs[3:]
+    half = down.shape[2]
+    second[5 * half :, :] = down[0, 0]
+    pack_half(1, chips, mixed, entry, down, saved, lower, second, factors)
 
 
 def expert_kernel(chips, *refs):
     arrived = refs[:chips]
-    first, second, factors = refs[chips : chips + 3]
-    results = refs[chips + 3 :]
+    entries = refs[chips : chips + 2]
+    lower, second, factors = refs[chips + 2 : chips + 5]
+    results = refs[chips + 5 :]
     rows = jnp.concatenate([ref[...] for ref in arrived], axis=0)
-    made = dot(rows, first[...])
-    both = made.shape[1] // 3
-    gate = made[:, :both]
-    upper = made[:, both : 2 * both]
-    back = made[:, 2 * both :]
-    line = lax.broadcasted_iota(jnp.int32, back.shape, 0) % PAIR
-    hidden = jnp.where(line < SLOTS, gate * jax.nn.sigmoid(gate) * upper, 0.0)
+    back = dot(rows, lower[...])
+    half = back.shape[1] // 2
     grads = jnp.concatenate([back, back], axis=1) * factors[...]
+    hidden = []
+    for entry in entries:
+        made = dot(rows, entry[0, 0])
+        gate = made[:, :half]
+        hidden.append(gate * jax.nn.sigmoid(gate) * made[:, half:])
+    hidden = jnp.concatenate(hidden, axis=1)
+    line = lax.broadcasted_iota(jnp.int32, hidden.shape, 0) % PAIR
+    hidden = jnp.where(line < SLOTS, hidden, 0.0)
     inner = jnp.concatenate([grads.astype(jnp.bfloat16), hidden.astype(jnp.bfloat16)], axis=1)
     total = dot(inner, second[...]).astype(jnp.bfloat16)
     for index, ref in enumerate(results):
@@ -194,7 +207,7 @@
 
 def finish_kernel(groups, chips, *refs):
     x, u, place_x, place_u, sum_scale = refs[:5]
-    returned = refs[5 : 5 + chips]
+    returned = refs[5 : 5 + chips][::-1]
     out_x, out_u = refs[5 + chips :]
     share = chips // groups
     sums = []
@@ -268,18 +281,18 @@
         shape((groups * SLOTS, width), bf16),
         (asked, staged),
         8 * MIB,
-        50_000_000_000,
+        10_000_000_000,
         1_000_000_000,
     )
     weights = (entry_weights, down_weights, saved_projections)
     packs = (
-        shape((width, 6 * half), bf16),
+        shape((width, 2 * half), bf16),
         shape((6 * half, width), bf16),
         shape((chips * PAIR, 4 * half), f32),
     )
-    packed = call(
+    entry_own, down_own, *packed = call(
         functools.partial(pack_own_kernel, chips, direct),
-        packs,
+        (shape(entry_weights.shape, bf16), shape(down_weights.shape, bf16), *packs),
         (),
         8 * MIB,
         10_000_000,
@@ -287,20 +300,29 @@
         after=(rows_b,),
         far=weights,
         scratch=[
-            *[pltpu.VMEM(value.shape, value.dtype) for value in weights],
-            pltpu.SemaphoreType.DMA((len(weights),)),
+            pltpu.VMEM(saved_projections.shape, bf16),
+            pltpu.SemaphoreType.DMA((len(weights) + 1,)),
         ],
     )
     rows_b = along_sections(rows_b, -1)
-    weights = [across_owners(value, 1) for value in weights]
-    message, whole = call(
+    weights = [across_owners(value, 1) for value in (entry_own, down_own, saved_projections)]
+    message = call(
         functools.partial(merge_kernel, groups),
-        (shape((groups, PAIR, width), bf16), block),
-        (layer_input, pick_x, rows_b, send_scale, staged),
-        8 * MIB,
+        shape((groups, PAIR, width), bf16),
+        (layer_input, pick_x, rows_b, send_scale),
+        8 * MIB,
+        50_000_000_000,
         100_000,
-        100_000,
-        after=(*packed, *weights),
+        after=(*packed, weights[2]),
+    )
+    whole = call(
+        release_kernel,
+        block,
+        (staged,),
+        8 * MIB,
+        1,
+        1,
+        after=(message, *weights[:2]),
     )
     upstream = along_sections(whole, -1)
     if direct:
@@ -317,7 +339,7 @@
         packs,
         (*weights, *packed),
         8 * MIB,
-        10_000_000,
+        10_000_000_000,
         5_000_000,
         after=(arrived[-1],),
         aliases={3: 0, 4: 1, 5: 2},
@@ -325,7 +347,7 @@
     results = call(
         functools.partial(expert_kernel, chips),
         (shape((PAIR, width), bf16),) * chips,
-        (*arrived, *packed),
+        (*arrived, entry_own, weights[0], *packed),
         16 * MIB,
         800_000_000,
         5_000_000,
@@ -342,7 +364,7 @@
     return call(
         functools.partial(finish_kernel, groups, chips),
         (block, block),
-        (layer_input, upstream, place_x, place_u, sum_scale, *returned),
+        (layer_input, upstream, place_x, place_u, sum_scale, *returned[::-1]),
         16 * MIB,
         10_000_000,
         1_000_000,

time: 34.6 us -> 32 us (0.925)
  waiting for transfers between devices: 8.1 us -> 6.16 us
  Pallas kernels: 9.52 us -> 8.7 us
    ppermute x9, waiting for transfers between devices: 6.48 us -> 4.59 us  [across_owners(): lax.ppermute(value, 'expert', [(source, source ^ flip) for source in rang...]
    pallas_call x7 -> x8, Pallas kernels: 9.52 us -> 8.7 us  [call(): pl.pallas_call(body, out_shape=outs, in_specs=[anywhere] * waits + [dista...]
  transfers between devices with their start and end apart: 13 -> 13, of which waited for: 6 -> 7; matrix products, arithmetic and copies ran while one was open for 0% -> 0% of each run, Pallas kernels for 24% -> 24%
where the time goes in v3:
time: 32 us; the launch traced here: 31.8 us
  starting transfers between devices  16.3 us (51%)
  Pallas kernels  8.7 us (27%)
  waiting for transfers between devices  6.16 us (19%)
  between operations  0.69 us (2%)
    pallas_call x8, Pallas kernels, call(): pl.pallas_call(body, out_shape=outs, in_specs=[anywhere] * waits + [dista...  8.7 us
    ppermute x4, starting transfers between devices, along_sections(): return lax.ppermute(value, 'segment', pairs)  8.51 us
    ppermute x9, starting transfers between devices, across_owners(): lax.ppermute(value, 'expert', [(source, source ^ flip) for source in rang...  7.76 us
    ppermute x9, waiting for transfers between devices, across_owners(): lax.ppermute(value, 'expert', [(source, source ^ flip) for source in rang...  4.59 us
    ppermute x4, waiting for transfers between devices, along_sections(): return lax.ppermute(value, 'segment', pairs)  1.57 us
  transfers between devices with their start and end apart: 13, of which 7 were waited for; matrix products, arithmetic and copies ran while one was open for 0% of the time, Pallas kernels for 24%

profile of v3, /device:TPU:0, one launch (start us, length us, event | category | flops | bytes accessed | tf_op | source)
XLA Modules:
  0.0 31.8 jit_solution(4728835527936590130)
XLA Ops:
  0.6 3.1 %collective-permute-start.1 = (s32[1,8,64]{2,1,0:T(8,128)}, s32[1,8,64]{2,1,0:T(8,128)S(1)}, u32[]{:S(2)}, u32[]{:S(2)}) collective-permute-start(s32[1,8,64]{2,1,0:T(8,128)} %bitcast.12), channel_id=1, source_target_pairs={{0,8},{8,16},{16,24},{24,0},{1,9},{9,17},{17,25},{25,1},{2,10},{10... | collective-permute-start | bytes 6152 | tf_op jit(solution)/shard_map/ppermute | solution.py:21
  3.7 1.6 %collective-permute-start = (bf16[1,64,2048]{2,1,0:T(8,128)(2,1)}, bf16[1,64,2048]{2,1,0:T(8,128)(2,1)S(1)}, u32[]{:S(2)}, u32[]{:S(2)}) collective-permute-start(bf16[1,64,2048]{2,1,0:T(8,128)(2,1)} %param.9), channel_id=1, source_target_pairs={{0,8},{8,16},{16,24},{24,0},{1,9},{9,17},{17,25},{25,1},{2,10},{10... | collective-permute-start | bytes 786440 | tf_op jit(solution)/shard_map/ppermute | solution.py:21
  5.3 1.1 %shard_map.104 = (bf16[1,64,2048]{2,1,0:T(8,128)(2,1)S(1)}, bf16[16,64]{1,0:T(8,128)(2,1)S(1)}, bf16[64,48]{1,0:T(8,128)(2,1)S(1)}, bf16[64,48]{1,0:T(8,128)(2,1...) custom-call(s32[1,8,64]{2,1,0:T(8,128)} %bitcast.9, f32[1,8,64]{2,1,0:T(8,128)} %bitcast.10, s32[1,8,64]{2,1,0:T(8,128)} %bitcast.13, ...), custom_call_target="tpu_custom_call" | custom-call | flops 10000000 | bytes 1000000 | tf_op jit(solution)/shard_map/pallas_call | solution.py:38
  6.4 1.2 %collective-permute-done.1.refs_0_ = s32[1,8,64]{2,1,0:T(8,128)S(1)} collective-permute-done((s32[1,8,64]{2,1,0:T(8,128)}, s32[1,8,64]{2,1,0:T(8,128)S(1)}, u32[]{:S(2)}, u32[]{:S(2)}) %collective-permute-start.1) | collective-permute-done | bytes 2080 | tf_op jit(solution)/shard_map/ppermute | solution.py:21
  7.5 0.0 copy-start
  7.5 0.3 shard_map.105.refs_0_
  7.8 2.1 %collective-permute-start.3 = (bf16[8,2048]{1,0:T(8,128)(2,1)S(1)}, bf16[8,2048]{1,0:T(8,128)(2,1)S(1)}, u32[]{:S(2)}, u32[]{:S(2)}) collective-permute-start(bf16[8,2048]{1,0:T(8,128)(2,1)S(1)} %shard_map.105.refs_0_), channel_id=1, source_target_pairs={{0,24},{8,0},{16,8},{24,16},{1,25},{9,1},{17,9},{25,17},{2,26},{10... | collective-permute-start | bytes 98312 | tf_op jit(solution)/shard_map/ppermute | solution.py:21
  9.9 0.0 copy-done
  9.9 0.0 collective-permute-start.2
  9.9 3.2 %shard_map.106 = (bf16[1,1,2048,384]{3,2,1,0:T(8,128)(2,1)S(1)}, bf16[1,1,192,2048]{3,2,1,0:T(8,128)(2,1)S(1)}, bf16[2048,384]{1,0:T(8,128)(2,1)S(1)}, bf16[1152,2048]{1,0:T(8,128)(2,1)S(1)}, f32[64,768]{1,0:T(8,128)S(1)}) custom-call(bf16[8,2048]{1,0:T(8,128)(2,1)S(1)} %shard_map.105.refs_0_, bf16[1,1,2048,384]{3,2,1,0:T(8,128)(2,1)} %refs_1_.1, ...), custom_call_target="tpu_custom_call" | custom-call | flops 10000000 | bytes 5000000 | tf_op jit(solution)/shard_map/pallas_call | solution.py:38
  13.1 0.6 %collective-permute-start.4 = (bf16[1,1,2048,384]{3,2,1,0:T(8,128)(2,1)S(1)}, bf16[1,1,2048,384]{3,2,1,0:T(8,128)(2,1)S(1)}, u32[]{:S(2)}, u32[]{:S(2)}) collective-permute-start(bf16[1,1,2048,384]{3,2,1,0:T(8,128)(2,1)S(1)} %get-tuple-element.26.refs_4_), channel_id=1, source_target_pairs={{0,1},{1,0},{2,3},{3,2},{4,5},{5,4},{6,7},{7,6},{8,9},{9,8},{10,11... | collective-permute-start | bytes 4718600 | tf_op jit(solution)/shard_map/ppermute | solution.py:26
  13.7 0.1 collective-permute-start.5
  13.8 0.0 collective-permute-done.2.refs_3_
  13.8 0.4 %collective-permute-done.3.refs_6_ = bf16[8,2048]{1,0:T(8,128)(2,1)S(1)} collective-permute-done((bf16[8,2048]{1,0:T(8,128)(2,1)S(1)}, bf16[8,2048]{1,0:T(8,128)(2,1)S(1)}, u32[]{:S(2)}, u32[]{:S(2)}) %collective-permute-start.3) | collective-permute-done | bytes 32800 | tf_op jit(solution)/shard_map/ppermute | solution.py:21
  14.2 0.0 collective-permute-done.refs_4_.refs_0_
  14.2 0.1 shard_map.107.refs_0_
  14.3 2.5 %collective-permute-start.9 = (bf16[16,2048]{1,0:T(8,128)(2,1)S(1)}, bf16[16,2048]{1,0:T(8,128)(2,1)S(1)}, u32[]{:S(2)}, u32[]{:S(2)}) collective-permute-start(bf16[16,2048]{1,0:T(8,128)(2,1)S(1)} %bitcast.5), channel_id=1, source_target_pairs={{0,6},{1,7},{2,4},{3,5},{4,2},{5,3},{6,0},{7,1},{8,14},{9,15},{10,... | collective-permute-start | bytes 196616 | tf_op jit(solution)/shard_map/ppermute | solution.py:26
  16.8 0.5 %collective-permute-start.7 = (bf16[16,2048]{1,0:T(8,128)(2,1)S(1)}, bf16[16,2048]{1,0:T(8,128)(2,1)S(1)}, u32[]{:S(2)}, u32[]{:S(2)}) collective-permute-start(bf16[16,2048]{1,0:T(8,128)(2,1)S(1)} %bitcast.6), channel_id=1, source_target_pairs={{0,2},{1,3},{2,0},{3,1},{4,6},{5,7},{6,4},{7,5},{8,10},{9,11},{10,... | collective-permute-start | bytes 196616 | tf_op jit(solution)/shard_map/ppermute | solution.py:26
  17.4 0.5 %collective-permute-start.8 = (bf16[16,2048]{1,0:T(8,128)(2,1)S(1)}, bf16[16,2048]{1,0:T(8,128)(2,1)S(1)}, u32[]{:S(2)}, u32[]{:S(2)}) collective-permute-start(bf16[16,2048]{1,0:T(8,128)(2,1)S(1)} %bitcast.7), channel_id=1, source_target_pairs={{0,4},{1,5},{2,6},{3,7},{4,0},{5,1},{6,2},{7,3},{8,12},{9,13},{10,... | collective-permute-start | bytes 196616 | tf_op jit(solution)/shard_map/ppermute | solution.py:26
  17.9 0.0 collective-permute-done.5.refs_2_
  17.9 0.0 collective-permute-done.4.refs_1_.refs_5_
  17.9 1.7 %collective-permute-start.6 = (bf16[1,64,2048]{2,1,0:T(8,128)(2,1)S(1)}, bf16[1,64,2048]{2,1,0:T(8,128)(2,1)S(1)}, u32[]{:S(2)}, u32[]{:S(2)}) collective-permute-start(bf16[1,64,2048]{2,1,0:T(8,128)(2,1)S(1)} %shard_map.108), channel_id=1, source_target_pairs={{0,24},{8,0},{16,8},{24,16},{1,25},{9,1},{17,9},{25,17},{2,26},{10... | collective-permute-start | bytes 786440 | tf_op jit(solution)/shard_map/ppermute | solution.py:21
  19.6 0.3 %collective-permute-done.9.refs_0_.refs_3_ = bf16[16,2048]{1,0:T(8,128)(2,1)S(1)} collective-permute-done((bf16[16,2048]{1,0:T(8,128)(2,1)S(1)}, bf16[16,2048]{1,0:T(8,128)(2,1)S(1)}, u32[]{:S(2)}, u32[]{:S(2)}) %collective-permute-start.9) | collective-permute-done | bytes 65568 | tf_op jit(solution)/shard_map/ppermute | solution.py:26
  20.0 1.1 %shard_map.109 = (bf16[2048,384]{1,0:T(8,128)(2,1)S(1)}, bf16[1152,2048]{1,0:T(8,128)(2,1)S(1)}, f32[64,768]{1,0:T(8,128)S(1)}) custom-call(bf16[16,2048]{1,0:T(8,128)(2,1)S(1)} %collective-permute-done.9.refs_0_.refs_3_, ...), custom_call_target="tpu_custom_call", output_to_operand_aliasing={{0}: (4, {}), {1}: (5, {}), {2}: (6, {})} | custom-call | flops 10000000000 | bytes 5000000 | tf_op jit(solution)/shard_map/pallas_call | solution.py:38
  21.1 0.0 collective-permute-done.7.refs_1_
  21.1 0.5 %collective-permute-done.8.refs_2_ = bf16[16,2048]{1,0:T(8,128)(2,1)S(1)} collective-permute-done((bf16[16,2048]{1,0:T(8,128)(2,1)S(1)}, bf16[16,2048]{1,0:T(8,128)(2,1)S(1)}, u32[]{:S(2)}, u32[]{:S(2)}) %collective-permute-start.8) | collective-permute-done | bytes 65568 | tf_op jit(solution)/shard_map/ppermute | solution.py:26
  21.6 1.8 %shard_map.110 = (bf16[16,2048]{1,0:T(8,128)(2,1)S(1)}, bf16[16,2048]{1,0:T(8,128)(2,1)S(1)}, bf16[16,2048]{1,0:T(8,128)(2,1)S(1)}, bf16[16,2048]{1,0:T(8,128)(2,1)S(1)}) custom-call(bf16[16,2048]{1,0:T(8,128)(2,1)S(1)} %bitcast.8, bf16[16,2048]{1,0:T(8,128)(2,1)S(1)} %collective-permute-done.7.refs_1_, bf16[16,2048]{1,0:T(8,128)(2,1)S(1)} %collective-permute-done.8.refs_2_, ...), custom_call_target="tpu_custom_call" | custom-call | flops 800000000 | bytes 5000000 | tf_op jit(solution)/shard_map/pallas_call | solution.py:38
  23.5 2.0 %collective-permute-start.10 = (bf16[16,2048]{1,0:T(8,128)(2,1)S(1)}, bf16[16,2048]{1,0:T(8,128)(2,1)S(1)}, u32[]{:S(2)}, u32[]{:S(2)}) collective-permute-start(bf16[16,2048]{1,0:T(8,128)(2,1)S(1)} %get-tuple-element.34), channel_id=1, source_target_pairs={{0,6},{1,7},{2,4},{3,5},{4,2},{5,3},{6,0},{7,1},{8,14},{9,15},{10,... | collective-permute-start | bytes 196616 | tf_op jit(solution)/shard_map/ppermute | solution.py:26
  25.5 1.0 %collective-permute-start.11 = (bf16[16,2048]{1,0:T(8,128)(2,1)S(1)}, bf16[16,2048]{1,0:T(8,128)(2,1)S(1)}, u32[]{:S(2)}, u32[]{:S(2)}) collective-permute-start(bf16[16,2048]{1,0:T(8,128)(2,1)S(1)} %get-tuple-element.35), channel_id=1, source_target_pairs={{0,4},{1,5},{2,6},{3,7},{4,0},{5,1},{6,2},{7,3},{8,12},{9,13},{10,... | collective-permute-start | bytes 196616 | tf_op jit(solution)/shard_map/ppermute | solution.py:26
  26.5 0.5 %collective-permute-start.12 = (bf16[16,2048]{1,0:T(8,128)(2,1)S(1)}, bf16[16,2048]{1,0:T(8,128)(2,1)S(1)}, u32[]{:S(2)}, u32[]{:S(2)}) collective-permute-start(bf16[16,2048]{1,0:T(8,128)(2,1)S(1)} %get-tuple-element.36), channel_id=1, source_target_pairs={{0,2},{1,3},{2,0},{3,1},{4,6},{5,7},{6,4},{7,5},{8,10},{9,11},{10,... | collective-permute-start | bytes 196616 | tf_op jit(solution)/shard_map/ppermute | solution.py:26
  27.0 2.1 %collective-permute-done.10.refs_5_ = bf16[16,2048]{1,0:T(8,128)(2,1)S(1)} collective-permute-done((bf16[16,2048]{1,0:T(8,128)(2,1)S(1)}, bf16[16,2048]{1,0:T(8,128)(2,1)S(1)}, u32[]{:S(2)}, u32[]{:S(2)}) %collective-permute-start.10) | collective-permute-done | bytes 65568 | tf_op jit(solution)/shard_map/ppermute | solution.py:26
  29.2 0.7 %collective-permute-done.11.refs_6_ = bf16[16,2048]{1,0:T(8,128)(2,1)S(1)} collective-permute-done((bf16[16,2048]{1,0:T(8,128)(2,1)S(1)}, bf16[16,2048]{1,0:T(8,128)(2,1)S(1)}, u32[]{:S(2)}, u32[]{:S(2)}) %collective-permute-start.11) | collective-permute-done | bytes 65568 | tf_op jit(solution)/shard_map/ppermute | solution.py:26
  29.9 0.9 %collective-permute-done.12.refs_7_ = bf16[16,2048]{1,0:T(8,128)(2,1)S(1)} collective-permute-done((bf16[16,2048]{1,0:T(8,128)(2,1)S(1)}, bf16[16,2048]{1,0:T(8,128)(2,1)S(1)}, u32[]{:S(2)}, u32[]{:S(2)}) %collective-permute-start.12) | collective-permute-done | bytes 65568 | tf_op jit(solution)/shard_map/ppermute | solution.py:26
  30.7 0.0 collective-permute-done.6.refs_1_
  30.8 1.1 %shard_map.111 = (bf16[1,64,2048]{2,1,0:T(8,128)(2,1)}, bf16[1,64,2048]{2,1,0:T(8,128)(2,1)}) custom-call(bf16[1,64,2048]{2,1,0:T(8,128)(2,1)S(1)} %collective-permute-done.refs_4_.refs_0_, bf16[1,64,2048]{2,1,0:T(8,128)(2,1)S(1)} %collective-permute-done.6.refs_1_, bf16[64,48]{1,0:T(8,128)(2,1)S(1)} %get-tuple-element.28.refs_2_, ...), custom_call_target="tpu_custom_call" | custom-call | flops 10000000 | bytes 1000000 | tf_op jit(solution)/shard_map/pallas_call | solution.py:38
  (1 shorter events, 0.0 us)
Async XLA Ops:
  0.6 6.9 %collective-permute-start.1 = (s32[1,8,64]{2,1,0:T(8,128)}, s32[1,8,64]{2,1,0:T(8,128)S(1)}, u32[]{:S(2)}, u32[]{:S(2)}) collective-permute-start(s32[1,8,64]{2,1,0:T(8,128)} %bitcast.12), channel_id=1, source_target_pairs={{0,8},{8,16},{16,24},{24,0},{1,9},{9,17},{17,25},{25,1},{2,10},{10... | collective-permute-start | bytes 6152 | tf_op jit(solution)/shard_map/ppermute | solution.py:21
  3.7 10.5 %collective-permute-start = (bf16[1,64,2048]{2,1,0:T(8,128)(2,1)}, bf16[1,64,2048]{2,1,0:T(8,128)(2,1)S(1)}, u32[]{:S(2)}, u32[]{:S(2)}) collective-permute-start(bf16[1,64,2048]{2,1,0:T(8,128)(2,1)} %param.9), channel_id=1, source_target_pairs={{0,8},{8,16},{16,24},{24,0},{1,9},{9,17},{17,25},{25,1},{2,10},{10... | collective-permute-start | bytes 786440 | tf_op jit(solution)/shard_map/ppermute | solution.py:21
  7.5 2.4 %copy-start = (bf16[1,1,40,384]{3,2,1,0:T(8,128)(2,1)S(1)}, bf16[1,1,40,384]{3,2,1,0:T(8,128)(2,1)}, u32[]{:S(2)}) copy-start(bf16[1,1,40,384]{3,2,1,0:T(8,128)(2,1)} %refs_3_.1) | copy-start | bytes 92164
  7.8 6.4 %collective-permute-start.3 = (bf16[8,2048]{1,0:T(8,128)(2,1)S(1)}, bf16[8,2048]{1,0:T(8,128)(2,1)S(1)}, u32[]{:S(2)}, u32[]{:S(2)}) collective-permute-start(bf16[8,2048]{1,0:T(8,128)(2,1)S(1)} %shard_map.105.refs_0_), channel_id=1, source_target_pairs={{0,24},{8,0},{16,8},{24,16},{1,25},{9,1},{17,9},{25,17},{2,26},{10... | collective-permute-start | bytes 98312 | tf_op jit(solution)/shard_map/ppermute | solution.py:21
  9.9 3.9 %collective-permute-start.2 = (bf16[1,1,40,384]{3,2,1,0:T(8,128)(2,1)S(1)}, bf16[1,1,40,384]{3,2,1,0:T(8,128)(2,1)S(1)}, u32[]{:S(2)}, u32[]{:S(2)}) collective-permute-start(bf16[1,1,40,384]{3,2,1,0:T(8,128)(2,1)S(1)} %copy-done), channel_id=1, source_target_pairs={{0,1},{1,0},{2,3},{3,2},{4,5},{5,4},{6,7},{7,6},{8,9},{9,8},{10,11... | collective-permute-start | bytes 92168 | tf_op jit(solution)/shard_map/ppermute | solution.py:26
  13.1 4.8 %collective-permute-start.4 = (bf16[1,1,2048,384]{3,2,1,0:T(8,128)(2,1)S(1)}, bf16[1,1,2048,384]{3,2,1,0:T(8,128)(2,1)S(1)}, u32[]{:S(2)}, u32[]{:S(2)}) collective-permute-start(bf16[1,1,2048,384]{3,2,1,0:T(8,128)(2,1)S(1)} %get-tuple-element.26.refs_4_), channel_id=1, source_target_pairs={{0,1},{1,0},{2,3},{3,2},{4,5},{5,4},{6,7},{7,6},{8,9},{9,8},{10,11... | collective-permute-start | bytes 4718600 | tf_op jit(solution)/shard_map/ppermute | solution.py:26
  13.7 4.2 %collective-permute-start.5 = (bf16[1,1,192,2048]{3,2,1,0:T(8,128)(2,1)S(1)}, bf16[1,1,192,2048]{3,2,1,0:T(8,128)(2,1)S(1)}, u32[]{:S(2)}, u32[]{:S(2)}) collective-permute-start(bf16[1,1,192,2048]{3,2,1,0:T(8,128)(2,1)S(1)} %get-tuple-element.27), channel_id=1, source_target_pairs={{0,1},{1,0},{2,3},{3,2},{4,5},{5,4},{6,7},{7,6},{8,9},{9,8},{10,11... | collective-permute-start | bytes 2359304 | tf_op jit(solution)/shard_map/ppermute | solution.py:26
  14.3 5.6 %collective-permute-start.9 = (bf16[16,2048]{1,0:T(8,128)(2,1)S(1)}, bf16[16,2048]{1,0:T(8,128)(2,1)S(1)}, u32[]{:S(2)}, u32[]{:S(2)}) collective-permute-start(bf16[16,2048]{1,0:T(8,128)(2,1)S(1)} %bitcast.5), channel_id=1, source_target_pairs={{0,6},{1,7},{2,4},{3,5},{4,2},{5,3},{6,0},{7,1},{8,14},{9,15},{10,... | collective-permute-start | bytes 196616 | tf_op jit(solution)/shard_map/ppermute | solution.py:26
  16.8 4.3 %collective-permute-start.7 = (bf16[16,2048]{1,0:T(8,128)(2,1)S(1)}, bf16[16,2048]{1,0:T(8,128)(2,1)S(1)}, u32[]{:S(2)}, u32[]{:S(2)}) collective-permute-start(bf16[16,2048]{1,0:T(8,128)(2,1)S(1)} %bitcast.6), channel_id=1, source_target_pairs={{0,2},{1,3},{2,0},{3,1},{4,6},{5,7},{6,4},{7,5},{8,10},{9,11},{10,... | collective-permute-start | bytes 196616 | tf_op jit(solution)/shard_map/ppermute | solution.py:26
  17.4 4.3 %collective-permute-start.8 = (bf16[16,2048]{1,0:T(8,128)(2,1)S(1)}, bf16[16,2048]{1,0:T(8,128)(2,1)S(1)}, u32[]{:S(2)}, u32[]{:S(2)}) collective-permute-start(bf16[16,2048]{1,0:T(8,128)(2,1)S(1)} %bitcast.7), channel_id=1, source_target_pairs={{0,4},{1,5},{2,6},{3,7},{4,0},{5,1},{6,2},{7,3},{8,12},{9,13},{10,... | collective-permute-start | bytes 196616 | tf_op jit(solution)/shard_map/ppermute | solution.py:26
  17.9 12.8 %collective-permute-start.6 = (bf16[1,64,2048]{2,1,0:T(8,128)(2,1)S(1)}, bf16[1,64,2048]{2,1,0:T(8,128)(2,1)S(1)}, u32[]{:S(2)}, u32[]{:S(2)}) collective-permute-start(bf16[1,64,2048]{2,1,0:T(8,128)(2,1)S(1)} %shard_map.108), channel_id=1, source_target_pairs={{0,24},{8,0},{16,8},{24,16},{1,25},{9,1},{17,9},{25,17},{2,26},{10... | collective-permute-start | bytes 786440 | tf_op jit(solution)/shard_map/ppermute | solution.py:21
  23.5 5.7 %collective-permute-start.10 = (bf16[16,2048]{1,0:T(8,128)(2,1)S(1)}, bf16[16,2048]{1,0:T(8,128)(2,1)S(1)}, u32[]{:S(2)}, u32[]{:S(2)}) collective-permute-start(bf16[16,2048]{1,0:T(8,128)(2,1)S(1)} %get-tuple-element.34), channel_id=1, source_target_pairs={{0,6},{1,7},{2,4},{3,5},{4,2},{5,3},{6,0},{7,1},{8,14},{9,15},{10,... | collective-permute-start | bytes 196616 | tf_op jit(solution)/shard_map/ppermute | solution.py:26
  25.5 4.3 %collective-permute-start.11 = (bf16[16,2048]{1,0:T(8,128)(2,1)S(1)}, bf16[16,2048]{1,0:T(8,128)(2,1)S(1)}, u32[]{:S(2)}, u32[]{:S(2)}) collective-permute-start(bf16[16,2048]{1,0:T(8,128)(2,1)S(1)} %get-tuple-element.35), channel_id=1, source_target_pairs={{0,4},{1,5},{2,6},{3,7},{4,0},{5,1},{6,2},{7,3},{8,12},{9,13},{10,... | collective-permute-start | bytes 196616 | tf_op jit(solution)/shard_map/ppermute | solution.py:26
  26.5 4.3 %collective-permute-start.12 = (bf16[16,2048]{1,0:T(8,128)(2,1)S(1)}, bf16[16,2048]{1,0:T(8,128)(2,1)S(1)}, u32[]{:S(2)}, u32[]{:S(2)}) collective-permute-start(bf16[16,2048]{1,0:T(8,128)(2,1)S(1)} %get-tuple-element.36), channel_id=1, source_target_pairs={{0,2},{1,3},{2,0},{3,1},{4,6},{5,7},{6,4},{7,5},{8,10},{9,11},{10,... | collective-permute-start | bytes 196616 | tf_op jit(solution)/shard_map/ppermute | solution.py:26

commit v4 on v3

--- a/solution.py
+++ b/solution.py
@@ -10,8 +10,10 @@
 FSPLIT = 8
 CAP = 5
 CORES = 2
-SLOTS = 8
-PAIR = 2 * SLOTS
+ROWS = 16
+LINES = 8
+FEW = 2 * CAP - LINES
+PARTS = LINES // FEW
 MIB = 1 << 20
 
 
@@ -57,16 +59,27 @@
     return jnp.where(routes == group, 1.0, 0.0)
 
 
-def slot_picks(routes, group, rows, offset):
-    toks = routes.shape[1]
+def slot_picks(routes, group, slot):
+    rows, toks = slot.shape
     shape = (toks, toks)
     before = lax.broadcasted_iota(jnp.int32, shape, 0) < lax.broadcasted_iota(jnp.int32, shape, 1)
     before = jnp.where(before, 1.0, 0.0).astype(jnp.bfloat16)
     along = jnp.sum(hits(routes, group), axis=0, keepdims=True)
     along = jnp.broadcast_to(along, (rows, toks))
     rank = dot(along.astype(jnp.bfloat16), before)
-    slot = lax.broadcasted_iota(jnp.int32, (rows, toks), 0) - offset
     return jnp.where(rank == slot.astype(jnp.float32), along, 0.0)
+
+
+def fold(first, few):
+    part = few.shape[1] // PARTS
+    few = [few[:, index * part : (index + 1) * part] for index in range(PARTS)]
+    return jnp.concatenate([first, jnp.concatenate(few, axis=0)], axis=1)
+
+
+def unfold(message):
+    width = message.shape[1] * PARTS // (PARTS + 1)
+    few = [message[index * FEW : (index + 1) * FEW, width:] for index in range(PARTS)]
+    return message[:, :width], jnp.concatenate(few, axis=1)
 
 
 def fetch(sources, targets, semaphores):
@@ -81,7 +94,9 @@
 
 
 def pick_kernel(groups, routes, staged, rows):
-    picks = [slot_picks(routes[0], group, SLOTS, 0) for group in range(groups)]
+    row = lax.broadcasted_iota(jnp.int32, (LINES, staged.shape[1]), 0)
+    slot = jnp.where(row < FEW, CAP - FEW + row, row - CAP)
+    picks = [slot_picks(routes[0], group, slot) for group in range(groups)]
     picks = picks[0] if groups == 1 else jnp.concatenate(picks, axis=0)
     rows[...] = dot(picks.astype(jnp.bfloat16), staged[0]).astype(jnp.bfloat16)
 
@@ -90,20 +105,21 @@
     whole[...] = staged[...]
 
 
-def merge_kernel(groups, x, pick_x, rows_b, send_scale, message):
+def merge_kernel(groups, x, pick_x, rows_b, message):
     all_a = dot(pick_x[...], x[0])
     all_b = rows_b[...].astype(jnp.float32)
     for group in range(groups):
-        one = slice(group * SLOTS, (group + 1) * SLOTS)
-        scaled = all_b[one] * send_scale[pl.ds(group * SLOTS, SLOTS), :1]
-        both = [all_a[group * PAIR : group * PAIR + SLOTS], scaled]
-        message[group] = jnp.concatenate(both, axis=0).astype(jnp.bfloat16)
+        rows = slice(group * LINES, (group + 1) * LINES)
+        b = all_b[rows]
+        line = lax.broadcasted_iota(jnp.int32, b.shape, 0)
+        first = jnp.where(line < CAP, all_a[rows], b)
+        message[group] = fold(first, b[:FEW]).astype(jnp.bfloat16)
 
 
 def prepare_kernel(groups, *refs):
     far, refs = refs[:5], refs[5:]
-    staged, pick_x, place_x, place_u, send_scale, sum_scale = refs[:6]
-    near, semaphores, stage_semaphore = refs[6:10], refs[10], refs[11]
+    staged, pick_x, place_x, place_u, sum_scale = refs[:5]
+    near, semaphores, stage_semaphore = refs[5:9], refs[9], refs[10]
     stage = pltpu.make_async_copy(far[4], staged, stage_semaphore.at[0])
     stage.start()
     fetch(far[:4], near, semaphores)
@@ -112,27 +128,34 @@
     def micro(routes, logits, offset):
         scores = jnp.exp(logits[0])
         probs = scores / jnp.sum(scores, axis=0, keepdims=True)
+        slot = lax.broadcasted_iota(jnp.int32, (ROWS, routes.shape[2]), 0) - offset
         picks, scales = [], []
         for group in range(groups):
-            pick = slot_picks(routes[0], group, PAIR, offset)
+            pick = slot_picks(routes[0], group, slot)
             prob = jnp.sum(hits(routes[0], group) * probs, axis=0, keepdims=True)
             scales.append(jnp.sum(pick * prob, axis=1, keepdims=True))
             picks.append(pick)
         return picks, scales
 
     picks_a, scales_a = micro(routes_a, logits_a, 0)
-    picks_b, scales_b = micro(routes_b, logits_b, SLOTS)
+    picks_b, scales_b = micro(routes_b, logits_b, CAP)
     place_x[...] = jnp.concatenate(picks_a * 3, axis=0).T.astype(jnp.bfloat16)
     place_u[...] = jnp.concatenate(picks_b * 3, axis=0).T.astype(jnp.bfloat16)
-    half_row = lax.broadcasted_iota(jnp.int32, (PAIR, 128), 0)
+    first = [pick[:LINES] for pick in picks_a]
+    pick_x[...] = (first[0] if groups == 1 else jnp.concatenate(first, axis=0)).astype(jnp.bfloat16)
     for group in range(groups):
-        rows = pl.ds(group * PAIR, PAIR)
-        pick_x[rows, :] = picks_a[group].astype(jnp.bfloat16)
-        send_scale[pl.ds(group * SLOTS, SLOTS), :] = jnp.broadcast_to(
-            scales_b[group][SLOTS:], (SLOTS, 128)
-        )
-        sum_scale[rows, :] = jnp.where(half_row < SLOTS, scales_a[group], 1.0)
+        scale = scales_a[group] + scales_b[group]
+        sum_scale[pl.ds(group * ROWS, ROWS), :] = jnp.broadcast_to(scale, (ROWS, 128))
     stage.wait()
+
+
+def lines_of(shape, chips):
+    line = lax.broadcasted_iota(jnp.int32, shape, 0)
+    early = line < chips * LINES
+    late = line - chips * LINES
+    origin = jnp.where(early, line // LINES, late // FEW)
+    slot = jnp.where(early, line % LINES - CAP, CAP - FEW + late % FEW)
+    return origin, slot
 
 
 def pack_half(index, chips, mixed, entry, down, saved, lower, second, factors):
@@ -146,14 +169,12 @@
 
     me = lax.axis_index("expert")
     held = saved.shape[2]
-    shape = (chips * PAIR, held)
-    line = lax.broadcasted_iota(jnp.int32, shape, 0)
-    origin = line // PAIR
+    shape = (factors.shape[0], held)
+    origin, slot = lines_of(shape, chips)
     if mixed:
         origin = origin ^ (me // CORES)
-    slot = line % PAIR - SLOTS
     wanted = (CORES * origin + me % CORES) * CAP + slot
-    wanted = jnp.where((slot >= 0) & (slot < CAP), wanted, -1)
+    wanted = jnp.where(slot >= 0, wanted, -1)
     chosen = jnp.where(wanted == lax.broadcasted_iota(jnp.int32, shape, 1), 1.0, 0.0)
     stored = dot(chosen.astype(jnp.bfloat16), saved[0, 0])
     gates = stored[:, :half]
@@ -187,7 +208,8 @@
     entries = refs[chips : chips + 2]
     lower, second, factors = refs[chips + 2 : chips + 5]
     results = refs[chips + 5 :]
-    rows = jnp.concatenate([ref[...] for ref in arrived], axis=0)
+    firsts, fews = zip(*[unfold(ref[...].astype(jnp.float32)) for ref in arrived])
+    rows = jnp.concatenate([*firsts, *fews], axis=0).astype(jnp.bfloat16)
     back = dot(rows, lower[...])
     half = back.shape[1] // 2
     grads = jnp.concatenate([back, back], axis=1) * factors[...]
@@ -197,12 +219,14 @@
         gate = made[:, :half]
         hidden.append(gate * jax.nn.sigmoid(gate) * made[:, half:])
     hidden = jnp.concatenate(hidden, axis=1)
-    line = lax.broadcasted_iota(jnp.int32, hidden.shape, 0) % PAIR
-    hidden = jnp.where(line < SLOTS, hidden, 0.0)
+    _, slot = lines_of(hidden.shape, chips)
+    hidden = jnp.where(slot < 0, hidden, 0.0)
     inner = jnp.concatenate([grads.astype(jnp.bfloat16), hidden.astype(jnp.bfloat16)], axis=1)
-    total = dot(inner, second[...]).astype(jnp.bfloat16)
+    total = dot(inner, second[...])
     for index, ref in enumerate(results):
-        ref[...] = total[index * PAIR : (index + 1) * PAIR]
+        late = chips * LINES + index * FEW
+        first = total[index * LINES : (index + 1) * LINES]
+        ref[...] = fold(first, total[late : late + FEW]).astype(jnp.bfloat16)
 
 
 def finish_kernel(groups, chips, *refs):
@@ -215,7 +239,10 @@
         total = returned[group * share][...].astype(jnp.float32)
         for ref in returned[group * share + 1 : (group + 1) * share]:
             total = total + ref[...].astype(jnp.float32)
-        sums.append(total * sum_scale[pl.ds(group * PAIR, PAIR), :1])
+        first, few = unfold(total)
+        empty = jnp.zeros((ROWS - 2 * CAP, first.shape[1]), jnp.float32)
+        total = jnp.concatenate([first, few, empty], axis=0)
+        sums.append(total * sum_scale[pl.ds(group * ROWS, ROWS), :1])
     rest = sums[0] if groups == 1 else jnp.concatenate(sums, axis=0)
     pieces = []
     for _ in range(3):
@@ -252,18 +279,18 @@
     ]
 
     block = shape((1, toks, width), bf16)
+    folded = (LINES, width + width // PARTS)
     asked = along_sections(routes_b, 1)
     layer_input = along_sections(section_output, 1)
     own_values = (routes_a, logits_a, routes_b, logits_b)
-    staged, pick_x, place_x, place_u, send_scale, sum_scale = call(
+    staged, pick_x, place_x, place_u, sum_scale = call(
         functools.partial(prepare_kernel, groups),
         (
             block,
-            shape((groups * PAIR, toks), bf16),
-            shape((toks, 3 * groups * PAIR), bf16),
-            shape((toks, 3 * groups * PAIR), bf16),
-            shape((groups * SLOTS, 128), f32),
-            shape((groups * PAIR, 128), f32),
+            shape((groups * LINES, toks), bf16),
+            shape((toks, 3 * groups * ROWS), bf16),
+            shape((toks, 3 * groups * ROWS), bf16),
+            shape((groups * ROWS, 128), f32),
         ),
         (),
         8 * MIB,
@@ -278,7 +305,7 @@
     )
     rows_b = call(
         functools.partial(pick_kernel, groups),
-        shape((groups * SLOTS, width), bf16),
+        shape((groups * LINES, width), bf16),
         (asked, staged),
         8 * MIB,
         10_000_000_000,
@@ -288,7 +315,7 @@
     packs = (
         shape((width, 2 * half), bf16),
         shape((6 * half, width), bf16),
-        shape((chips * PAIR, 4 * half), f32),
+        shape((2 * CAP * chips, 4 * half), f32),
     )
     entry_own, down_own, *packed = call(
         functools.partial(pack_own_kernel, chips, direct),
@@ -308,8 +335,8 @@
     weights = [across_owners(value, 1) for value in (entry_own, down_own, saved_projections)]
     message = call(
         functools.partial(merge_kernel, groups),
-        shape((groups, PAIR, width), bf16),
-        (layer_input, pick_x, rows_b, send_scale),
+        shape((groups, *folded), bf16),
+        (layer_input, pick_x, rows_b),
         8 * MIB,
         50_000_000_000,
         100_000,
@@ -346,7 +373,7 @@
     )
     results = call(
         functools.partial(expert_kernel, chips),
-        (shape((PAIR, width), bf16),) * chips,
+        (shape(folded, bf16),) * chips,
         (*arrived, entry_own, weights[0], *packed),
         16 * MIB,
         800_000_000,

time: 32 us -> 31.5 us (0.984)
  Pallas kernels: 8.7 us -> 8.18 us
    pallas_call x8, Pallas kernels: 8.7 us -> 8.18 us  [call(): pl.pallas_call(body, out_shape=outs, in_specs=[anywhere] * waits + [dista...]
    ppermute x9, waiting for transfers between devices: 4.59 us -> 4.1 us  [across_owners(): lax.ppermute(value, 'expert', [(source, source ^ flip) for source in rang...]
    ppermute x4, waiting for transfers between devices: 1.57 us -> 2.03 us  [along_sections(): return lax.ppermute(value, 'segment', pairs)]
  transfers between devices with their start and end apart: 13 -> 13, of which waited for: 7 -> 7; matrix products, arithmetic and copies ran while one was open for 0% -> 0% of each run, Pallas kernels for 24% -> 23%
where the time goes in v4:
time: 31.5 us; the launch traced here: 31.2 us
  starting transfers between devices  16.3 us (52%)
  Pallas kernels  8.18 us (26%)
  waiting for transfers between devices  6.13 us (19%)
  between operations  0.68 us (2%)
    ppermute x4, starting transfers between devices, along_sections(): return lax.ppermute(value, 'segment', pairs)  8.51 us
    pallas_call x8, Pallas kernels, call(): pl.pallas_call(body, out_shape=outs, in_specs=[anywhere] * waits + [dista...  8.18 us
    ppermute x9, starting transfers between devices, across_owners(): lax.ppermute(value, 'expert', [(source, source ^ flip) for source in rang...  7.74 us
    ppermute x9, waiting for transfers between devices, across_owners(): lax.ppermute(value, 'expert', [(source, source ^ flip) for source in rang...  4.1 us
    ppermute x4, waiting for transfers between devices, along_sections(): return lax.ppermute(value, 'segment', pairs)  2.03 us
  transfers between devices with their start and end apart: 13, of which 7 were waited for; matrix products, arithmetic and copies ran while one was open for 0% of the time, Pallas kernels for 23%

profile of v4, /device:TPU:0, one launch (start us, length us, event | category | flops | bytes accessed | tf_op | source)
XLA Modules:
  0.0 31.2 jit_solution(2652352921537522189)
XLA Ops:
  0.6 3.1 %collective-permute-start.1 = (s32[1,8,64]{2,1,0:T(8,128)}, s32[1,8,64]{2,1,0:T(8,128)S(1)}, u32[]{:S(2)}, u32[]{:S(2)}) collective-permute-start(s32[1,8,64]{2,1,0:T(8,128)} %bitcast.12), channel_id=1, source_target_pairs={{0,8},{8,16},{16,24},{24,0},{1,9},{9,17},{17,25},{25,1},{2,10},{10... | collective-permute-start | bytes 6152 | tf_op jit(solution)/shard_map/ppermute | solution.py:23
  3.7 1.6 %collective-permute-start = (bf16[1,64,2048]{2,1,0:T(8,128)(2,1)}, bf16[1,64,2048]{2,1,0:T(8,128)(2,1)S(1)}, u32[]{:S(2)}, u32[]{:S(2)}) collective-permute-start(bf16[1,64,2048]{2,1,0:T(8,128)(2,1)} %param.9), channel_id=1, source_target_pairs={{0,8},{8,16},{16,24},{24,0},{1,9},{9,17},{17,25},{25,1},{2,10},{10... | collective-permute-start | bytes 786440 | tf_op jit(solution)/shard_map/ppermute | solution.py:23
  5.3 1.1 %shard_map.104 = (bf16[1,64,2048]{2,1,0:T(8,128)(2,1)S(1)}, bf16[8,64]{1,0:T(8,128)(2,1)S(1)}, bf16[64,48]{1,0:T(8,128)(2,1)S(1)}, bf16[64,48]{1,0:T(8,128)(2,1)S(1)}, f32[16,128]{1,0:T(8,128)S(1)}) custom-call(s32[1,8,64]{2,1,0:T(8,128)} %bitcast.9, f32[1,8,64]{2,1,0:T(8,128)} %bitcast.10, s32[1,8,64]{2,1,0:T(8,128)} %bitcast.13, f32[1,8,64]{2,1,0:T(8,128)} %bitcast.11, ...), custom_call_target="tpu_custom_call" | custom-call | flops 10000000 | bytes 1000000 | tf_op jit(solution)/shard_map/pallas_call | solution.py:40
  6.4 1.1 %collective-permute-done.1.refs_0_ = s32[1,8,64]{2,1,0:T(8,128)S(1)} collective-permute-done((s32[1,8,64]{2,1,0:T(8,128)}, s32[1,8,64]{2,1,0:T(8,128)S(1)}, u32[]{:S(2)}, u32[]{:S(2)}) %collective-permute-start.1) | collective-permute-done | bytes 2080 | tf_op jit(solution)/shard_map/ppermute | solution.py:23
  7.5 0.0 copy-start
  7.5 0.3 shard_map.105.refs_0_
  7.8 2.1 %collective-permute-start.3 = (bf16[8,2048]{1,0:T(8,128)(2,1)S(1)}, bf16[8,2048]{1,0:T(8,128)(2,1)S(1)}, u32[]{:S(2)}, u32[]{:S(2)}) collective-permute-start(bf16[8,2048]{1,0:T(8,128)(2,1)S(1)} %shard_map.105.refs_0_), channel_id=1, source_target_pairs={{0,24},{8,0},{16,8},{24,16},{1,25},{9,1},{17,9},{25,17},{2,26},{10... | collective-permute-start | bytes 98312 | tf_op jit(solution)/shard_map/ppermute | solution.py:23
  9.9 0.0 copy-done
  9.9 0.0 collective-permute-start.2
  9.9 2.7 %shard_map.106 = (bf16[1,1,2048,384]{3,2,1,0:T(8,128)(2,1)S(1)}, bf16[1,1,192,2048]{3,2,1,0:T(8,128)(2,1)S(1)}, bf16[2048,384]{1,0:T(8,128)(2,1)S(1)}, bf16[1152,2048]{1,0:T(8,128)(2,1)S(1)}, f32[40,768]{1,0:T(8,128)S(1)}) custom-call(bf16[8,2048]{1,0:T(8,128)(2,1)S(1)} %shard_map.105.refs_0_, bf16[1,1,2048,384]{3,2,1,0:T(8,128)(2,1)} %refs_1_.1, ...), custom_call_target="tpu_custom_call" | custom-call | flops 10000000 | bytes 5000000 | tf_op jit(solution)/shard_map/pallas_call | solution.py:40
  12.7 0.6 %collective-permute-start.4 = (bf16[1,1,2048,384]{3,2,1,0:T(8,128)(2,1)S(1)}, bf16[1,1,2048,384]{3,2,1,0:T(8,128)(2,1)S(1)}, u32[]{:S(2)}, u32[]{:S(2)}) collective-permute-start(bf16[1,1,2048,384]{3,2,1,0:T(8,128)(2,1)S(1)} %get-tuple-element.24.refs_4_), channel_id=1, source_target_pairs={{0,1},{1,0},{2,3},{3,2},{4,5},{5,4},{6,7},{7,6},{8,9},{9,8},{10,11... | collective-permute-start | bytes 4718600 | tf_op jit(solution)/shard_map/ppermute | solution.py:28
  13.2 0.1 collective-permute-start.5
  13.3 0.0 collective-permute-done.2.refs_3_
  13.3 0.9 %collective-permute-done.3.refs_6_ = bf16[8,2048]{1,0:T(8,128)(2,1)S(1)} collective-permute-done((bf16[8,2048]{1,0:T(8,128)(2,1)S(1)}, bf16[8,2048]{1,0:T(8,128)(2,1)S(1)}, u32[]{:S(2)}, u32[]{:S(2)}) %collective-permute-start.3) | collective-permute-done | bytes 32800 | tf_op jit(solution)/shard_map/ppermute | solution.py:23
  14.2 0.0 collective-permute-done.refs_4_.refs_0_
  14.2 0.2 shard_map.107.refs_0_
  14.3 2.5 %collective-permute-start.9 = (bf16[8,2560]{1,0:T(8,128)(2,1)S(1)}, bf16[8,2560]{1,0:T(8,128)(2,1)S(1)}, u32[]{:S(2)}, u32[]{:S(2)}) collective-permute-start(bf16[8,2560]{1,0:T(8,128)(2,1)S(1)} %bitcast.5), channel_id=1, source_target_pairs={{0,6},{1,7},{2,4},{3,5},{4,2},{5,3},{6,0},{7,1},{8,14},{9,15},{10,... | collective-permute-start | bytes 122888 | tf_op jit(solution)/shard_map/ppermute | solution.py:28
  16.8 0.5 %collective-permute-start.7 = (bf16[8,2560]{1,0:T(8,128)(2,1)S(1)}, bf16[8,2560]{1,0:T(8,128)(2,1)S(1)}, u32[]{:S(2)}, u32[]{:S(2)}) collective-permute-start(bf16[8,2560]{1,0:T(8,128)(2,1)S(1)} %bitcast.6), channel_id=1, source_target_pairs={{0,2},{1,3},{2,0},{3,1},{4,6},{5,7},{6,4},{7,5},{8,10},{9,11},{10,... | collective-permute-start | bytes 122888 | tf_op jit(solution)/shard_map/ppermute | solution.py:28
  17.4 0.5 %collective-permute-start.8 = (bf16[8,2560]{1,0:T(8,128)(2,1)S(1)}, bf16[8,2560]{1,0:T(8,128)(2,1)S(1)}, u32[]{:S(2)}, u32[]{:S(2)}) collective-permute-start(bf16[8,2560]{1,0:T(8,128)(2,1)S(1)} %bitcast.7), channel_id=1, source_target_pairs={{0,4},{1,5},{2,6},{3,7},{4,0},{5,1},{6,2},{7,3},{8,12},{9,13},{10,... | collective-permute-start | bytes 122888 | tf_op jit(solution)/shard_map/ppermute | solution.py:28
  17.9 0.0 collective-permute-done.5.refs_2_
  17.9 0.0 collective-permute-done.4.refs_1_.refs_5_
  17.9 1.7 %collective-permute-start.6 = (bf16[1,64,2048]{2,1,0:T(8,128)(2,1)S(1)}, bf16[1,64,2048]{2,1,0:T(8,128)(2,1)S(1)}, u32[]{:S(2)}, u32[]{:S(2)}) collective-permute-start(bf16[1,64,2048]{2,1,0:T(8,128)(2,1)S(1)} %shard_map.108), channel_id=1, source_target_pairs={{0,24},{8,0},{16,8},{24,16},{1,25},{9,1},{17,9},{25,17},{2,26},{10... | collective-permute-start | bytes 786440 | tf_op jit(solution)/shard_map/ppermute | solution.py:23
  19.6 0.0 collective-permute-done.9.refs_0_.refs_3_
  19.7 1.1 %shard_map.109 = (bf16[2048,384]{1,0:T(8,128)(2,1)S(1)}, bf16[1152,2048]{1,0:T(8,128)(2,1)S(1)}, f32[40,768]{1,0:T(8,128)S(1)}) custom-call(bf16[8,2560]{1,0:T(8,128)(2,1)S(1)} %collective-permute-done.9.refs_0_.refs_3_, ...), custom_call_target="tpu_custom_call", output_to_operand_aliasing={{0}: (4, {}), {1}: (5, {}), {2}: (6, {})} | custom-call | flops 10000000000 | bytes 5000000 | tf_op jit(solution)/shard_map/pallas_call | solution.py:40
  20.7 0.1 collective-permute-done.7.refs_1_
  20.8 0.5 %collective-permute-done.8.refs_2_ = bf16[8,2560]{1,0:T(8,128)(2,1)S(1)} collective-permute-done((bf16[8,2560]{1,0:T(8,128)(2,1)S(1)}, bf16[8,2560]{1,0:T(8,128)(2,1)S(1)}, u32[]{:S(2)}, u32[]{:S(2)}) %collective-permute-start.8) | collective-permute-done | bytes 40992 | tf_op jit(solution)/shard_map/ppermute | solution.py:28
  21.4 1.8 %shard_map.110 = (bf16[8,2560]{1,0:T(8,128)(2,1)S(1)}, bf16[8,2560]{1,0:T(8,128)(2,1)S(1)}, bf16[8,2560]{1,0:T(8,128)(2,1)S(1)}, bf16[8,2560]{1,0:T(8,128)(2,1)S(1)}) custom-call(bf16[8,2560]{1,0:T(8,128)(2,1)S(1)} %bitcast.8, bf16[8,2560]{1,0:T(8,128)(2,1)S(1)} %collective-permute-done.7.refs_1_, bf16[8,2560]{1,0:T(8,128)(2,1)S(1)} %collective-permute-done.8.refs_2_, ...), custom_call_target="tpu_custom_call" | custom-call | flops 800000000 | bytes 5000000 | tf_op jit(solution)/shard_map/pallas_call | solution.py:40
  23.2 1.9 %collective-permute-start.10 = (bf16[8,2560]{1,0:T(8,128)(2,1)S(1)}, bf16[8,2560]{1,0:T(8,128)(2,1)S(1)}, u32[]{:S(2)}, u32[]{:S(2)}) collective-permute-start(bf16[8,2560]{1,0:T(8,128)(2,1)S(1)} %get-tuple-element.32), channel_id=1, source_target_pairs={{0,6},{1,7},{2,4},{3,5},{4,2},{5,3},{6,0},{7,1},{8,14},{9,15},{10,... | collective-permute-start | bytes 122888 | tf_op jit(solution)/shard_map/ppermute | solution.py:28
  25.1 1.1 %collective-permute-start.11 = (bf16[8,2560]{1,0:T(8,128)(2,1)S(1)}, bf16[8,2560]{1,0:T(8,128)(2,1)S(1)}, u32[]{:S(2)}, u32[]{:S(2)}) collective-permute-start(bf16[8,2560]{1,0:T(8,128)(2,1)S(1)} %get-tuple-element.33), channel_id=1, source_target_pairs={{0,4},{1,5},{2,6},{3,7},{4,0},{5,1},{6,2},{7,3},{8,12},{9,13},{10,... | collective-permute-start | bytes 122888 | tf_op jit(solution)/shard_map/ppermute | solution.py:28
  26.2 0.5 %collective-permute-start.12 = (bf16[8,2560]{1,0:T(8,128)(2,1)S(1)}, bf16[8,2560]{1,0:T(8,128)(2,1)S(1)}, u32[]{:S(2)}, u32[]{:S(2)}) collective-permute-start(bf16[8,2560]{1,0:T(8,128)(2,1)S(1)} %get-tuple-element.34), channel_id=1, source_target_pairs={{0,2},{1,3},{2,0},{3,1},{4,6},{5,7},{6,4},{7,5},{8,10},{9,11},{10,... | collective-permute-start | bytes 122888 | tf_op jit(solution)/shard_map/ppermute | solution.py:28
  26.7 1.4 %collective-permute-done.10.refs_5_ = bf16[8,2560]{1,0:T(8,128)(2,1)S(1)} collective-permute-done((bf16[8,2560]{1,0:T(8,128)(2,1)S(1)}, bf16[8,2560]{1,0:T(8,128)(2,1)S(1)}, u32[]{:S(2)}, u32[]{:S(2)}) %collective-permute-start.10) | collective-permute-done | bytes 40992 | tf_op jit(solution)/shard_map/ppermute | solution.py:28
  28.1 0.9 %collective-permute-done.11.refs_6_ = bf16[8,2560]{1,0:T(8,128)(2,1)S(1)} collective-permute-done((bf16[8,2560]{1,0:T(8,128)(2,1)S(1)}, bf16[8,2560]{1,0:T(8,128)(2,1)S(1)}, u32[]{:S(2)}, u32[]{:S(2)}) %collective-permute-start.11) | collective-permute-done | bytes 40992 | tf_op jit(solution)/shard_map/ppermute | solution.py:28
  29.1 1.1 %collective-permute-done.12.refs_7_ = bf16[8,2560]{1,0:T(8,128)(2,1)S(1)} collective-permute-done((bf16[8,2560]{1,0:T(8,128)(2,1)S(1)}, bf16[8,2560]{1,0:T(8,128)(2,1)S(1)}, u32[]{:S(2)}, u32[]{:S(2)}) %collective-permute-start.12) | collective-permute-done | bytes 40992 | tf_op jit(solution)/shard_map/ppermute | solution.py:28
  30.2 0.0 collective-permute-done.6.refs_1_
  30.2 1.1 %shard_map.111 = (bf16[1,64,2048]{2,1,0:T(8,128)(2,1)}, bf16[1,64,2048]{2,1,0:T(8,128)(2,1)}) custom-call(bf16[1,64,2048]{2,1,0:T(8,128)(2,1)S(1)} %collective-permute-done.refs_4_.refs_0_, bf16[1,64,2048]{2,1,0:T(8,128)(2,1)S(1)} %collective-permute-done.6.refs_1_, bf16[64,48]{1,0:T(8,128)(2,1)S(1)} %get-tuple-element.26.refs_2_, ...), custom_call_target="tpu_custom_call" | custom-call | flops 10000000 | bytes 1000000 | tf_op jit(solution)/shard_map/pallas_call | solution.py:40
  (1 shorter events, 0.0 us)
Async XLA Ops:
  0.6 6.9 %collective-permute-start.1 = (s32[1,8,64]{2,1,0:T(8,128)}, s32[1,8,64]{2,1,0:T(8,128)S(1)}, u32[]{:S(2)}, u32[]{:S(2)}) collective-permute-start(s32[1,8,64]{2,1,0:T(8,128)} %bitcast.12), channel_id=1, source_target_pairs={{0,8},{8,16},{16,24},{24,0},{1,9},{9,17},{17,25},{25,1},{2,10},{10... | collective-permute-start | bytes 6152 | tf_op jit(solution)/shard_map/ppermute | solution.py:23
  3.7 10.5 %collective-permute-start = (bf16[1,64,2048]{2,1,0:T(8,128)(2,1)}, bf16[1,64,2048]{2,1,0:T(8,128)(2,1)S(1)}, u32[]{:S(2)}, u32[]{:S(2)}) collective-permute-start(bf16[1,64,2048]{2,1,0:T(8,128)(2,1)} %param.9), channel_id=1, source_target_pairs={{0,8},{8,16},{16,24},{24,0},{1,9},{9,17},{17,25},{25,1},{2,10},{10... | collective-permute-start | bytes 786440 | tf_op jit(solution)/shard_map/ppermute | solution.py:23
  7.5 2.4 %copy-start = (bf16[1,1,40,384]{3,2,1,0:T(8,128)(2,1)S(1)}, bf16[1,1,40,384]{3,2,1,0:T(8,128)(2,1)}, u32[]{:S(2)}) copy-start(bf16[1,1,40,384]{3,2,1,0:T(8,128)(2,1)} %refs_3_.1) | copy-start | bytes 92164
  7.8 6.4 %collective-permute-start.3 = (bf16[8,2048]{1,0:T(8,128)(2,1)S(1)}, bf16[8,2048]{1,0:T(8,128)(2,1)S(1)}, u32[]{:S(2)}, u32[]{:S(2)}) collective-permute-start(bf16[8,2048]{1,0:T(8,128)(2,1)S(1)} %shard_map.105.refs_0_), channel_id=1, source_target_pairs={{0,24},{8,0},{16,8},{24,16},{1,25},{9,1},{17,9},{25,17},{2,26},{10... | collective-permute-start | bytes 98312 | tf_op jit(solution)/shard_map/ppermute | solution.py:23
  9.9 3.4 %collective-permute-start.2 = (bf16[1,1,40,384]{3,2,1,0:T(8,128)(2,1)S(1)}, bf16[1,1,40,384]{3,2,1,0:T(8,128)(2,1)S(1)}, u32[]{:S(2)}, u32[]{:S(2)}) collective-permute-start(bf16[1,1,40,384]{3,2,1,0:T(8,128)(2,1)S(1)} %copy-done), channel_id=1, source_target_pairs={{0,1},{1,0},{2,3},{3,2},{4,5},{5,4},{6,7},{7,6},{8,9},{9,8},{10,11... | collective-permute-start | bytes 92168 | tf_op jit(solution)/shard_map/ppermute | solution.py:28
  12.7 5.2 %collective-permute-start.4 = (bf16[1,1,2048,384]{3,2,1,0:T(8,128)(2,1)S(1)}, bf16[1,1,2048,384]{3,2,1,0:T(8,128)(2,1)S(1)}, u32[]{:S(2)}, u32[]{:S(2)}) collective-permute-start(bf16[1,1,2048,384]{3,2,1,0:T(8,128)(2,1)S(1)} %get-tuple-element.24.refs_4_), channel_id=1, source_target_pairs={{0,1},{1,0},{2,3},{3,2},{4,5},{5,4},{6,7},{7,6},{8,9},{9,8},{10,11... | collective-permute-start | bytes 4718600 | tf_op jit(solution)/shard_map/ppermute | solution.py:28
  13.2 4.7 %collective-permute-start.5 = (bf16[1,1,192,2048]{3,2,1,0:T(8,128)(2,1)S(1)}, bf16[1,1,192,2048]{3,2,1,0:T(8,128)(2,1)S(1)}, u32[]{:S(2)}, u32[]{:S(2)}) collective-permute-start(bf16[1,1,192,2048]{3,2,1,0:T(8,128)(2,1)S(1)} %get-tuple-element.25), channel_id=1, source_target_pairs={{0,1},{1,0},{2,3},{3,2},{4,5},{5,4},{6,7},{7,6},{8,9},{9,8},{10,11... | collective-permute-start | bytes 2359304 | tf_op jit(solution)/shard_map/ppermute | solution.py:28
  14.3 5.3 %collective-permute-start.9 = (bf16[8,2560]{1,0:T(8,128)(2,1)S(1)}, bf16[8,2560]{1,0:T(8,128)(2,1)S(1)}, u32[]{:S(2)}, u32[]{:S(2)}) collective-permute-start(bf16[8,2560]{1,0:T(8,128)(2,1)S(1)} %bitcast.5), channel_id=1, source_target_pairs={{0,6},{1,7},{2,4},{3,5},{4,2},{5,3},{6,0},{7,1},{8,14},{9,15},{10,... | collective-permute-start | bytes 122888 | tf_op jit(solution)/shard_map/ppermute | solution.py:28
  16.8 4.0 %collective-permute-start.7 = (bf16[8,2560]{1,0:T(8,128)(2,1)S(1)}, bf16[8,2560]{1,0:T(8,128)(2,1)S(1)}, u32[]{:S(2)}, u32[]{:S(2)}) collective-permute-start(bf16[8,2560]{1,0:T(8,128)(2,1)S(1)} %bitcast.6), channel_id=1, source_target_pairs={{0,2},{1,3},{2,0},{3,1},{4,6},{5,7},{6,4},{7,5},{8,10},{9,11},{10,... | collective-permute-start | bytes 122888 | tf_op jit(solution)/shard_map/ppermute | solution.py:28
  17.4 4.0 %collective-permute-start.8 = (bf16[8,2560]{1,0:T(8,128)(2,1)S(1)}, bf16[8,2560]{1,0:T(8,128)(2,1)S(1)}, u32[]{:S(2)}, u32[]{:S(2)}) collective-permute-start(bf16[8,2560]{1,0:T(8,128)(2,1)S(1)} %bitcast.7), channel_id=1, source_target_pairs={{0,4},{1,5},{2,6},{3,7},{4,0},{5,1},{6,2},{7,3},{8,12},{9,13},{10,... | collective-permute-start | bytes 122888 | tf_op jit(solution)/shard_map/ppermute | solution.py:28
  17.9 12.3 %collective-permute-start.6 = (bf16[1,64,2048]{2,1,0:T(8,128)(2,1)S(1)}, bf16[1,64,2048]{2,1,0:T(8,128)(2,1)S(1)}, u32[]{:S(2)}, u32[]{:S(2)}) collective-permute-start(bf16[1,64,2048]{2,1,0:T(8,128)(2,1)S(1)} %shard_map.108), channel_id=1, source_target_pairs={{0,24},{8,0},{16,8},{24,16},{1,25},{9,1},{17,9},{25,17},{2,26},{10... | collective-permute-start | bytes 786440 | tf_op jit(solution)/shard_map/ppermute | solution.py:23
  23.2 5.0 %collective-permute-start.10 = (bf16[8,2560]{1,0:T(8,128)(2,1)S(1)}, bf16[8,2560]{1,0:T(8,128)(2,1)S(1)}, u32[]{:S(2)}, u32[]{:S(2)}) collective-permute-start(bf16[8,2560]{1,0:T(8,128)(2,1)S(1)} %get-tuple-element.32), channel_id=1, source_target_pairs={{0,6},{1,7},{2,4},{3,5},{4,2},{5,3},{6,0},{7,1},{8,14},{9,15},{10,... | collective-permute-start | bytes 122888 | tf_op jit(solution)/shard_map/ppermute | solution.py:28
  25.1 4.0 %collective-permute-start.11 = (bf16[8,2560]{1,0:T(8,128)(2,1)S(1)}, bf16[8,2560]{1,0:T(8,128)(2,1)S(1)}, u32[]{:S(2)}, u32[]{:S(2)}) collective-permute-start(bf16[8,2560]{1,0:T(8,128)(2,1)S(1)} %get-tuple-element.33), channel_id=1, source_target_pairs={{0,4},{1,5},{2,6},{3,7},{4,0},{5,1},{6,2},{7,3},{8,12},{9,13},{10,... | collective-permute-start | bytes 122888 | tf_op jit(solution)/shard_map/ppermute | solution.py:28
  26.2 4.0 %collective-permute-start.12 = (bf16[8,2560]{1,0:T(8,128)(2,1)S(1)}, bf16[8,2560]{1,0:T(8,128)(2,1)S(1)}, u32[]{:S(2)}, u32[]{:S(2)}) collective-permute-start(bf16[8,2560]{1,0:T(8,128)(2,1)S(1)} %get-tuple-element.34), channel_id=1, source_target_pairs={{0,2},{1,3},{2,0},{3,1},{4,6},{5,7},{6,4},{7,5},{8,10},{9,11},{10,... | collective-permute-start | bytes 122888 | tf_op jit(solution)/shard_map/ppermute | solution.py:28

commit v5 on v4

--- a/solution.py
+++ b/solution.py
@@ -55,6 +55,11 @@
     return jnp.dot(left, right, preferred_element_type=jnp.float32)
 
 
+def dot_by_columns(left, right):
+    spans = range(0, right.shape[1], 128)
+    return jnp.concatenate([dot(left, right[:, start : start + 128]) for start in spans], axis=1)
+
+
 def hits(routes, group):
     return jnp.where(routes == group, 1.0, 0.0)
 
@@ -76,6 +81,36 @@
     return jnp.concatenate([first, jnp.concatenate(few, axis=0)], axis=1)
 
 
+def runs(width):
+    line_width = width * CAP // LINES
+    rest = width - line_width
+    place, found = 0, []
+    while place < CAP * rest:
+        row, column = divmod(place, rest)
+        line, start = divmod(place, line_width)
+        length = min(rest - column, line_width - start)
+        found.append((row, line_width + column, CAP + line, start, length))
+        place += length
+    return line_width, found
+
+
+def fold_rows(rows):
+    line_width, found = runs(rows.shape[1])
+    lines = [[] for _ in range(LINES - CAP)]
+    for row, column, line, _, length in found:
+        lines[line - CAP].append(rows[row : row + 1, column : column + length])
+    lines = [jnp.concatenate(parts, axis=1) for parts in lines]
+    return jnp.concatenate([rows[:CAP, :line_width], *lines], axis=0)
+
+
+def unfold_rows(lines, width):
+    line_width, found = runs(width)
+    rows = [[lines[row : row + 1]] for row in range(CAP)]
+    for row, _, line, start, length in found:
+        rows[row].append(lines[line : line + 1, start : start + length])
+    return jnp.concatenate([jnp.concatenate(parts, axis=1) for parts in rows], axis=0)
+
+
 def unfold(message):
     width = message.shape[1] * PARTS // (PARTS + 1)
     few = [message[index * FEW : (index + 1) * FEW, width:] for index in range(PARTS)]
@@ -94,11 +129,10 @@
 
 
 def pick_kernel(groups, routes, staged, rows):
-    row = lax.broadcasted_iota(jnp.int32, (LINES, staged.shape[1]), 0)
-    slot = jnp.where(row < FEW, CAP - FEW + row, row - CAP)
-    picks = [slot_picks(routes[0], group, slot) for group in range(groups)]
-    picks = picks[0] if groups == 1 else jnp.concatenate(picks, axis=0)
-    rows[...] = dot(picks.astype(jnp.bfloat16), staged[0]).astype(jnp.bfloat16)
+    slot = lax.broadcasted_iota(jnp.int32, (LINES, staged.shape[1]), 0)
+    for group in range(groups):
+        pick = slot_picks(routes[0], group, slot).astype(jnp.bfloat16)
+        rows[group] = fold_rows(dot(pick, staged[0])).astype(jnp.bfloat16)
 
 
 def release_kernel(staged, whole):
@@ -107,13 +141,11 @@
 
 def merge_kernel(groups, x, pick_x, rows_b, message):
     all_a = dot(pick_x[...], x[0])
-    all_b = rows_b[...].astype(jnp.float32)
     for group in range(groups):
-        rows = slice(group * LINES, (group + 1) * LINES)
-        b = all_b[rows]
-        line = lax.broadcasted_iota(jnp.int32, b.shape, 0)
-        first = jnp.where(line < CAP, all_a[rows], b)
-        message[group] = fold(first, b[:FEW]).astype(jnp.bfloat16)
+        a = all_a[group * LINES : group * LINES + CAP]
+        b = unfold_rows(rows_b[group].astype(jnp.float32), x.shape[2])
+        first = jnp.concatenate([a, b[: CAP - FEW]], axis=0)
+        message[group] = fold(first, b[CAP - FEW :]).astype(jnp.bfloat16)
 
 
 def prepare_kernel(groups, *refs):
@@ -210,12 +242,12 @@
     results = refs[chips + 5 :]
     firsts, fews = zip(*[unfold(ref[...].astype(jnp.float32)) for ref in arrived])
     rows = jnp.concatenate([*firsts, *fews], axis=0).astype(jnp.bfloat16)
-    back = dot(rows, lower[...])
+    back = dot_by_columns(rows, lower)
     half = back.shape[1] // 2
     grads = jnp.concatenate([back, back], axis=1) * factors[...]
     hidden = []
     for entry in entries:
-        made = dot(rows, entry[0, 0])
+        made = dot_by_columns(rows, entry.at[0, 0])
         gate = made[:, :half]
         hidden.append(gate * jax.nn.sigmoid(gate) * made[:, half:])
     hidden = jnp.concatenate(hidden, axis=1)
@@ -305,7 +337,7 @@
     )
     rows_b = call(
         functools.partial(pick_kernel, groups),
-        shape((groups * LINES, width), bf16),
+        shape((groups, LINES, width * CAP // LINES), bf16),
         (asked, staged),
         8 * MIB,
         10_000_000_000,

time: 31.5 us -> 31.2 us (level)
  no operation moved by 1% of the time
where the time goes in v5:
time: 31.2 us; the launch traced here: 30.9 us
  starting transfers between devices  16.2 us (52%)
  Pallas kernels  8.16 us (26%)
  waiting for transfers between devices  5.92 us (19%)
  between operations  0.69 us (2%)
    ppermute x4, starting transfers between devices, along_sections(): return lax.ppermute(value, 'segment', pairs)  8.51 us
    pallas_call x8, Pallas kernels, call(): pl.pallas_call(body, out_shape=outs, in_specs=[anywhere] * waits + [dista...  8.16 us
    ppermute x9, starting transfers between devices, across_owners(): lax.ppermute(value, 'expert', [(source, source ^ flip) for source in rang...  7.66 us
    ppermute x9, waiting for transfers between devices, across_owners(): lax.ppermute(value, 'expert', [(source, source ^ flip) for source in rang...  4.1 us
    ppermute x4, waiting for transfers between devices, along_sections(): return lax.ppermute(value, 'segment', pairs)  1.82 us
  transfers between devices with their start and end apart: 13, of which 7 were waited for; matrix products, arithmetic and copies ran while one was open for 0% of the time, Pallas kernels for 23%

profile of v5, /device:TPU:0, one launch (start us, length us, event | category | flops | bytes accessed | tf_op | source)
XLA Modules:
  0.0 30.9 jit_solution(10569959376988648122)
XLA Ops:
  0.6 3.1 %collective-permute-start.1 = (s32[1,8,64]{2,1,0:T(8,128)}, s32[1,8,64]{2,1,0:T(8,128)S(1)}, u32[]{:S(2)}, u32[]{:S(2)}) collective-permute-start(s32[1,8,64]{2,1,0:T(8,128)} %bitcast.12), channel_id=1, source_target_pairs={{0,8},{8,16},{16,24},{24,0},{1,9},{9,17},{17,25},{25,1},{2,10},{10... | collective-permute-start | bytes 6152 | tf_op jit(solution)/shard_map/ppermute | solution.py:23
  3.7 1.6 %collective-permute-start = (bf16[1,64,2048]{2,1,0:T(8,128)(2,1)}, bf16[1,64,2048]{2,1,0:T(8,128)(2,1)S(1)}, u32[]{:S(2)}, u32[]{:S(2)}) collective-permute-start(bf16[1,64,2048]{2,1,0:T(8,128)(2,1)} %param.9), channel_id=1, source_target_pairs={{0,8},{8,16},{16,24},{24,0},{1,9},{9,17},{17,25},{25,1},{2,10},{10... | collective-permute-start | bytes 786440 | tf_op jit(solution)/shard_map/ppermute | solution.py:23
  5.3 0.0 collective-permute-start.2
  5.3 1.1 %shard_map.104 = (bf16[1,64,2048]{2,1,0:T(8,128)(2,1)S(1)}, bf16[8,64]{1,0:T(8,128)(2,1)S(1)}, bf16[64,48]{1,0:T(8,128)(2,1)S(1)}, bf16[64,48]{1,0:T(8,128)(2,1)S(1)}, f32[16,128]{1,0:T(8,128)S(1)}) custom-call(s32[1,8,64]{2,1,0:T(8,128)} %bitcast.9, f32[1,8,64]{2,1,0:T(8,128)} %bitcast.10, s32[1,8,64]{2,1,0:T(8,128)} %bitcast.13, f32[1,8,64]{2,1,0:T(8,128)} %bitcast.11, ...), custom_call_target="tpu_custom_call" | custom-call | flops 10000000 | bytes 1000000 | tf_op jit(solution)/shard_map/pallas_call | solution.py:40
  6.4 1.1 %collective-permute-done.1.refs_0_ = s32[1,8,64]{2,1,0:T(8,128)S(1)} collective-permute-done((s32[1,8,64]{2,1,0:T(8,128)}, s32[1,8,64]{2,1,0:T(8,128)S(1)}, u32[]{:S(2)}, u32[]{:S(2)}) %collective-permute-start.1) | collective-permute-done | bytes 2080 | tf_op jit(solution)/shard_map/ppermute | solution.py:23
  7.5 0.3 shard_map.105.refs_0_
  7.8 2.1 %collective-permute-start.3 = (bf16[1,8,1280]{2,1,0:T(8,128)(2,1)S(1)}, bf16[1,8,1280]{2,1,0:T(8,128)(2,1)S(1)}, u32[]{:S(2)}, u32[]{:S(2)}) collective-permute-start(bf16[1,8,1280]{2,1,0:T(8,128)(2,1)S(1)} %shard_map.105.refs_0_), channel_id=1, source_target_pairs={{0,24},{8,0},{16,8},{24,16},{1,25},{9,1},{17,9},{25,17},{2,26},{10... | collective-permute-start | bytes 61448 | tf_op jit(solution)/shard_map/ppermute | solution.py:23
  9.9 2.7 %shard_map.106 = (bf16[1,1,2048,384]{3,2,1,0:T(8,128)(2,1)S(1)}, bf16[1,1,192,2048]{3,2,1,0:T(8,128)(2,1)S(1)}, bf16[2048,384]{1,0:T(8,128)(2,1)S(1)}, bf16[1152,2048]{1,0:T(8,128)(2,1)S(1)}, f32[40,768]{1,0:T(8,128)S(1)}) custom-call(bf16[1,8,1280]{2,1,0:T(8,128)(2,1)S(1)} %shard_map.105.refs_0_, bf16[1,1,2048,384]{3,2,1,0:T(8,128)(2,1)} %refs_1_.1, ...), custom_call_target="tpu_custom_call" | custom-call | flops 10000000 | bytes 5000000 | tf_op jit(solution)/shard_map/pallas_call | solution.py:40
  12.7 0.1 collective-permute-start.4
  12.7 0.5 %collective-permute-start.5 = (bf16[1,1,192,2048]{3,2,1,0:T(8,128)(2,1)S(1)}, bf16[1,1,192,2048]{3,2,1,0:T(8,128)(2,1)S(1)}, u32[]{:S(2)}, u32[]{:S(2)}) collective-permute-start(bf16[1,1,192,2048]{3,2,1,0:T(8,128)(2,1)S(1)} %get-tuple-element.25), channel_id=1, source_target_pairs={{0,1},{1,0},{2,3},{3,2},{4,5},{5,4},{6,7},{7,6},{8,9},{9,8},{10,11... | collective-permute-start | bytes 2359304 | tf_op jit(solution)/shard_map/ppermute | solution.py:28
  13.2 0.7 %collective-permute-done.3.refs_6_ = bf16[1,8,1280]{2,1,0:T(8,128)(2,1)S(1)} collective-permute-done((bf16[1,8,1280]{2,1,0:T(8,128)(2,1)S(1)}, bf16[1,8,1280]{2,1,0:T(8,128)(2,1)S(1)}, u32[]{:S(2)}, u32[]{:S(2)}) %collective-permute-start.3) | collective-permute-done | bytes 20512 | tf_op jit(solution)/shard_map/ppermute | solution.py:23
  13.9 0.0 collective-permute-done.2.refs_3_
  13.9 0.0 collective-permute-done.refs_4_.refs_0_
  13.9 0.2 shard_map.107.refs_0_
  14.1 2.5 %collective-permute-start.9 = (bf16[8,2560]{1,0:T(8,128)(2,1)S(1)}, bf16[8,2560]{1,0:T(8,128)(2,1)S(1)}, u32[]{:S(2)}, u32[]{:S(2)}) collective-permute-start(bf16[8,2560]{1,0:T(8,128)(2,1)S(1)} %bitcast.5), channel_id=1, source_target_pairs={{0,6},{1,7},{2,4},{3,5},{4,2},{5,3},{6,0},{7,1},{8,14},{9,15},{10,... | collective-permute-start | bytes 122888 | tf_op jit(solution)/shard_map/ppermute | solution.py:28
  16.6 0.5 %collective-permute-start.7 = (bf16[8,2560]{1,0:T(8,128)(2,1)S(1)}, bf16[8,2560]{1,0:T(8,128)(2,1)S(1)}, u32[]{:S(2)}, u32[]{:S(2)}) collective-permute-start(bf16[8,2560]{1,0:T(8,128)(2,1)S(1)} %bitcast.6), channel_id=1, source_target_pairs={{0,2},{1,3},{2,0},{3,1},{4,6},{5,7},{6,4},{7,5},{8,10},{9,11},{10,... | collective-permute-start | bytes 122888 | tf_op jit(solution)/shard_map/ppermute | solution.py:28
  17.1 0.5 %collective-permute-start.8 = (bf16[8,2560]{1,0:T(8,128)(2,1)S(1)}, bf16[8,2560]{1,0:T(8,128)(2,1)S(1)}, u32[]{:S(2)}, u32[]{:S(2)}) collective-permute-start(bf16[8,2560]{1,0:T(8,128)(2,1)S(1)} %bitcast.7), channel_id=1, source_target_pairs={{0,4},{1,5},{2,6},{3,7},{4,0},{5,1},{6,2},{7,3},{8,12},{9,13},{10,... | collective-permute-start | bytes 122888 | tf_op jit(solution)/shard_map/ppermute | solution.py:28
  17.6 0.0 collective-permute-done.5.refs_2_
  17.6 0.0 collective-permute-done.4.refs_1_.refs_5_
  17.7 1.7 %collective-permute-start.6 = (bf16[1,64,2048]{2,1,0:T(8,128)(2,1)S(1)}, bf16[1,64,2048]{2,1,0:T(8,128)(2,1)S(1)}, u32[]{:S(2)}, u32[]{:S(2)}) collective-permute-start(bf16[1,64,2048]{2,1,0:T(8,128)(2,1)S(1)} %shard_map.108), channel_id=1, source_target_pairs={{0,24},{8,0},{16,8},{24,16},{1,25},{9,1},{17,9},{25,17},{2,26},{10... | collective-permute-start | bytes 786440 | tf_op jit(solution)/shard_map/ppermute | solution.py:23
  19.4 0.0 collective-permute-done.9.refs_0_.refs_3_
  19.4 1.1 %shard_map.109 = (bf16[2048,384]{1,0:T(8,128)(2,1)S(1)}, bf16[1152,2048]{1,0:T(8,128)(2,1)S(1)}, f32[40,768]{1,0:T(8,128)S(1)}) custom-call(bf16[8,2560]{1,0:T(8,128)(2,1)S(1)} %collective-permute-done.9.refs_0_.refs_3_, ...), custom_call_target="tpu_custom_call", output_to_operand_aliasing={{0}: (4, {}), {1}: (5, {}), {2}: (6, {})} | custom-call | flops 10000000000 | bytes 5000000 | tf_op jit(solution)/shard_map/pallas_call | solution.py:40
  20.5 0.1 collective-permute-done.7.refs_1_
  20.6 0.5 %collective-permute-done.8.refs_2_ = bf16[8,2560]{1,0:T(8,128)(2,1)S(1)} collective-permute-done((bf16[8,2560]{1,0:T(8,128)(2,1)S(1)}, bf16[8,2560]{1,0:T(8,128)(2,1)S(1)}, u32[]{:S(2)}, u32[]{:S(2)}) %collective-permute-start.8) | collective-permute-done | bytes 40992 | tf_op jit(solution)/shard_map/ppermute | solution.py:28
  21.1 1.7 %shard_map.110 = (bf16[8,2560]{1,0:T(8,128)(2,1)S(1)}, bf16[8,2560]{1,0:T(8,128)(2,1)S(1)}, bf16[8,2560]{1,0:T(8,128)(2,1)S(1)}, bf16[8,2560]{1,0:T(8,128)(2,1)S(1)}) custom-call(bf16[8,2560]{1,0:T(8,128)(2,1)S(1)} %bitcast.8, bf16[8,2560]{1,0:T(8,128)(2,1)S(1)} %collective-permute-done.7.refs_1_, bf16[8,2560]{1,0:T(8,128)(2,1)S(1)} %collective-permute-done.8.refs_2_, ...), custom_call_target="tpu_custom_call" | custom-call | flops 800000000 | bytes 5000000 | tf_op jit(solution)/shard_map/pallas_call | solution.py:40
  22.8 1.9 %collective-permute-start.10 = (bf16[8,2560]{1,0:T(8,128)(2,1)S(1)}, bf16[8,2560]{1,0:T(8,128)(2,1)S(1)}, u32[]{:S(2)}, u32[]{:S(2)}) collective-permute-start(bf16[8,2560]{1,0:T(8,128)(2,1)S(1)} %get-tuple-element.32), channel_id=1, source_target_pairs={{0,6},{1,7},{2,4},{3,5},{4,2},{5,3},{6,0},{7,1},{8,14},{9,15},{10,... | collective-permute-start | bytes 122888 | tf_op jit(solution)/shard_map/ppermute | solution.py:28
  24.8 1.1 %collective-permute-start.11 = (bf16[8,2560]{1,0:T(8,128)(2,1)S(1)}, bf16[8,2560]{1,0:T(8,128)(2,1)S(1)}, u32[]{:S(2)}, u32[]{:S(2)}) collective-permute-start(bf16[8,2560]{1,0:T(8,128)(2,1)S(1)} %get-tuple-element.33), channel_id=1, source_target_pairs={{0,4},{1,5},{2,6},{3,7},{4,0},{5,1},{6,2},{7,3},{8,12},{9,13},{10,... | collective-permute-start | bytes 122888 | tf_op jit(solution)/shard_map/ppermute | solution.py:28
  25.9 0.5 %collective-permute-start.12 = (bf16[8,2560]{1,0:T(8,128)(2,1)S(1)}, bf16[8,2560]{1,0:T(8,128)(2,1)S(1)}, u32[]{:S(2)}, u32[]{:S(2)}) collective-permute-start(bf16[8,2560]{1,0:T(8,128)(2,1)S(1)} %get-tuple-element.34), channel_id=1, source_target_pairs={{0,2},{1,3},{2,0},{3,1},{4,6},{5,7},{6,4},{7,5},{8,10},{9,11},{10,... | collective-permute-start | bytes 122888 | tf_op jit(solution)/shard_map/ppermute | solution.py:28
  26.4 1.4 %collective-permute-done.10.refs_5_ = bf16[8,2560]{1,0:T(8,128)(2,1)S(1)} collective-permute-done((bf16[8,2560]{1,0:T(8,128)(2,1)S(1)}, bf16[8,2560]{1,0:T(8,128)(2,1)S(1)}, u32[]{:S(2)}, u32[]{:S(2)}) %collective-permute-start.10) | collective-permute-done | bytes 40992 | tf_op jit(solution)/shard_map/ppermute | solution.py:28
  27.8 0.9 %collective-permute-done.11.refs_6_ = bf16[8,2560]{1,0:T(8,128)(2,1)S(1)} collective-permute-done((bf16[8,2560]{1,0:T(8,128)(2,1)S(1)}, bf16[8,2560]{1,0:T(8,128)(2,1)S(1)}, u32[]{:S(2)}, u32[]{:S(2)}) %collective-permute-start.11) | collective-permute-done | bytes 40992 | tf_op jit(solution)/shard_map/ppermute | solution.py:28
  28.8 1.1 %collective-permute-done.12.refs_7_ = bf16[8,2560]{1,0:T(8,128)(2,1)S(1)} collective-permute-done((bf16[8,2560]{1,0:T(8,128)(2,1)S(1)}, bf16[8,2560]{1,0:T(8,128)(2,1)S(1)}, u32[]{:S(2)}, u32[]{:S(2)}) %collective-permute-start.12) | collective-permute-done | bytes 40992 | tf_op jit(solution)/shard_map/ppermute | solution.py:28
  29.9 0.0 collective-permute-done.6.refs_1_
  29.9 1.1 %shard_map.111 = (bf16[1,64,2048]{2,1,0:T(8,128)(2,1)}, bf16[1,64,2048]{2,1,0:T(8,128)(2,1)}) custom-call(bf16[1,64,2048]{2,1,0:T(8,128)(2,1)S(1)} %collective-permute-done.refs_4_.refs_0_, bf16[1,64,2048]{2,1,0:T(8,128)(2,1)S(1)} %collective-permute-done.6.refs_1_, bf16[64,48]{1,0:T(8,128)(2,1)S(1)} %get-tuple-element.26.refs_2_, ...), custom_call_target="tpu_custom_call" | custom-call | flops 10000000 | bytes 1000000 | tf_op jit(solution)/shard_map/pallas_call | solution.py:40
  (1 shorter events, 0.0 us)
Async XLA Ops:
  0.6 6.9 %collective-permute-start.1 = (s32[1,8,64]{2,1,0:T(8,128)}, s32[1,8,64]{2,1,0:T(8,128)S(1)}, u32[]{:S(2)}, u32[]{:S(2)}) collective-permute-start(s32[1,8,64]{2,1,0:T(8,128)} %bitcast.12), channel_id=1, source_target_pairs={{0,8},{8,16},{16,24},{24,0},{1,9},{9,17},{17,25},{25,1},{2,10},{10... | collective-permute-start | bytes 6152 | tf_op jit(solution)/shard_map/ppermute | solution.py:23
  3.7 10.2 %collective-permute-start = (bf16[1,64,2048]{2,1,0:T(8,128)(2,1)}, bf16[1,64,2048]{2,1,0:T(8,128)(2,1)S(1)}, u32[]{:S(2)}, u32[]{:S(2)}) collective-permute-start(bf16[1,64,2048]{2,1,0:T(8,128)(2,1)} %param.9), channel_id=1, source_target_pairs={{0,8},{8,16},{16,24},{24,0},{1,9},{9,17},{17,25},{25,1},{2,10},{10... | collective-permute-start | bytes 786440 | tf_op jit(solution)/shard_map/ppermute | solution.py:23
  5.3 8.6 %collective-permute-start.2 = (bf16[1,1,40,384]{3,2,1,0:T(8,128)(2,1)}, bf16[1,1,40,384]{3,2,1,0:T(8,128)(2,1)S(1)}, u32[]{:S(2)}, u32[]{:S(2)}) collective-permute-start(bf16[1,1,40,384]{3,2,1,0:T(8,128)(2,1)} %refs_3_.1), channel_id=1, source_target_pairs={{0,1},{1,0},{2,3},{3,2},{4,5},{5,4},{6,7},{7,6},{8,9},{9,8},{10,11... | collective-permute-start | bytes 92168 | tf_op jit(solution)/shard_map/ppermute | solution.py:28
  7.8 6.1 %collective-permute-start.3 = (bf16[1,8,1280]{2,1,0:T(8,128)(2,1)S(1)}, bf16[1,8,1280]{2,1,0:T(8,128)(2,1)S(1)}, u32[]{:S(2)}, u32[]{:S(2)}) collective-permute-start(bf16[1,8,1280]{2,1,0:T(8,128)(2,1)S(1)} %shard_map.105.refs_0_), channel_id=1, source_target_pairs={{0,24},{8,0},{16,8},{24,16},{1,25},{9,1},{17,9},{25,17},{2,26},{10... | collective-permute-start | bytes 61448 | tf_op jit(solution)/shard_map/ppermute | solution.py:23
  12.7 5.0 %collective-permute-start.4 = (bf16[1,1,2048,384]{3,2,1,0:T(8,128)(2,1)S(1)}, bf16[1,1,2048,384]{3,2,1,0:T(8,128)(2,1)S(1)}, u32[]{:S(2)}, u32[]{:S(2)}) collective-permute-start(bf16[1,1,2048,384]{3,2,1,0:T(8,128)(2,1)S(1)} %get-tuple-element.24.refs_4_), channel_id=1, source_target_pairs={{0,1},{1,0},{2,3},{3,2},{4,5},{5,4},{6,7},{7,6},{8,9},{9,8},{10,11... | collective-permute-start | bytes 4718600 | tf_op jit(solution)/shard_map/ppermute | solution.py:28
  12.7 4.9 %collective-permute-start.5 = (bf16[1,1,192,2048]{3,2,1,0:T(8,128)(2,1)S(1)}, bf16[1,1,192,2048]{3,2,1,0:T(8,128)(2,1)S(1)}, u32[]{:S(2)}, u32[]{:S(2)}) collective-permute-start(bf16[1,1,192,2048]{3,2,1,0:T(8,128)(2,1)S(1)} %get-tuple-element.25), channel_id=1, source_target_pairs={{0,1},{1,0},{2,3},{3,2},{4,5},{5,4},{6,7},{7,6},{8,9},{9,8},{10,11... | collective-permute-start | bytes 2359304 | tf_op jit(solution)/shard_map/ppermute | solution.py:28
  14.1 5.3 %collective-permute-start.9 = (bf16[8,2560]{1,0:T(8,128)(2,1)S(1)}, bf16[8,2560]{1,0:T(8,128)(2,1)S(1)}, u32[]{:S(2)}, u32[]{:S(2)}) collective-permute-start(bf16[8,2560]{1,0:T(8,128)(2,1)S(1)} %bitcast.5), channel_id=1, source_target_pairs={{0,6},{1,7},{2,4},{3,5},{4,2},{5,3},{6,0},{7,1},{8,14},{9,15},{10,... | collective-permute-start | bytes 122888 | tf_op jit(solution)/shard_map/ppermute | solution.py:28
  16.6 4.0 %collective-permute-start.7 = (bf16[8,2560]{1,0:T(8,128)(2,1)S(1)}, bf16[8,2560]{1,0:T(8,128)(2,1)S(1)}, u32[]{:S(2)}, u32[]{:S(2)}) collective-permute-start(bf16[8,2560]{1,0:T(8,128)(2,1)S(1)} %bitcast.6), channel_id=1, source_target_pairs={{0,2},{1,3},{2,0},{3,1},{4,6},{5,7},{6,4},{7,5},{8,10},{9,11},{10,... | collective-permute-start | bytes 122888 | tf_op jit(solution)/shard_map/ppermute | solution.py:28
  17.1 4.0 %collective-permute-start.8 = (bf16[8,2560]{1,0:T(8,128)(2,1)S(1)}, bf16[8,2560]{1,0:T(8,128)(2,1)S(1)}, u32[]{:S(2)}, u32[]{:S(2)}) collective-permute-start(bf16[8,2560]{1,0:T(8,128)(2,1)S(1)} %bitcast.7), channel_id=1, source_target_pairs={{0,4},{1,5},{2,6},{3,7},{4,0},{5,1},{6,2},{7,3},{8,12},{9,13},{10,... | collective-permute-start | bytes 122888 | tf_op jit(solution)/shard_map/ppermute | solution.py:28
  17.7 12.2 %collective-permute-start.6 = (bf16[1,64,2048]{2,1,0:T(8,128)(2,1)S(1)}, bf16[1,64,2048]{2,1,0:T(8,128)(2,1)S(1)}, u32[]{:S(2)}, u32[]{:S(2)}) collective-permute-start(bf16[1,64,2048]{2,1,0:T(8,128)(2,1)S(1)} %shard_map.108), channel_id=1, source_target_pairs={{0,24},{8,0},{16,8},{24,16},{1,25},{9,1},{17,9},{25,17},{2,26},{10... | collective-permute-start | bytes 786440 | tf_op jit(solution)/shard_map/ppermute | solution.py:23
  22.8 5.0 %collective-permute-start.10 = (bf16[8,2560]{1,0:T(8,128)(2,1)S(1)}, bf16[8,2560]{1,0:T(8,128)(2,1)S(1)}, u32[]{:S(2)}, u32[]{:S(2)}) collective-permute-start(bf16[8,2560]{1,0:T(8,128)(2,1)S(1)} %get-tuple-element.32), channel_id=1, source_target_pairs={{0,6},{1,7},{2,4},{3,5},{4,2},{5,3},{6,0},{7,1},{8,14},{9,15},{10,... | collective-permute-start | bytes 122888 | tf_op jit(solution)/shard_map/ppermute | solution.py:28
  24.8 4.0 %collective-permute-start.11 = (bf16[8,2560]{1,0:T(8,128)(2,1)S(1)}, bf16[8,2560]{1,0:T(8,128)(2,1)S(1)}, u32[]{:S(2)}, u32[]{:S(2)}) collective-permute-start(bf16[8,2560]{1,0:T(8,128)(2,1)S(1)} %get-tuple-element.33), channel_id=1, source_target_pairs={{0,4},{1,5},{2,6},{3,7},{4,0},{5,1},{6,2},{7,3},{8,12},{9,13},{10,... | collective-permute-start | bytes 122888 | tf_op jit(solution)/shard_map/ppermute | solution.py:28
  25.9 4.0 %collective-permute-start.12 = (bf16[8,2560]{1,0:T(8,128)(2,1)S(1)}, bf16[8,2560]{1,0:T(8,128)(2,1)S(1)}, u32[]{:S(2)}, u32[]{:S(2)}) collective-permute-start(bf16[8,2560]{1,0:T(8,128)(2,1)S(1)} %get-tuple-element.34), channel_id=1, source_target_pairs={{0,2},{1,3},{2,0},{3,1},{4,6},{5,7},{6,4},{7,5},{8,10},{9,11},{10,... | collective-permute-start | bytes 122888 | tf_op jit(solution)/shard_map/ppermute | solution.py:28

commit v6 on v5

--- a/solution.py
+++ b/solution.py
@@ -33,6 +33,11 @@
     anywhere = pl.BlockSpec(memory_space=pl.ANY)
     distant = pl.BlockSpec(memory_space=pltpu.HBM)
     waits = len(after)
+    aliases = aliases or {}
+    args = [
+        pltpu.with_memory_space_constraint(value, pltpu.VMEM) if index in aliases else value
+        for index, value in enumerate(args)
+    ]
 
     def body(*refs):
         kernel(*refs[waits:])
@@ -44,7 +49,7 @@
         out_specs=jax.tree.map(lambda _: whole, outs),
         scratch_shapes=scratch,
         input_output_aliases={
-            waits + len(far) + key: value for key, value in (aliases or {}).items()
+            waits + len(far) + key: value for key, value in aliases.items()
         },
         compiler_params=pltpu.CompilerParams(vmem_limit_bytes=limit),
         cost_estimate=pl.CostEstimate(flops=flops, bytes_accessed=moved, transcendentals=0),
@@ -236,7 +241,7 @@
 
 
 def expert_kernel(chips, *refs):
-    arrived = refs[:chips]
+    arrived = [refs[0], *refs[chips - 1 : 0 : -1]]
     entries = refs[chips : chips + 2]
     lower, second, factors = refs[chips + 2 : chips + 5]
     results = refs[chips + 5 :]
@@ -400,13 +405,13 @@
         8 * MIB,
         10_000_000_000,
         5_000_000,
-        after=(arrived[-1],),
+        after=(arrived[2],),
         aliases={3: 0, 4: 1, 5: 2},
     )
     results = call(
         functools.partial(expert_kernel, chips),
         (shape(folded, bf16),) * chips,
-        (*arrived, entry_own, weights[0], *packed),
+        (arrived[0], *arrived[:0:-1], entry_own, weights[0], *packed),
         16 * MIB,
         800_000_000,
         5_000_000,

time: 31.2 us -> 30.6 us (0.981)
  waiting for transfers between devices: 5.92 us -> 5.36 us
    ppermute x9, waiting for transfers between devices: 4.1 us -> 3.54 us  [across_owners(): lax.ppermute(value, 'expert', [(source, source ^ flip) for source in rang...]
where the time goes in v6:
time: 30.6 us; the launch traced here: 30.4 us
  starting transfers between devices  16.2 us (53%)
  Pallas kernels  8.17 us (27%)
  waiting for transfers between devices  5.36 us (18%)
  between operations  0.69 us (2%)
    ppermute x4, starting transfers between devices, along_sections(): return lax.ppermute(value, 'segment', pairs)  8.51 us
    pallas_call x8, Pallas kernels, call(): pl.pallas_call(body, out_shape=outs, in_specs=[anywhere] * waits + [dista...  8.17 us
    ppermute x9, starting transfers between devices, across_owners(): lax.ppermute(value, 'expert', [(source, source ^ flip) for source in rang...  7.66 us
    ppermute x9, waiting for transfers between devices, across_owners(): lax.ppermute(value, 'expert', [(source, source ^ flip) for source in rang...  3.54 us
    ppermute x4, waiting for transfers between devices, along_sections(): return lax.ppermute(value, 'segment', pairs)  1.82 us
  transfers between devices with their start and end apart: 13, of which 7 were waited for; matrix products, arithmetic and copies ran while one was open for 0% of the time, Pallas kernels for 23%

profile of v6, /device:TPU:0, one launch (start us, length us, event | category | flops | bytes accessed | tf_op | source)
XLA Modules:
  0.0 30.4 jit_solution(9246595607834214700)
XLA Ops:
  0.6 3.1 %collective-permute-start.1 = (s32[1,8,64]{2,1,0:T(8,128)}, s32[1,8,64]{2,1,0:T(8,128)S(1)}, u32[]{:S(2)}, u32[]{:S(2)}) collective-permute-start(s32[1,8,64]{2,1,0:T(8,128)} %bitcast.12), channel_id=1, source_target_pairs={{0,8},{8,16},{16,24},{24,0},{1,9},{9,17},{17,25},{25,1},{2,10},{10... | collective-permute-start | bytes 6152 | tf_op jit(solution)/shard_map/ppermute | solution.py:23
  3.7 1.6 %collective-permute-start = (bf16[1,64,2048]{2,1,0:T(8,128)(2,1)}, bf16[1,64,2048]{2,1,0:T(8,128)(2,1)S(1)}, u32[]{:S(2)}, u32[]{:S(2)}) collective-permute-start(bf16[1,64,2048]{2,1,0:T(8,128)(2,1)} %param.9), channel_id=1, source_target_pairs={{0,8},{8,16},{16,24},{24,0},{1,9},{9,17},{17,25},{25,1},{2,10},{10... | collective-permute-start | bytes 786440 | tf_op jit(solution)/shard_map/ppermute | solution.py:23
  5.3 0.0 collective-permute-start.2
  5.3 1.1 %shard_map.104 = (bf16[1,64,2048]{2,1,0:T(8,128)(2,1)S(1)}, bf16[8,64]{1,0:T(8,128)(2,1)S(1)}, bf16[64,48]{1,0:T(8,128)(2,1)S(1)}, bf16[64,48]{1,0:T(8,128)(2,1)S(1)}, f32[16,128]{1,0:T(8,128)S(1)}) custom-call(s32[1,8,64]{2,1,0:T(8,128)} %bitcast.9, f32[1,8,64]{2,1,0:T(8,128)} %bitcast.10, s32[1,8,64]{2,1,0:T(8,128)} %bitcast.13, f32[1,8,64]{2,1,0:T(8,128)} %bitcast.11, ...), custom_call_target="tpu_custom_call" | custom-call | flops 10000000 | bytes 1000000 | tf_op jit(solution)/shard_map/pallas_call | solution.py:45
  6.4 1.1 %collective-permute-done.1.refs_0_ = s32[1,8,64]{2,1,0:T(8,128)S(1)} collective-permute-done((s32[1,8,64]{2,1,0:T(8,128)}, s32[1,8,64]{2,1,0:T(8,128)S(1)}, u32[]{:S(2)}, u32[]{:S(2)}) %collective-permute-start.1) | collective-permute-done | bytes 2080 | tf_op jit(solution)/shard_map/ppermute | solution.py:23
  7.5 0.3 shard_map.105.refs_0_
  7.8 2.1 %collective-permute-start.3 = (bf16[1,8,1280]{2,1,0:T(8,128)(2,1)S(1)}, bf16[1,8,1280]{2,1,0:T(8,128)(2,1)S(1)}, u32[]{:S(2)}, u32[]{:S(2)}) collective-permute-start(bf16[1,8,1280]{2,1,0:T(8,128)(2,1)S(1)} %shard_map.105.refs_0_), channel_id=1, source_target_pairs={{0,24},{8,0},{16,8},{24,16},{1,25},{9,1},{17,9},{25,17},{2,26},{10... | collective-permute-start | bytes 61448 | tf_op jit(solution)/shard_map/ppermute | solution.py:23
  9.9 2.7 %shard_map.106 = (bf16[1,1,2048,384]{3,2,1,0:T(8,128)(2,1)S(1)}, bf16[1,1,192,2048]{3,2,1,0:T(8,128)(2,1)S(1)}, bf16[2048,384]{1,0:T(8,128)(2,1)S(1)}, bf16[1152,2048]{1,0:T(8,128)(2,1)S(1)}, f32[40,768]{1,0:T(8,128)S(1)}) custom-call(bf16[1,8,1280]{2,1,0:T(8,128)(2,1)S(1)} %shard_map.105.refs_0_, bf16[1,1,2048,384]{3,2,1,0:T(8,128)(2,1)} %refs_1_.1, ...), custom_call_target="tpu_custom_call" | custom-call | flops 10000000 | bytes 5000000 | tf_op jit(solution)/shard_map/pallas_call | solution.py:45
  12.7 0.1 collective-permute-start.4
  12.7 0.5 %collective-permute-start.5 = (bf16[1,1,192,2048]{3,2,1,0:T(8,128)(2,1)S(1)}, bf16[1,1,192,2048]{3,2,1,0:T(8,128)(2,1)S(1)}, u32[]{:S(2)}, u32[]{:S(2)}) collective-permute-start(bf16[1,1,192,2048]{3,2,1,0:T(8,128)(2,1)S(1)} %get-tuple-element.25), channel_id=1, source_target_pairs={{0,1},{1,0},{2,3},{3,2},{4,5},{5,4},{6,7},{7,6},{8,9},{9,8},{10,11... | collective-permute-start | bytes 2359304 | tf_op jit(solution)/shard_map/ppermute | solution.py:28
  13.2 0.7 %collective-permute-done.3.refs_6_ = bf16[1,8,1280]{2,1,0:T(8,128)(2,1)S(1)} collective-permute-done((bf16[1,8,1280]{2,1,0:T(8,128)(2,1)S(1)}, bf16[1,8,1280]{2,1,0:T(8,128)(2,1)S(1)}, u32[]{:S(2)}, u32[]{:S(2)}) %collective-permute-start.3) | collective-permute-done | bytes 20512 | tf_op jit(solution)/shard_map/ppermute | solution.py:23
  13.9 0.0 collective-permute-done.2.refs_3_
  13.9 0.0 collective-permute-done.refs_4_.refs_0_
  13.9 0.2 shard_map.107.refs_0_
  14.1 1.6 %collective-permute-start.8 = (bf16[8,2560]{1,0:T(8,128)(2,1)S(1)}, bf16[8,2560]{1,0:T(8,128)(2,1)S(1)}, u32[]{:S(2)}, u32[]{:S(2)}) collective-permute-start(bf16[8,2560]{1,0:T(8,128)(2,1)S(1)} %bitcast.5), channel_id=1, source_target_pairs={{0,4},{1,5},{2,6},{3,7},{4,0},{5,1},{6,2},{7,3},{8,12},{9,13},{10,... | collective-permute-start | bytes 122888 | tf_op jit(solution)/shard_map/ppermute | solution.py:28
  15.7 1.4 %collective-permute-start.7 = (bf16[8,2560]{1,0:T(8,128)(2,1)S(1)}, bf16[8,2560]{1,0:T(8,128)(2,1)S(1)}, u32[]{:S(2)}, u32[]{:S(2)}) collective-permute-start(bf16[8,2560]{1,0:T(8,128)(2,1)S(1)} %bitcast.6), channel_id=1, source_target_pairs={{0,6},{1,7},{2,4},{3,5},{4,2},{5,3},{6,0},{7,1},{8,14},{9,15},{10,... | collective-permute-start | bytes 122888 | tf_op jit(solution)/shard_map/ppermute | solution.py:28
  17.1 0.5 %collective-permute-start.9 = (bf16[8,2560]{1,0:T(8,128)(2,1)S(1)}, bf16[8,2560]{1,0:T(8,128)(2,1)S(1)}, u32[]{:S(2)}, u32[]{:S(2)}) collective-permute-start(bf16[8,2560]{1,0:T(8,128)(2,1)S(1)} %bitcast.7), channel_id=1, source_target_pairs={{0,2},{1,3},{2,0},{3,1},{4,6},{5,7},{6,4},{7,5},{8,10},{9,11},{10,... | collective-permute-start | bytes 122888 | tf_op jit(solution)/shard_map/ppermute | solution.py:28
  17.6 0.0 collective-permute-done.5.refs_2_
  17.6 0.0 collective-permute-done.4.refs_1_.refs_5_
  17.7 1.7 %collective-permute-start.6 = (bf16[1,64,2048]{2,1,0:T(8,128)(2,1)S(1)}, bf16[1,64,2048]{2,1,0:T(8,128)(2,1)S(1)}, u32[]{:S(2)}, u32[]{:S(2)}) collective-permute-start(bf16[1,64,2048]{2,1,0:T(8,128)(2,1)S(1)} %shard_map.108), channel_id=1, source_target_pairs={{0,24},{8,0},{16,8},{24,16},{1,25},{9,1},{17,9},{25,17},{2,26},{10... | collective-permute-start | bytes 786440 | tf_op jit(solution)/shard_map/ppermute | solution.py:23
  19.4 0.0 collective-permute-done.8.refs_0_.refs_2_
  19.4 1.1 %shard_map.109 = (bf16[2048,384]{1,0:T(8,128)(2,1)S(1)}, bf16[1152,2048]{1,0:T(8,128)(2,1)S(1)}, f32[40,768]{1,0:T(8,128)S(1)}) custom-call(bf16[8,2560]{1,0:T(8,128)(2,1)S(1)} %collective-permute-done.8.refs_0_.refs_2_, ...), custom_call_target="tpu_custom_call", output_to_operand_aliasing={{0}: (4, {}), {1}: (5, {}), {2}: (6, {})} | custom-call | flops 10000000000 | bytes 5000000 | tf_op jit(solution)/shard_map/pallas_call | solution.py:45
  20.5 0.1 collective-permute-done.7.refs_1_
  20.6 0.5 %collective-permute-done.9.refs_3_ = bf16[8,2560]{1,0:T(8,128)(2,1)S(1)} collective-permute-done((bf16[8,2560]{1,0:T(8,128)(2,1)S(1)}, bf16[8,2560]{1,0:T(8,128)(2,1)S(1)}, u32[]{:S(2)}, u32[]{:S(2)}) %collective-permute-start.9) | collective-permute-done | bytes 40992 | tf_op jit(solution)/shard_map/ppermute | solution.py:28
  21.1 1.7 %shard_map.110 = (bf16[8,2560]{1,0:T(8,128)(2,1)S(1)}, bf16[8,2560]{1,0:T(8,128)(2,1)S(1)}, bf16[8,2560]{1,0:T(8,128)(2,1)S(1)}, bf16[8,2560]{1,0:T(8,128)(2,1)S(1)}) custom-call(bf16[8,2560]{1,0:T(8,128)(2,1)S(1)} %bitcast.8, bf16[8,2560]{1,0:T(8,128)(2,1)S(1)} %collective-permute-done.7.refs_1_, ...), custom_call_target="tpu_custom_call" | custom-call | flops 800000000 | bytes 5000000 | tf_op jit(solution)/shard_map/pallas_call | solution.py:45
  22.8 1.9 %collective-permute-start.10 = (bf16[8,2560]{1,0:T(8,128)(2,1)S(1)}, bf16[8,2560]{1,0:T(8,128)(2,1)S(1)}, u32[]{:S(2)}, u32[]{:S(2)}) collective-permute-start(bf16[8,2560]{1,0:T(8,128)(2,1)S(1)} %get-tuple-element.32), channel_id=1, source_target_pairs={{0,6},{1,7},{2,4},{3,5},{4,2},{5,3},{6,0},{7,1},{8,14},{9,15},{10,... | collective-permute-start | bytes 122888 | tf_op jit(solution)/shard_map/ppermute | solution.py:28
  24.8 0.5 %collective-permute-start.11 = (bf16[8,2560]{1,0:T(8,128)(2,1)S(1)}, bf16[8,2560]{1,0:T(8,128)(2,1)S(1)}, u32[]{:S(2)}, u32[]{:S(2)}) collective-permute-start(bf16[8,2560]{1,0:T(8,128)(2,1)S(1)} %get-tuple-element.33), channel_id=1, source_target_pairs={{0,4},{1,5},{2,6},{3,7},{4,0},{5,1},{6,2},{7,3},{8,12},{9,13},{10,... | collective-permute-start | bytes 122888 | tf_op jit(solution)/shard_map/ppermute | solution.py:28
  25.3 1.1 %collective-permute-start.12 = (bf16[8,2560]{1,0:T(8,128)(2,1)S(1)}, bf16[8,2560]{1,0:T(8,128)(2,1)S(1)}, u32[]{:S(2)}, u32[]{:S(2)}) collective-permute-start(bf16[8,2560]{1,0:T(8,128)(2,1)S(1)} %get-tuple-element.34), channel_id=1, source_target_pairs={{0,2},{1,3},{2,0},{3,1},{4,6},{5,7},{6,4},{7,5},{8,10},{9,11},{10,... | collective-permute-start | bytes 122888 | tf_op jit(solution)/shard_map/ppermute | solution.py:28
  26.4 1.4 %collective-permute-done.10.refs_5_ = bf16[8,2560]{1,0:T(8,128)(2,1)S(1)} collective-permute-done((bf16[8,2560]{1,0:T(8,128)(2,1)S(1)}, bf16[8,2560]{1,0:T(8,128)(2,1)S(1)}, u32[]{:S(2)}, u32[]{:S(2)}) %collective-permute-start.10) | collective-permute-done | bytes 40992 | tf_op jit(solution)/shard_map/ppermute | solution.py:28
  27.8 1.0 %collective-permute-done.11.refs_6_ = bf16[8,2560]{1,0:T(8,128)(2,1)S(1)} collective-permute-done((bf16[8,2560]{1,0:T(8,128)(2,1)S(1)}, bf16[8,2560]{1,0:T(8,128)(2,1)S(1)}, u32[]{:S(2)}, u32[]{:S(2)}) %collective-permute-start.11) | collective-permute-done | bytes 40992 | tf_op jit(solution)/shard_map/ppermute | solution.py:28
  28.8 0.5 %collective-permute-done.12.refs_7_ = bf16[8,2560]{1,0:T(8,128)(2,1)S(1)} collective-permute-done((bf16[8,2560]{1,0:T(8,128)(2,1)S(1)}, bf16[8,2560]{1,0:T(8,128)(2,1)S(1)}, u32[]{:S(2)}, u32[]{:S(2)}) %collective-permute-start.12) | collective-permute-done | bytes 40992 | tf_op jit(solution)/shard_map/ppermute | solution.py:28
  29.3 0.0 collective-permute-done.6.refs_1_
  29.3 1.1 %shard_map.111 = (bf16[1,64,2048]{2,1,0:T(8,128)(2,1)}, bf16[1,64,2048]{2,1,0:T(8,128)(2,1)}) custom-call(bf16[1,64,2048]{2,1,0:T(8,128)(2,1)S(1)} %collective-permute-done.refs_4_.refs_0_, bf16[1,64,2048]{2,1,0:T(8,128)(2,1)S(1)} %collective-permute-done.6.refs_1_, bf16[64,48]{1,0:T(8,128)(2,1)S(1)} %get-tuple-element.26.refs_2_, ...), custom_call_target="tpu_custom_call" | custom-call | flops 10000000 | bytes 1000000 | tf_op jit(solution)/shard_map/pallas_call | solution.py:45
  (1 shorter events, 0.0 us)
Async XLA Ops:
  0.6 6.9 %collective-permute-start.1 = (s32[1,8,64]{2,1,0:T(8,128)}, s32[1,8,64]{2,1,0:T(8,128)S(1)}, u32[]{:S(2)}, u32[]{:S(2)}) collective-permute-start(s32[1,8,64]{2,1,0:T(8,128)} %bitcast.12), channel_id=1, source_target_pairs={{0,8},{8,16},{16,24},{24,0},{1,9},{9,17},{17,25},{25,1},{2,10},{10... | collective-permute-start | bytes 6152 | tf_op jit(solution)/shard_map/ppermute | solution.py:23
  3.7 10.2 %collective-permute-start = (bf16[1,64,2048]{2,1,0:T(8,128)(2,1)}, bf16[1,64,2048]{2,1,0:T(8,128)(2,1)S(1)}, u32[]{:S(2)}, u32[]{:S(2)}) collective-permute-start(bf16[1,64,2048]{2,1,0:T(8,128)(2,1)} %param.9), channel_id=1, source_target_pairs={{0,8},{8,16},{16,24},{24,0},{1,9},{9,17},{17,25},{25,1},{2,10},{10... | collective-permute-start | bytes 786440 | tf_op jit(solution)/shard_map/ppermute | solution.py:23
  5.3 8.6 %collective-permute-start.2 = (bf16[1,1,40,384]{3,2,1,0:T(8,128)(2,1)}, bf16[1,1,40,384]{3,2,1,0:T(8,128)(2,1)S(1)}, u32[]{:S(2)}, u32[]{:S(2)}) collective-permute-start(bf16[1,1,40,384]{3,2,1,0:T(8,128)(2,1)} %refs_3_.1), channel_id=1, source_target_pairs={{0,1},{1,0},{2,3},{3,2},{4,5},{5,4},{6,7},{7,6},{8,9},{9,8},{10,11... | collective-permute-start | bytes 92168 | tf_op jit(solution)/shard_map/ppermute | solution.py:28
  7.8 6.1 %collective-permute-start.3 = (bf16[1,8,1280]{2,1,0:T(8,128)(2,1)S(1)}, bf16[1,8,1280]{2,1,0:T(8,128)(2,1)S(1)}, u32[]{:S(2)}, u32[]{:S(2)}) collective-permute-start(bf16[1,8,1280]{2,1,0:T(8,128)(2,1)S(1)} %shard_map.105.refs_0_), channel_id=1, source_target_pairs={{0,24},{8,0},{16,8},{24,16},{1,25},{9,1},{17,9},{25,17},{2,26},{10... | collective-permute-start | bytes 61448 | tf_op jit(solution)/shard_map/ppermute | solution.py:23
  12.7 5.0 %collective-permute-start.4 = (bf16[1,1,2048,384]{3,2,1,0:T(8,128)(2,1)S(1)}, bf16[1,1,2048,384]{3,2,1,0:T(8,128)(2,1)S(1)}, u32[]{:S(2)}, u32[]{:S(2)}) collective-permute-start(bf16[1,1,2048,384]{3,2,1,0:T(8,128)(2,1)S(1)} %get-tuple-element.24.refs_4_), channel_id=1, source_target_pairs={{0,1},{1,0},{2,3},{3,2},{4,5},{5,4},{6,7},{7,6},{8,9},{9,8},{10,11... | collective-permute-start | bytes 4718600 | tf_op jit(solution)/shard_map/ppermute | solution.py:28
  12.7 4.9 %collective-permute-start.5 = (bf16[1,1,192,2048]{3,2,1,0:T(8,128)(2,1)S(1)}, bf16[1,1,192,2048]{3,2,1,0:T(8,128)(2,1)S(1)}, u32[]{:S(2)}, u32[]{:S(2)}) collective-permute-start(bf16[1,1,192,2048]{3,2,1,0:T(8,128)(2,1)S(1)} %get-tuple-element.25), channel_id=1, source_target_pairs={{0,1},{1,0},{2,3},{3,2},{4,5},{5,4},{6,7},{7,6},{8,9},{9,8},{10,11... | collective-permute-start | bytes 2359304 | tf_op jit(solution)/shard_map/ppermute | solution.py:28
  14.1 5.3 %collective-permute-start.8 = (bf16[8,2560]{1,0:T(8,128)(2,1)S(1)}, bf16[8,2560]{1,0:T(8,128)(2,1)S(1)}, u32[]{:S(2)}, u32[]{:S(2)}) collective-permute-start(bf16[8,2560]{1,0:T(8,128)(2,1)S(1)} %bitcast.5), channel_id=1, source_target_pairs={{0,4},{1,5},{2,6},{3,7},{4,0},{5,1},{6,2},{7,3},{8,12},{9,13},{10,... | collective-permute-start | bytes 122888 | tf_op jit(solution)/shard_map/ppermute | solution.py:28
  15.7 4.9 %collective-permute-start.7 = (bf16[8,2560]{1,0:T(8,128)(2,1)S(1)}, bf16[8,2560]{1,0:T(8,128)(2,1)S(1)}, u32[]{:S(2)}, u32[]{:S(2)}) collective-permute-start(bf16[8,2560]{1,0:T(8,128)(2,1)S(1)} %bitcast.6), channel_id=1, source_target_pairs={{0,6},{1,7},{2,4},{3,5},{4,2},{5,3},{6,0},{7,1},{8,14},{9,15},{10,... | collective-permute-start | bytes 122888 | tf_op jit(solution)/shard_map/ppermute | solution.py:28
  17.1 4.0 %collective-permute-start.9 = (bf16[8,2560]{1,0:T(8,128)(2,1)S(1)}, bf16[8,2560]{1,0:T(8,128)(2,1)S(1)}, u32[]{:S(2)}, u32[]{:S(2)}) collective-permute-start(bf16[8,2560]{1,0:T(8,128)(2,1)S(1)} %bitcast.7), channel_id=1, source_target_pairs={{0,2},{1,3},{2,0},{3,1},{4,6},{5,7},{6,4},{7,5},{8,10},{9,11},{10,... | collective-permute-start | bytes 122888 | tf_op jit(solution)/shard_map/ppermute | solution.py:28
  17.7 11.7 %collective-permute-start.6 = (bf16[1,64,2048]{2,1,0:T(8,128)(2,1)S(1)}, bf16[1,64,2048]{2,1,0:T(8,128)(2,1)S(1)}, u32[]{:S(2)}, u32[]{:S(2)}) collective-permute-start(bf16[1,64,2048]{2,1,0:T(8,128)(2,1)S(1)} %shard_map.108), channel_id=1, source_target_pairs={{0,24},{8,0},{16,8},{24,16},{1,25},{9,1},{17,9},{25,17},{2,26},{10... | collective-permute-start | bytes 786440 | tf_op jit(solution)/shard_map/ppermute | solution.py:23
  22.8 5.0 %collective-permute-start.10 = (bf16[8,2560]{1,0:T(8,128)(2,1)S(1)}, bf16[8,2560]{1,0:T(8,128)(2,1)S(1)}, u32[]{:S(2)}, u32[]{:S(2)}) collective-permute-start(bf16[8,2560]{1,0:T(8,128)(2,1)S(1)} %get-tuple-element.32), channel_id=1, source_target_pairs={{0,6},{1,7},{2,4},{3,5},{4,2},{5,3},{6,0},{7,1},{8,14},{9,15},{10,... | collective-permute-start | bytes 122888 | tf_op jit(solution)/shard_map/ppermute | solution.py:28
  24.8 4.0 %collective-permute-start.11 = (bf16[8,2560]{1,0:T(8,128)(2,1)S(1)}, bf16[8,2560]{1,0:T(8,128)(2,1)S(1)}, u32[]{:S(2)}, u32[]{:S(2)}) collective-permute-start(bf16[8,2560]{1,0:T(8,128)(2,1)S(1)} %get-tuple-element.33), channel_id=1, source_target_pairs={{0,4},{1,5},{2,6},{3,7},{4,0},{5,1},{6,2},{7,3},{8,12},{9,13},{10,... | collective-permute-start | bytes 122888 | tf_op jit(solution)/shard_map/ppermute | solution.py:28
  25.3 4.0 %collective-permute-start.12 = (bf16[8,2560]{1,0:T(8,128)(2,1)S(1)}, bf16[8,2560]{1,0:T(8,128)(2,1)S(1)}, u32[]{:S(2)}, u32[]{:S(2)}) collective-permute-start(bf16[8,2560]{1,0:T(8,128)(2,1)S(1)} %get-tuple-element.34), channel_id=1, source_target_pairs={{0,2},{1,3},{2,0},{3,1},{4,6},{5,7},{6,4},{7,5},{8,10},{9,11},{10,... | collective-permute-start | bytes 122888 | tf_op jit(solution)/shard_map/ppermute | solution.py:28

commit v7 on v6

--- a/solution.py
+++ b/solution.py
@@ -60,9 +60,9 @@
     return jnp.dot(left, right, preferred_element_type=jnp.float32)
 
 
-def dot_by_columns(left, right):
-    spans = range(0, right.shape[1], 128)
-    return jnp.concatenate([dot(left, right[:, start : start + 128]) for start in spans], axis=1)
+def dot_by_columns(left, right, step):
+    spans = range(0, right.shape[1], step)
+    return jnp.concatenate([dot(left, right[:, start : start + step]) for start in spans], axis=1)
 
 
 def hits(routes, group):
@@ -247,19 +247,19 @@
     results = refs[chips + 5 :]
     firsts, fews = zip(*[unfold(ref[...].astype(jnp.float32)) for ref in arrived])
     rows = jnp.concatenate([*firsts, *fews], axis=0).astype(jnp.bfloat16)
-    back = dot_by_columns(rows, lower)
+    back = dot_by_columns(rows, lower, 128)
     half = back.shape[1] // 2
     grads = jnp.concatenate([back, back], axis=1) * factors[...]
     hidden = []
     for entry in entries:
-        made = dot_by_columns(rows, entry.at[0, 0])
+        made = dot_by_columns(rows, entry.at[0, 0], 128)
         gate = made[:, :half]
         hidden.append(gate * jax.nn.sigmoid(gate) * made[:, half:])
     hidden = jnp.concatenate(hidden, axis=1)
     _, slot = lines_of(hidden.shape, chips)
     hidden = jnp.where(slot < 0, hidden, 0.0)
     inner = jnp.concatenate([grads.astype(jnp.bfloat16), hidden.astype(jnp.bfloat16)], axis=1)
-    total = dot(inner, second[...])
+    total = dot_by_columns(inner, second, 256)
     for index, ref in enumerate(results):
         late = chips * LINES + index * FEW
         first = total[index * LINES : (index + 1) * LINES]

time: 30.6 us -> 30.6 us (level)
  no operation moved by 1% of the time
where the time goes in v7:
time: 30.6 us; the launch traced here: 30.4 us
  starting transfers between devices  16.2 us (53%)
  Pallas kernels  8.17 us (27%)
  waiting for transfers between devices  5.36 us (18%)
  between operations  0.69 us (2%)
    ppermute x4, starting transfers between devices, along_sections(): return lax.ppermute(value, 'segment', pairs)  8.51 us
    pallas_call x8, Pallas kernels, call(): pl.pallas_call(body, out_shape=outs, in_specs=[anywhere] * waits + [dista...  8.17 us
    ppermute x9, starting transfers between devices, across_owners(): lax.ppermute(value, 'expert', [(source, source ^ flip) for source in rang...  7.66 us
    ppermute x9, waiting for transfers between devices, across_owners(): lax.ppermute(value, 'expert', [(source, source ^ flip) for source in rang...  3.54 us
    ppermute x4, waiting for transfers between devices, along_sections(): return lax.ppermute(value, 'segment', pairs)  1.82 us
  transfers between devices with their start and end apart: 13, of which 7 were waited for; matrix products, arithmetic and copies ran while one was open for 0% of the time, Pallas kernels for 23%

profile of v7, /device:TPU:0, one launch (start us, length us, event | category | flops | bytes accessed | tf_op | source)
XLA Modules:
  0.0 30.4 jit_solution(9246595607834214700)
XLA Ops:
  0.6 3.1 %collective-permute-start.1 = (s32[1,8,64]{2,1,0:T(8,128)}, s32[1,8,64]{2,1,0:T(8,128)S(1)}, u32[]{:S(2)}, u32[]{:S(2)}) collective-permute-start(s32[1,8,64]{2,1,0:T(8,128)} %bitcast.12), channel_id=1, source_target_pairs={{0,8},{8,16},{16,24},{24,0},{1,9},{9,17},{17,25},{25,1},{2,10},{10... | collective-permute-start | bytes 6152 | tf_op jit(solution)/shard_map/ppermute | solution.py:23
  3.7 1.6 %collective-permute-start = (bf16[1,64,2048]{2,1,0:T(8,128)(2,1)}, bf16[1,64,2048]{2,1,0:T(8,128)(2,1)S(1)}, u32[]{:S(2)}, u32[]{:S(2)}) collective-permute-start(bf16[1,64,2048]{2,1,0:T(8,128)(2,1)} %param.9), channel_id=1, source_target_pairs={{0,8},{8,16},{16,24},{24,0},{1,9},{9,17},{17,25},{25,1},{2,10},{10... | collective-permute-start | bytes 786440 | tf_op jit(solution)/shard_map/ppermute | solution.py:23
  5.3 0.0 collective-permute-start.2
  5.3 1.1 %shard_map.104 = (bf16[1,64,2048]{2,1,0:T(8,128)(2,1)S(1)}, bf16[8,64]{1,0:T(8,128)(2,1)S(1)}, bf16[64,48]{1,0:T(8,128)(2,1)S(1)}, bf16[64,48]{1,0:T(8,128)(2,1)S(1)}, f32[16,128]{1,0:T(8,128)S(1)}) custom-call(s32[1,8,64]{2,1,0:T(8,128)} %bitcast.9, f32[1,8,64]{2,1,0:T(8,128)} %bitcast.10, s32[1,8,64]{2,1,0:T(8,128)} %bitcast.13, f32[1,8,64]{2,1,0:T(8,128)} %bitcast.11, ...), custom_call_target="tpu_custom_call" | custom-call | flops 10000000 | bytes 1000000 | tf_op jit(solution)/shard_map/pallas_call | solution.py:45
  6.4 1.1 %collective-permute-done.1.refs_0_ = s32[1,8,64]{2,1,0:T(8,128)S(1)} collective-permute-done((s32[1,8,64]{2,1,0:T(8,128)}, s32[1,8,64]{2,1,0:T(8,128)S(1)}, u32[]{:S(2)}, u32[]{:S(2)}) %collective-permute-start.1) | collective-permute-done | bytes 2080 | tf_op jit(solution)/shard_map/ppermute | solution.py:23
  7.5 0.3 shard_map.105.refs_0_
  7.8 2.1 %collective-permute-start.3 = (bf16[1,8,1280]{2,1,0:T(8,128)(2,1)S(1)}, bf16[1,8,1280]{2,1,0:T(8,128)(2,1)S(1)}, u32[]{:S(2)}, u32[]{:S(2)}) collective-permute-start(bf16[1,8,1280]{2,1,0:T(8,128)(2,1)S(1)} %shard_map.105.refs_0_), channel_id=1, source_target_pairs={{0,24},{8,0},{16,8},{24,16},{1,25},{9,1},{17,9},{25,17},{2,26},{10... | collective-permute-start | bytes 61448 | tf_op jit(solution)/shard_map/ppermute | solution.py:23
  9.9 2.7 %shard_map.106 = (bf16[1,1,2048,384]{3,2,1,0:T(8,128)(2,1)S(1)}, bf16[1,1,192,2048]{3,2,1,0:T(8,128)(2,1)S(1)}, bf16[2048,384]{1,0:T(8,128)(2,1)S(1)}, bf16[1152,2048]{1,0:T(8,128)(2,1)S(1)}, f32[40,768]{1,0:T(8,128)S(1)}) custom-call(bf16[1,8,1280]{2,1,0:T(8,128)(2,1)S(1)} %shard_map.105.refs_0_, bf16[1,1,2048,384]{3,2,1,0:T(8,128)(2,1)} %refs_1_.1, ...), custom_call_target="tpu_custom_call" | custom-call | flops 10000000 | bytes 5000000 | tf_op jit(solution)/shard_map/pallas_call | solution.py:45
  12.7 0.1 collective-permute-start.4
  12.7 0.5 %collective-permute-start.5 = (bf16[1,1,192,2048]{3,2,1,0:T(8,128)(2,1)S(1)}, bf16[1,1,192,2048]{3,2,1,0:T(8,128)(2,1)S(1)}, u32[]{:S(2)}, u32[]{:S(2)}) collective-permute-start(bf16[1,1,192,2048]{3,2,1,0:T(8,128)(2,1)S(1)} %get-tuple-element.25), channel_id=1, source_target_pairs={{0,1},{1,0},{2,3},{3,2},{4,5},{5,4},{6,7},{7,6},{8,9},{9,8},{10,11... | collective-permute-start | bytes 2359304 | tf_op jit(solution)/shard_map/ppermute | solution.py:28
  13.2 0.7 %collective-permute-done.3.refs_6_ = bf16[1,8,1280]{2,1,0:T(8,128)(2,1)S(1)} collective-permute-done((bf16[1,8,1280]{2,1,0:T(8,128)(2,1)S(1)}, bf16[1,8,1280]{2,1,0:T(8,128)(2,1)S(1)}, u32[]{:S(2)}, u32[]{:S(2)}) %collective-permute-start.3) | collective-permute-done | bytes 20512 | tf_op jit(solution)/shard_map/ppermute | solution.py:23
  13.9 0.0 collective-permute-done.2.refs_3_
  13.9 0.0 collective-permute-done.refs_4_.refs_0_
  13.9 0.2 shard_map.107.refs_0_
  14.1 1.6 %collective-permute-start.8 = (bf16[8,2560]{1,0:T(8,128)(2,1)S(1)}, bf16[8,2560]{1,0:T(8,128)(2,1)S(1)}, u32[]{:S(2)}, u32[]{:S(2)}) collective-permute-start(bf16[8,2560]{1,0:T(8,128)(2,1)S(1)} %bitcast.5), channel_id=1, source_target_pairs={{0,4},{1,5},{2,6},{3,7},{4,0},{5,1},{6,2},{7,3},{8,12},{9,13},{10,... | collective-permute-start | bytes 122888 | tf_op jit(solution)/shard_map/ppermute | solution.py:28
  15.7 1.4 %collective-permute-start.7 = (bf16[8,2560]{1,0:T(8,128)(2,1)S(1)}, bf16[8,2560]{1,0:T(8,128)(2,1)S(1)}, u32[]{:S(2)}, u32[]{:S(2)}) collective-permute-start(bf16[8,2560]{1,0:T(8,128)(2,1)S(1)} %bitcast.6), channel_id=1, source_target_pairs={{0,6},{1,7},{2,4},{3,5},{4,2},{5,3},{6,0},{7,1},{8,14},{9,15},{10,... | collective-permute-start | bytes 122888 | tf_op jit(solution)/shard_map/ppermute | solution.py:28
  17.1 0.5 %collective-permute-start.9 = (bf16[8,2560]{1,0:T(8,128)(2,1)S(1)}, bf16[8,2560]{1,0:T(8,128)(2,1)S(1)}, u32[]{:S(2)}, u32[]{:S(2)}) collective-permute-start(bf16[8,2560]{1,0:T(8,128)(2,1)S(1)} %bitcast.7), channel_id=1, source_target_pairs={{0,2},{1,3},{2,0},{3,1},{4,6},{5,7},{6,4},{7,5},{8,10},{9,11},{10,... | collective-permute-start | bytes 122888 | tf_op jit(solution)/shard_map/ppermute | solution.py:28
  17.6 0.0 collective-permute-done.5.refs_2_
  17.6 0.0 collective-permute-done.4.refs_1_.refs_5_
  17.7 1.7 %collective-permute-start.6 = (bf16[1,64,2048]{2,1,0:T(8,128)(2,1)S(1)}, bf16[1,64,2048]{2,1,0:T(8,128)(2,1)S(1)}, u32[]{:S(2)}, u32[]{:S(2)}) collective-permute-start(bf16[1,64,2048]{2,1,0:T(8,128)(2,1)S(1)} %shard_map.108), channel_id=1, source_target_pairs={{0,24},{8,0},{16,8},{24,16},{1,25},{9,1},{17,9},{25,17},{2,26},{10... | collective-permute-start | bytes 786440 | tf_op jit(solution)/shard_map/ppermute | solution.py:23
  19.4 0.0 collective-permute-done.8.refs_0_.refs_2_
  19.4 1.1 %shard_map.109 = (bf16[2048,384]{1,0:T(8,128)(2,1)S(1)}, bf16[1152,2048]{1,0:T(8,128)(2,1)S(1)}, f32[40,768]{1,0:T(8,128)S(1)}) custom-call(bf16[8,2560]{1,0:T(8,128)(2,1)S(1)} %collective-permute-done.8.refs_0_.refs_2_, ...), custom_call_target="tpu_custom_call", output_to_operand_aliasing={{0}: (4, {}), {1}: (5, {}), {2}: (6, {})} | custom-call | flops 10000000000 | bytes 5000000 | tf_op jit(solution)/shard_map/pallas_call | solution.py:45
  20.5 0.1 collective-permute-done.7.refs_1_
  20.6 0.5 %collective-permute-done.9.refs_3_ = bf16[8,2560]{1,0:T(8,128)(2,1)S(1)} collective-permute-done((bf16[8,2560]{1,0:T(8,128)(2,1)S(1)}, bf16[8,2560]{1,0:T(8,128)(2,1)S(1)}, u32[]{:S(2)}, u32[]{:S(2)}) %collective-permute-start.9) | collective-permute-done | bytes 40992 | tf_op jit(solution)/shard_map/ppermute | solution.py:28
  21.1 1.7 %shard_map.110 = (bf16[8,2560]{1,0:T(8,128)(2,1)S(1)}, bf16[8,2560]{1,0:T(8,128)(2,1)S(1)}, bf16[8,2560]{1,0:T(8,128)(2,1)S(1)}, bf16[8,2560]{1,0:T(8,128)(2,1)S(1)}) custom-call(bf16[8,2560]{1,0:T(8,128)(2,1)S(1)} %bitcast.8, bf16[8,2560]{1,0:T(8,128)(2,1)S(1)} %collective-permute-done.7.refs_1_, ...), custom_call_target="tpu_custom_call" | custom-call | flops 800000000 | bytes 5000000 | tf_op jit(solution)/shard_map/pallas_call | solution.py:45
  22.8 1.9 %collective-permute-start.10 = (bf16[8,2560]{1,0:T(8,128)(2,1)S(1)}, bf16[8,2560]{1,0:T(8,128)(2,1)S(1)}, u32[]{:S(2)}, u32[]{:S(2)}) collective-permute-start(bf16[8,2560]{1,0:T(8,128)(2,1)S(1)} %get-tuple-element.32), channel_id=1, source_target_pairs={{0,6},{1,7},{2,4},{3,5},{4,2},{5,3},{6,0},{7,1},{8,14},{9,15},{10,... | collective-permute-start | bytes 122888 | tf_op jit(solution)/shard_map/ppermute | solution.py:28
  24.8 0.5 %collective-permute-start.11 = (bf16[8,2560]{1,0:T(8,128)(2,1)S(1)}, bf16[8,2560]{1,0:T(8,128)(2,1)S(1)}, u32[]{:S(2)}, u32[]{:S(2)}) collective-permute-start(bf16[8,2560]{1,0:T(8,128)(2,1)S(1)} %get-tuple-element.33), channel_id=1, source_target_pairs={{0,4},{1,5},{2,6},{3,7},{4,0},{5,1},{6,2},{7,3},{8,12},{9,13},{10,... | collective-permute-start | bytes 122888 | tf_op jit(solution)/shard_map/ppermute | solution.py:28
  25.3 1.1 %collective-permute-start.12 = (bf16[8,2560]{1,0:T(8,128)(2,1)S(1)}, bf16[8,2560]{1,0:T(8,128)(2,1)S(1)}, u32[]{:S(2)}, u32[]{:S(2)}) collective-permute-start(bf16[8,2560]{1,0:T(8,128)(2,1)S(1)} %get-tuple-element.34), channel_id=1, source_target_pairs={{0,2},{1,3},{2,0},{3,1},{4,6},{5,7},{6,4},{7,5},{8,10},{9,11},{10,... | collective-permute-start | bytes 122888 | tf_op jit(solution)/shard_map/ppermute | solution.py:28
  26.4 1.4 %collective-permute-done.10.refs_5_ = bf16[8,2560]{1,0:T(8,128)(2,1)S(1)} collective-permute-done((bf16[8,2560]{1,0:T(8,128)(2,1)S(1)}, bf16[8,2560]{1,0:T(8,128)(2,1)S(1)}, u32[]{:S(2)}, u32[]{:S(2)}) %collective-permute-start.10) | collective-permute-done | bytes 40992 | tf_op jit(solution)/shard_map/ppermute | solution.py:28
  27.8 1.0 %collective-permute-done.11.refs_6_ = bf16[8,2560]{1,0:T(8,128)(2,1)S(1)} collective-permute-done((bf16[8,2560]{1,0:T(8,128)(2,1)S(1)}, bf16[8,2560]{1,0:T(8,128)(2,1)S(1)}, u32[]{:S(2)}, u32[]{:S(2)}) %collective-permute-start.11) | collective-permute-done | bytes 40992 | tf_op jit(solution)/shard_map/ppermute | solution.py:28
  28.8 0.5 %collective-permute-done.12.refs_7_ = bf16[8,2560]{1,0:T(8,128)(2,1)S(1)} collective-permute-done((bf16[8,2560]{1,0:T(8,128)(2,1)S(1)}, bf16[8,2560]{1,0:T(8,128)(2,1)S(1)}, u32[]{:S(2)}, u32[]{:S(2)}) %collective-permute-start.12) | collective-permute-done | bytes 40992 | tf_op jit(solution)/shard_map/ppermute | solution.py:28
  29.3 0.0 collective-permute-done.6.refs_1_
  29.3 1.1 %shard_map.111 = (bf16[1,64,2048]{2,1,0:T(8,128)(2,1)}, bf16[1,64,2048]{2,1,0:T(8,128)(2,1)}) custom-call(bf16[1,64,2048]{2,1,0:T(8,128)(2,1)S(1)} %collective-permute-done.refs_4_.refs_0_, bf16[1,64,2048]{2,1,0:T(8,128)(2,1)S(1)} %collective-permute-done.6.refs_1_, bf16[64,48]{1,0:T(8,128)(2,1)S(1)} %get-tuple-element.26.refs_2_, ...), custom_call_target="tpu_custom_call" | custom-call | flops 10000000 | bytes 1000000 | tf_op jit(solution)/shard_map/pallas_call | solution.py:45
  (1 shorter events, 0.0 us)
Async XLA Ops:
  0.6 6.9 %collective-permute-start.1 = (s32[1,8,64]{2,1,0:T(8,128)}, s32[1,8,64]{2,1,0:T(8,128)S(1)}, u32[]{:S(2)}, u32[]{:S(2)}) collective-permute-start(s32[1,8,64]{2,1,0:T(8,128)} %bitcast.12), channel_id=1, source_target_pairs={{0,8},{8,16},{16,24},{24,0},{1,9},{9,17},{17,25},{25,1},{2,10},{10... | collective-permute-start | bytes 6152 | tf_op jit(solution)/shard_map/ppermute | solution.py:23
  3.7 10.2 %collective-permute-start = (bf16[1,64,2048]{2,1,0:T(8,128)(2,1)}, bf16[1,64,2048]{2,1,0:T(8,128)(2,1)S(1)}, u32[]{:S(2)}, u32[]{:S(2)}) collective-permute-start(bf16[1,64,2048]{2,1,0:T(8,128)(2,1)} %param.9), channel_id=1, source_target_pairs={{0,8},{8,16},{16,24},{24,0},{1,9},{9,17},{17,25},{25,1},{2,10},{10... | collective-permute-start | bytes 786440 | tf_op jit(solution)/shard_map/ppermute | solution.py:23
  5.3 8.6 %collective-permute-start.2 = (bf16[1,1,40,384]{3,2,1,0:T(8,128)(2,1)}, bf16[1,1,40,384]{3,2,1,0:T(8,128)(2,1)S(1)}, u32[]{:S(2)}, u32[]{:S(2)}) collective-permute-start(bf16[1,1,40,384]{3,2,1,0:T(8,128)(2,1)} %refs_3_.1), channel_id=1, source_target_pairs={{0,1},{1,0},{2,3},{3,2},{4,5},{5,4},{6,7},{7,6},{8,9},{9,8},{10,11... | collective-permute-start | bytes 92168 | tf_op jit(solution)/shard_map/ppermute | solution.py:28
  7.8 6.1 %collective-permute-start.3 = (bf16[1,8,1280]{2,1,0:T(8,128)(2,1)S(1)}, bf16[1,8,1280]{2,1,0:T(8,128)(2,1)S(1)}, u32[]{:S(2)}, u32[]{:S(2)}) collective-permute-start(bf16[1,8,1280]{2,1,0:T(8,128)(2,1)S(1)} %shard_map.105.refs_0_), channel_id=1, source_target_pairs={{0,24},{8,0},{16,8},{24,16},{1,25},{9,1},{17,9},{25,17},{2,26},{10... | collective-permute-start | bytes 61448 | tf_op jit(solution)/shard_map/ppermute | solution.py:23
  12.7 5.0 %collective-permute-start.4 = (bf16[1,1,2048,384]{3,2,1,0:T(8,128)(2,1)S(1)}, bf16[1,1,2048,384]{3,2,1,0:T(8,128)(2,1)S(1)}, u32[]{:S(2)}, u32[]{:S(2)}) collective-permute-start(bf16[1,1,2048,384]{3,2,1,0:T(8,128)(2,1)S(1)} %get-tuple-element.24.refs_4_), channel_id=1, source_target_pairs={{0,1},{1,0},{2,3},{3,2},{4,5},{5,4},{6,7},{7,6},{8,9},{9,8},{10,11... | collective-permute-start | bytes 4718600 | tf_op jit(solution)/shard_map/ppermute | solution.py:28
  12.7 4.9 %collective-permute-start.5 = (bf16[1,1,192,2048]{3,2,1,0:T(8,128)(2,1)S(1)}, bf16[1,1,192,2048]{3,2,1,0:T(8,128)(2,1)S(1)}, u32[]{:S(2)}, u32[]{:S(2)}) collective-permute-start(bf16[1,1,192,2048]{3,2,1,0:T(8,128)(2,1)S(1)} %get-tuple-element.25), channel_id=1, source_target_pairs={{0,1},{1,0},{2,3},{3,2},{4,5},{5,4},{6,7},{7,6},{8,9},{9,8},{10,11... | collective-permute-start | bytes 2359304 | tf_op jit(solution)/shard_map/ppermute | solution.py:28
  14.1 5.3 %collective-permute-start.8 = (bf16[8,2560]{1,0:T(8,128)(2,1)S(1)}, bf16[8,2560]{1,0:T(8,128)(2,1)S(1)}, u32[]{:S(2)}, u32[]{:S(2)}) collective-permute-start(bf16[8,2560]{1,0:T(8,128)(2,1)S(1)} %bitcast.5), channel_id=1, source_target_pairs={{0,4},{1,5},{2,6},{3,7},{4,0},{5,1},{6,2},{7,3},{8,12},{9,13},{10,... | collective-permute-start | bytes 122888 | tf_op jit(solution)/shard_map/ppermute | solution.py:28
  15.7 4.9 %collective-permute-start.7 = (bf16[8,2560]{1,0:T(8,128)(2,1)S(1)}, bf16[8,2560]{1,0:T(8,128)(2,1)S(1)}, u32[]{:S(2)}, u32[]{:S(2)}) collective-permute-start(bf16[8,2560]{1,0:T(8,128)(2,1)S(1)} %bitcast.6), channel_id=1, source_target_pairs={{0,6},{1,7},{2,4},{3,5},{4,2},{5,3},{6,0},{7,1},{8,14},{9,15},{10,... | collective-permute-start | bytes 122888 | tf_op jit(solution)/shard_map/ppermute | solution.py:28
  17.1 4.0 %collective-permute-start.9 = (bf16[8,2560]{1,0:T(8,128)(2,1)S(1)}, bf16[8,2560]{1,0:T(8,128)(2,1)S(1)}, u32[]{:S(2)}, u32[]{:S(2)}) collective-permute-start(bf16[8,2560]{1,0:T(8,128)(2,1)S(1)} %bitcast.7), channel_id=1, source_target_pairs={{0,2},{1,3},{2,0},{3,1},{4,6},{5,7},{6,4},{7,5},{8,10},{9,11},{10,... | collective-permute-start | bytes 122888 | tf_op jit(solution)/shard_map/ppermute | solution.py:28
  17.7 11.7 %collective-permute-start.6 = (bf16[1,64,2048]{2,1,0:T(8,128)(2,1)S(1)}, bf16[1,64,2048]{2,1,0:T(8,128)(2,1)S(1)}, u32[]{:S(2)}, u32[]{:S(2)}) collective-permute-start(bf16[1,64,2048]{2,1,0:T(8,128)(2,1)S(1)} %shard_map.108), channel_id=1, source_target_pairs={{0,24},{8,0},{16,8},{24,16},{1,25},{9,1},{17,9},{25,17},{2,26},{10... | collective-permute-start | bytes 786440 | tf_op jit(solution)/shard_map/ppermute | solution.py:23
  22.8 5.0 %collective-permute-start.10 = (bf16[8,2560]{1,0:T(8,128)(2,1)S(1)}, bf16[8,2560]{1,0:T(8,128)(2,1)S(1)}, u32[]{:S(2)}, u32[]{:S(2)}) collective-permute-start(bf16[8,2560]{1,0:T(8,128)(2,1)S(1)} %get-tuple-element.32), channel_id=1, source_target_pairs={{0,6},{1,7},{2,4},{3,5},{4,2},{5,3},{6,0},{7,1},{8,14},{9,15},{10,... | collective-permute-start | bytes 122888 | tf_op jit(solution)/shard_map/ppermute | solution.py:28
  24.8 4.0 %collective-permute-start.11 = (bf16[8,2560]{1,0:T(8,128)(2,1)S(1)}, bf16[8,2560]{1,0:T(8,128)(2,1)S(1)}, u32[]{:S(2)}, u32[]{:S(2)}) collective-permute-start(bf16[8,2560]{1,0:T(8,128)(2,1)S(1)} %get-tuple-element.33), channel_id=1, source_target_pairs={{0,4},{1,5},{2,6},{3,7},{4,0},{5,1},{6,2},{7,3},{8,12},{9,13},{10,... | collective-permute-start | bytes 122888 | tf_op jit(solution)/shard_map/ppermute | solution.py:28
  25.3 4.0 %collective-permute-start.12 = (bf16[8,2560]{1,0:T(8,128)(2,1)S(1)}, bf16[8,2560]{1,0:T(8,128)(2,1)S(1)}, u32[]{:S(2)}, u32[]{:S(2)}) collective-permute-start(bf16[8,2560]{1,0:T(8,128)(2,1)S(1)} %get-tuple-element.34), channel_id=1, source_target_pairs={{0,2},{1,3},{2,0},{3,1},{4,6},{5,7},{6,4},{7,5},{8,10},{9,11},{10,... | collective-permute-start | bytes 122888 | tf_op jit(solution)/shard_map/ppermute | solution.py:28

commit v8 on v6

--- a/solution.py
+++ b/solution.py
@@ -259,7 +259,8 @@
     _, slot = lines_of(hidden.shape, chips)
     hidden = jnp.where(slot < 0, hidden, 0.0)
     inner = jnp.concatenate([grads.astype(jnp.bfloat16), hidden.astype(jnp.bfloat16)], axis=1)
-    total = dot(inner, second[...])
+    cut = second.shape[1] // 2
+    total = jnp.concatenate([dot(inner, second[:, :cut]), dot(inner, second[:, cut:])], axis=1)
     for index, ref in enumerate(results):
         late = chips * LINES + index * FEW
         first = total[index * LINES : (index + 1) * LINES]
@@ -268,7 +269,9 @@
 
 def finish_kernel(groups, chips, *refs):
     x, u, place_x, place_u, sum_scale = refs[:5]
-    returned = refs[5 : 5 + chips][::-1]
+    returned = refs[5 : 5 + chips]
+    if chips == 4:
+        returned = [returned[k] for k in [3, 2, 0, 1]]
     out_x, out_u = refs[5 + chips :]
     share = chips // groups
     sums = []
@@ -428,7 +431,7 @@
     return call(
         functools.partial(finish_kernel, groups, chips),
         (block, block),
-        (layer_input, upstream, place_x, place_u, sum_scale, *returned[::-1]),
+        (layer_input, upstream, place_x, place_u, sum_scale, *([returned[k] for k in (2, 3, 1, 0)] if direct else returned)),
         16 * MIB,
         10_000_000,
         1_000_000,

time: 30.6 us -> 30.6 us (level)
  transfers between devices with their start and end apart: 13 -> 13, of which waited for: 7 -> 6; matrix products, arithmetic and copies ran while one was open for 0% -> 0% of each run, Pallas kernels for 23% -> 23%
where the time goes in v8:
time: 30.6 us; the launch traced here: 30.4 us
  starting transfers between devices  16.2 us (53%)
  Pallas kernels  8.17 us (27%)
  waiting for transfers between devices  5.36 us (18%)
  between operations  0.69 us (2%)
    ppermute x4, starting transfers between devices, along_sections(): return lax.ppermute(value, 'segment', pairs)  8.51 us
    pallas_call x8, Pallas kernels, call(): pl.pallas_call(body, out_shape=outs, in_specs=[anywhere] * waits + [dista...  8.17 us
    ppermute x9, starting transfers between devices, across_owners(): lax.ppermute(value, 'expert', [(source, source ^ flip) for source in rang...  7.66 us
    ppermute x9, waiting for transfers between devices, across_owners(): lax.ppermute(value, 'expert', [(source, source ^ flip) for source in rang...  3.54 us
    ppermute x4, waiting for transfers between devices, along_sections(): return lax.ppermute(value, 'segment', pairs)  1.82 us
  transfers between devices with their start and end apart: 13, of which 6 were waited for; matrix products, arithmetic and copies ran while one was open for 0% of the time, Pallas kernels for 23%

profile of v8, /device:TPU:0, one launch (start us, length us, event | category | flops | bytes accessed | tf_op | source)
XLA Modules:
  0.0 30.4 jit_solution(15582599707477849263)
XLA Ops:
  0.6 3.1 %collective-permute-start.1 = (s32[1,8,64]{2,1,0:T(8,128)}, s32[1,8,64]{2,1,0:T(8,128)S(1)}, u32[]{:S(2)}, u32[]{:S(2)}) collective-permute-start(s32[1,8,64]{2,1,0:T(8,128)} %bitcast.12), channel_id=1, source_target_pairs={{0,8},{8,16},{16,24},{24,0},{1,9},{9,17},{17,25},{25,1},{2,10},{10... | collective-permute-start | bytes 6152 | tf_op jit(solution)/shard_map/ppermute | solution.py:23
  3.7 1.6 %collective-permute-start = (bf16[1,64,2048]{2,1,0:T(8,128)(2,1)}, bf16[1,64,2048]{2,1,0:T(8,128)(2,1)S(1)}, u32[]{:S(2)}, u32[]{:S(2)}) collective-permute-start(bf16[1,64,2048]{2,1,0:T(8,128)(2,1)} %param.9), channel_id=1, source_target_pairs={{0,8},{8,16},{16,24},{24,0},{1,9},{9,17},{17,25},{25,1},{2,10},{10... | collective-permute-start | bytes 786440 | tf_op jit(solution)/shard_map/ppermute | solution.py:23
  5.3 0.0 collective-permute-start.2
  5.3 1.1 %shard_map.104 = (bf16[1,64,2048]{2,1,0:T(8,128)(2,1)S(1)}, bf16[8,64]{1,0:T(8,128)(2,1)S(1)}, bf16[64,48]{1,0:T(8,128)(2,1)S(1)}, bf16[64,48]{1,0:T(8,128)(2,1)S(1)}, f32[16,128]{1,0:T(8,128)S(1)}) custom-call(s32[1,8,64]{2,1,0:T(8,128)} %bitcast.9, f32[1,8,64]{2,1,0:T(8,128)} %bitcast.10, s32[1,8,64]{2,1,0:T(8,128)} %bitcast.13, f32[1,8,64]{2,1,0:T(8,128)} %bitcast.11, ...), custom_call_target="tpu_custom_call" | custom-call | flops 10000000 | bytes 1000000 | tf_op jit(solution)/shard_map/pallas_call | solution.py:45
  6.4 1.1 %collective-permute-done.1.refs_0_ = s32[1,8,64]{2,1,0:T(8,128)S(1)} collective-permute-done((s32[1,8,64]{2,1,0:T(8,128)}, s32[1,8,64]{2,1,0:T(8,128)S(1)}, u32[]{:S(2)}, u32[]{:S(2)}) %collective-permute-start.1) | collective-permute-done | bytes 2080 | tf_op jit(solution)/shard_map/ppermute | solution.py:23
  7.5 0.3 shard_map.105.refs_0_
  7.8 2.1 %collective-permute-start.3 = (bf16[1,8,1280]{2,1,0:T(8,128)(2,1)S(1)}, bf16[1,8,1280]{2,1,0:T(8,128)(2,1)S(1)}, u32[]{:S(2)}, u32[]{:S(2)}) collective-permute-start(bf16[1,8,1280]{2,1,0:T(8,128)(2,1)S(1)} %shard_map.105.refs_0_), channel_id=1, source_target_pairs={{0,24},{8,0},{16,8},{24,16},{1,25},{9,1},{17,9},{25,17},{2,26},{10... | collective-permute-start | bytes 61448 | tf_op jit(solution)/shard_map/ppermute | solution.py:23
  9.9 2.7 %shard_map.106 = (bf16[1,1,2048,384]{3,2,1,0:T(8,128)(2,1)S(1)}, bf16[1,1,192,2048]{3,2,1,0:T(8,128)(2,1)S(1)}, bf16[2048,384]{1,0:T(8,128)(2,1)S(1)}, bf16[1152,2048]{1,0:T(8,128)(2,1)S(1)}, f32[40,768]{1,0:T(8,128)S(1)}) custom-call(bf16[1,8,1280]{2,1,0:T(8,128)(2,1)S(1)} %shard_map.105.refs_0_, bf16[1,1,2048,384]{3,2,1,0:T(8,128)(2,1)} %refs_1_.1, ...), custom_call_target="tpu_custom_call" | custom-call | flops 10000000 | bytes 5000000 | tf_op jit(solution)/shard_map/pallas_call | solution.py:45
  12.7 0.1 collective-permute-start.4
  12.7 0.5 %collective-permute-start.5 = (bf16[1,1,192,2048]{3,2,1,0:T(8,128)(2,1)S(1)}, bf16[1,1,192,2048]{3,2,1,0:T(8,128)(2,1)S(1)}, u32[]{:S(2)}, u32[]{:S(2)}) collective-permute-start(bf16[1,1,192,2048]{3,2,1,0:T(8,128)(2,1)S(1)} %get-tuple-element.25), channel_id=1, source_target_pairs={{0,1},{1,0},{2,3},{3,2},{4,5},{5,4},{6,7},{7,6},{8,9},{9,8},{10,11... | collective-permute-start | bytes 2359304 | tf_op jit(solution)/shard_map/ppermute | solution.py:28
  13.2 0.7 %collective-permute-done.3.refs_6_ = bf16[1,8,1280]{2,1,0:T(8,128)(2,1)S(1)} collective-permute-done((bf16[1,8,1280]{2,1,0:T(8,128)(2,1)S(1)}, bf16[1,8,1280]{2,1,0:T(8,128)(2,1)S(1)}, u32[]{:S(2)}, u32[]{:S(2)}) %collective-permute-start.3) | collective-permute-done | bytes 20512 | tf_op jit(solution)/shard_map/ppermute | solution.py:23
  13.9 0.0 collective-permute-done.2.refs_3_
  13.9 0.0 collective-permute-done.refs_4_.refs_0_
  13.9 0.2 shard_map.107.refs_0_
  14.1 1.6 %collective-permute-start.8 = (bf16[8,2560]{1,0:T(8,128)(2,1)S(1)}, bf16[8,2560]{1,0:T(8,128)(2,1)S(1)}, u32[]{:S(2)}, u32[]{:S(2)}) collective-permute-start(bf16[8,2560]{1,0:T(8,128)(2,1)S(1)} %bitcast.5), channel_id=1, source_target_pairs={{0,4},{1,5},{2,6},{3,7},{4,0},{5,1},{6,2},{7,3},{8,12},{9,13},{10,... | collective-permute-start | bytes 122888 | tf_op jit(solution)/shard_map/ppermute | solution.py:28
  15.7 1.4 %collective-permute-start.7 = (bf16[8,2560]{1,0:T(8,128)(2,1)S(1)}, bf16[8,2560]{1,0:T(8,128)(2,1)S(1)}, u32[]{:S(2)}, u32[]{:S(2)}) collective-permute-start(bf16[8,2560]{1,0:T(8,128)(2,1)S(1)} %bitcast.6), channel_id=1, source_target_pairs={{0,6},{1,7},{2,4},{3,5},{4,2},{5,3},{6,0},{7,1},{8,14},{9,15},{10,... | collective-permute-start | bytes 122888 | tf_op jit(solution)/shard_map/ppermute | solution.py:28
  17.1 0.5 %collective-permute-start.9 = (bf16[8,2560]{1,0:T(8,128)(2,1)S(1)}, bf16[8,2560]{1,0:T(8,128)(2,1)S(1)}, u32[]{:S(2)}, u32[]{:S(2)}) collective-permute-start(bf16[8,2560]{1,0:T(8,128)(2,1)S(1)} %bitcast.7), channel_id=1, source_target_pairs={{0,2},{1,3},{2,0},{3,1},{4,6},{5,7},{6,4},{7,5},{8,10},{9,11},{10,... | collective-permute-start | bytes 122888 | tf_op jit(solution)/shard_map/ppermute | solution.py:28
  17.6 0.0 collective-permute-done.5.refs_2_
  17.6 0.0 collective-permute-done.4.refs_1_.refs_5_
  17.7 1.7 %collective-permute-start.6 = (bf16[1,64,2048]{2,1,0:T(8,128)(2,1)S(1)}, bf16[1,64,2048]{2,1,0:T(8,128)(2,1)S(1)}, u32[]{:S(2)}, u32[]{:S(2)}) collective-permute-start(bf16[1,64,2048]{2,1,0:T(8,128)(2,1)S(1)} %shard_map.108), channel_id=1, source_target_pairs={{0,24},{8,0},{16,8},{24,16},{1,25},{9,1},{17,9},{25,17},{2,26},{10... | collective-permute-start | bytes 786440 | tf_op jit(solution)/shard_map/ppermute | solution.py:23
  19.4 0.0 collective-permute-done.8.refs_0_.refs_2_
  19.4 1.1 %shard_map.109 = (bf16[2048,384]{1,0:T(8,128)(2,1)S(1)}, bf16[1152,2048]{1,0:T(8,128)(2,1)S(1)}, f32[40,768]{1,0:T(8,128)S(1)}) custom-call(bf16[8,2560]{1,0:T(8,128)(2,1)S(1)} %collective-permute-done.8.refs_0_.refs_2_, ...), custom_call_target="tpu_custom_call", output_to_operand_aliasing={{0}: (4, {}), {1}: (5, {}), {2}: (6, {})} | custom-call | flops 10000000000 | bytes 5000000 | tf_op jit(solution)/shard_map/pallas_call | solution.py:45
  20.5 0.1 collective-permute-done.7.refs_1_
  20.6 0.5 %collective-permute-done.9.refs_3_ = bf16[8,2560]{1,0:T(8,128)(2,1)S(1)} collective-permute-done((bf16[8,2560]{1,0:T(8,128)(2,1)S(1)}, bf16[8,2560]{1,0:T(8,128)(2,1)S(1)}, u32[]{:S(2)}, u32[]{:S(2)}) %collective-permute-start.9) | collective-permute-done | bytes 40992 | tf_op jit(solution)/shard_map/ppermute | solution.py:28
  21.1 1.7 %shard_map.110 = (bf16[8,2560]{1,0:T(8,128)(2,1)S(1)}, bf16[8,2560]{1,0:T(8,128)(2,1)S(1)}, bf16[8,2560]{1,0:T(8,128)(2,1)S(1)}, bf16[8,2560]{1,0:T(8,128)(2,1)S(1)}) custom-call(bf16[8,2560]{1,0:T(8,128)(2,1)S(1)} %bitcast.8, bf16[8,2560]{1,0:T(8,128)(2,1)S(1)} %collective-permute-done.7.refs_1_, ...), custom_call_target="tpu_custom_call" | custom-call | flops 800000000 | bytes 5000000 | tf_op jit(solution)/shard_map/pallas_call | solution.py:45
  22.8 1.6 %collective-permute-start.10 = (bf16[8,2560]{1,0:T(8,128)(2,1)S(1)}, bf16[8,2560]{1,0:T(8,128)(2,1)S(1)}, u32[]{:S(2)}, u32[]{:S(2)}) collective-permute-start(bf16[8,2560]{1,0:T(8,128)(2,1)S(1)} %get-tuple-element.32), channel_id=1, source_target_pairs={{0,4},{1,5},{2,6},{3,7},{4,0},{5,1},{6,2},{7,3},{8,12},{9,13},{10,... | collective-permute-start | bytes 122888 | tf_op jit(solution)/shard_map/ppermute | solution.py:28
  24.4 0.9 %collective-permute-start.11 = (bf16[8,2560]{1,0:T(8,128)(2,1)S(1)}, bf16[8,2560]{1,0:T(8,128)(2,1)S(1)}, u32[]{:S(2)}, u32[]{:S(2)}) collective-permute-start(bf16[8,2560]{1,0:T(8,128)(2,1)S(1)} %get-tuple-element.33), channel_id=1, source_target_pairs={{0,6},{1,7},{2,4},{3,5},{4,2},{5,3},{6,0},{7,1},{8,14},{9,15},{10,... | collective-permute-start | bytes 122888 | tf_op jit(solution)/shard_map/ppermute | solution.py:28
  25.3 1.1 %collective-permute-start.12 = (bf16[8,2560]{1,0:T(8,128)(2,1)S(1)}, bf16[8,2560]{1,0:T(8,128)(2,1)S(1)}, u32[]{:S(2)}, u32[]{:S(2)}) collective-permute-start(bf16[8,2560]{1,0:T(8,128)(2,1)S(1)} %get-tuple-element.34), channel_id=1, source_target_pairs={{0,2},{1,3},{2,0},{3,1},{4,6},{5,7},{6,4},{7,5},{8,10},{9,11},{10,... | collective-permute-start | bytes 122888 | tf_op jit(solution)/shard_map/ppermute | solution.py:28
  26.4 0.5 %collective-permute-done.10.refs_5_ = bf16[8,2560]{1,0:T(8,128)(2,1)S(1)} collective-permute-done((bf16[8,2560]{1,0:T(8,128)(2,1)S(1)}, bf16[8,2560]{1,0:T(8,128)(2,1)S(1)}, u32[]{:S(2)}, u32[]{:S(2)}) %collective-permute-start.10) | collective-permute-done | bytes 40992 | tf_op jit(solution)/shard_map/ppermute | solution.py:28
  26.9 2.4 %collective-permute-done.11.refs_6_ = bf16[8,2560]{1,0:T(8,128)(2,1)S(1)} collective-permute-done((bf16[8,2560]{1,0:T(8,128)(2,1)S(1)}, bf16[8,2560]{1,0:T(8,128)(2,1)S(1)}, u32[]{:S(2)}, u32[]{:S(2)}) %collective-permute-start.11) | collective-permute-done | bytes 40992 | tf_op jit(solution)/shard_map/ppermute | solution.py:28
  29.3 0.0 collective-permute-done.12.refs_7_
  29.3 0.0 collective-permute-done.6.refs_1_
  29.3 1.1 %shard_map.111 = (bf16[1,64,2048]{2,1,0:T(8,128)(2,1)}, bf16[1,64,2048]{2,1,0:T(8,128)(2,1)}) custom-call(bf16[1,64,2048]{2,1,0:T(8,128)(2,1)S(1)} %collective-permute-done.refs_4_.refs_0_, bf16[1,64,2048]{2,1,0:T(8,128)(2,1)S(1)} %collective-permute-done.6.refs_1_, bf16[64,48]{1,0:T(8,128)(2,1)S(1)} %get-tuple-element.26.refs_2_, ...), custom_call_target="tpu_custom_call" | custom-call | flops 10000000 | bytes 1000000 | tf_op jit(solution)/shard_map/pallas_call | solution.py:45
  (1 shorter events, 0.0 us)
Async XLA Ops:
  0.6 6.9 %collective-permute-start.1 = (s32[1,8,64]{2,1,0:T(8,128)}, s32[1,8,64]{2,1,0:T(8,128)S(1)}, u32[]{:S(2)}, u32[]{:S(2)}) collective-permute-start(s32[1,8,64]{2,1,0:T(8,128)} %bitcast.12), channel_id=1, source_target_pairs={{0,8},{8,16},{16,24},{24,0},{1,9},{9,17},{17,25},{25,1},{2,10},{10... | collective-permute-start | bytes 6152 | tf_op jit(solution)/shard_map/ppermute | solution.py:23
  3.7 10.2 %collective-permute-start = (bf16[1,64,2048]{2,1,0:T(8,128)(2,1)}, bf16[1,64,2048]{2,1,0:T(8,128)(2,1)S(1)}, u32[]{:S(2)}, u32[]{:S(2)}) collective-permute-start(bf16[1,64,2048]{2,1,0:T(8,128)(2,1)} %param.9), channel_id=1, source_target_pairs={{0,8},{8,16},{16,24},{24,0},{1,9},{9,17},{17,25},{25,1},{2,10},{10... | collective-permute-start | bytes 786440 | tf_op jit(solution)/shard_map/ppermute | solution.py:23
  5.3 8.6 %collective-permute-start.2 = (bf16[1,1,40,384]{3,2,1,0:T(8,128)(2,1)}, bf16[1,1,40,384]{3,2,1,0:T(8,128)(2,1)S(1)}, u32[]{:S(2)}, u32[]{:S(2)}) collective-permute-start(bf16[1,1,40,384]{3,2,1,0:T(8,128)(2,1)} %refs_3_.1), channel_id=1, source_target_pairs={{0,1},{1,0},{2,3},{3,2},{4,5},{5,4},{6,7},{7,6},{8,9},{9,8},{10,11... | collective-permute-start | bytes 92168 | tf_op jit(solution)/shard_map/ppermute | solution.py:28
  7.8 6.1 %collective-permute-start.3 = (bf16[1,8,1280]{2,1,0:T(8,128)(2,1)S(1)}, bf16[1,8,1280]{2,1,0:T(8,128)(2,1)S(1)}, u32[]{:S(2)}, u32[]{:S(2)}) collective-permute-start(bf16[1,8,1280]{2,1,0:T(8,128)(2,1)S(1)} %shard_map.105.refs_0_), channel_id=1, source_target_pairs={{0,24},{8,0},{16,8},{24,16},{1,25},{9,1},{17,9},{25,17},{2,26},{10... | collective-permute-start | bytes 61448 | tf_op jit(solution)/shard_map/ppermute | solution.py:23
  12.7 5.0 %collective-permute-start.4 = (bf16[1,1,2048,384]{3,2,1,0:T(8,128)(2,1)S(1)}, bf16[1,1,2048,384]{3,2,1,0:T(8,128)(2,1)S(1)}, u32[]{:S(2)}, u32[]{:S(2)}) collective-permute-start(bf16[1,1,2048,384]{3,2,1,0:T(8,128)(2,1)S(1)} %get-tuple-element.24.refs_4_), channel_id=1, source_target_pairs={{0,1},{1,0},{2,3},{3,2},{4,5},{5,4},{6,7},{7,6},{8,9},{9,8},{10,11... | collective-permute-start | bytes 4718600 | tf_op jit(solution)/shard_map/ppermute | solution.py:28
  12.7 4.9 %collective-permute-start.5 = (bf16[1,1,192,2048]{3,2,1,0:T(8,128)(2,1)S(1)}, bf16[1,1,192,2048]{3,2,1,0:T(8,128)(2,1)S(1)}, u32[]{:S(2)}, u32[]{:S(2)}) collective-permute-start(bf16[1,1,192,2048]{3,2,1,0:T(8,128)(2,1)S(1)} %get-tuple-element.25), channel_id=1, source_target_pairs={{0,1},{1,0},{2,3},{3,2},{4,5},{5,4},{6,7},{7,6},{8,9},{9,8},{10,11... | collective-permute-start | bytes 2359304 | tf_op jit(solution)/shard_map/ppermute | solution.py:28
  14.1 5.3 %collective-permute-start.8 = (bf16[8,2560]{1,0:T(8,128)(2,1)S(1)}, bf16[8,2560]{1,0:T(8,128)(2,1)S(1)}, u32[]{:S(2)}, u32[]{:S(2)}) collective-permute-start(bf16[8,2560]{1,0:T(8,128)(2,1)S(1)} %bitcast.5), channel_id=1, source_target_pairs={{0,4},{1,5},{2,6},{3,7},{4,0},{5,1},{6,2},{7,3},{8,12},{9,13},{10,... | collective-permute-start | bytes 122888 | tf_op jit(solution)/shard_map/ppermute | solution.py:28
  15.7 4.9 %collective-permute-start.7 = (bf16[8,2560]{1,0:T(8,128)(2,1)S(1)}, bf16[8,2560]{1,0:T(8,128)(2,1)S(1)}, u32[]{:S(2)}, u32[]{:S(2)}) collective-permute-start(bf16[8,2560]{1,0:T(8,128)(2,1)S(1)} %bitcast.6), channel_id=1, source_target_pairs={{0,6},{1,7},{2,4},{3,5},{4,2},{5,3},{6,0},{7,1},{8,14},{9,15},{10,... | collective-permute-start | bytes 122888 | tf_op jit(solution)/shard_map/ppermute | solution.py:28
  17.1 4.0 %collective-permute-start.9 = (bf16[8,2560]{1,0:T(8,128)(2,1)S(1)}, bf16[8,2560]{1,0:T(8,128)(2,1)S(1)}, u32[]{:S(2)}, u32[]{:S(2)}) collective-permute-start(bf16[8,2560]{1,0:T(8,128)(2,1)S(1)} %bitcast.7), channel_id=1, source_target_pairs={{0,2},{1,3},{2,0},{3,1},{4,6},{5,7},{6,4},{7,5},{8,10},{9,11},{10,... | collective-permute-start | bytes 122888 | tf_op jit(solution)/shard_map/ppermute | solution.py:28
  17.7 11.7 %collective-permute-start.6 = (bf16[1,64,2048]{2,1,0:T(8,128)(2,1)S(1)}, bf16[1,64,2048]{2,1,0:T(8,128)(2,1)S(1)}, u32[]{:S(2)}, u32[]{:S(2)}) collective-permute-start(bf16[1,64,2048]{2,1,0:T(8,128)(2,1)S(1)} %shard_map.108), channel_id=1, source_target_pairs={{0,24},{8,0},{16,8},{24,16},{1,25},{9,1},{17,9},{25,17},{2,26},{10... | collective-permute-start | bytes 786440 | tf_op jit(solution)/shard_map/ppermute | solution.py:23
  22.8 4.1 %collective-permute-start.10 = (bf16[8,2560]{1,0:T(8,128)(2,1)S(1)}, bf16[8,2560]{1,0:T(8,128)(2,1)S(1)}, u32[]{:S(2)}, u32[]{:S(2)}) collective-permute-start(bf16[8,2560]{1,0:T(8,128)(2,1)S(1)} %get-tuple-element.32), channel_id=1, source_target_pairs={{0,4},{1,5},{2,6},{3,7},{4,0},{5,1},{6,2},{7,3},{8,12},{9,13},{10,... | collective-permute-start | bytes 122888 | tf_op jit(solution)/shard_map/ppermute | solution.py:28
  24.4 4.9 %collective-permute-start.11 = (bf16[8,2560]{1,0:T(8,128)(2,1)S(1)}, bf16[8,2560]{1,0:T(8,128)(2,1)S(1)}, u32[]{:S(2)}, u32[]{:S(2)}) collective-permute-start(bf16[8,2560]{1,0:T(8,128)(2,1)S(1)} %get-tuple-element.33), channel_id=1, source_target_pairs={{0,6},{1,7},{2,4},{3,5},{4,2},{5,3},{6,0},{7,1},{8,14},{9,15},{10,... | collective-permute-start | bytes 122888 | tf_op jit(solution)/shard_map/ppermute | solution.py:28
  25.3 4.0 %collective-permute-start.12 = (bf16[8,2560]{1,0:T(8,128)(2,1)S(1)}, bf16[8,2560]{1,0:T(8,128)(2,1)S(1)}, u32[]{:S(2)}, u32[]{:S(2)}) collective-permute-start(bf16[8,2560]{1,0:T(8,128)(2,1)S(1)} %get-tuple-element.34), channel_id=1, source_target_pairs={{0,2},{1,3},{2,0},{3,1},{4,6},{5,7},{6,4},{7,5},{8,10},{9,11},{10,... | collective-permute-start | bytes 122888 | tf_op jit(solution)/shard_map/ppermute | solution.py:28
